TPU v7x, 128 devices: a whole 4x4x4 slice. The times are simulated.
128 devices in a mesh: ctx: 16 (over z, y_hi, core), row: 2 (over y_lo), col: 4 (over x).
Axes of the slice: x: 4, y: 4 (y_hi: 2, y_lo: 2; y = y_hi * 2 + y_lo), z: 4, core: 2. Of those that a mesh axis runs over, the one named last changes fastest.
Arguments:
- tokens: bfloat16 [4096, 4096], P('ctx', ('row', 'col')), may hold values from -6 to 6
- w_feat: bfloat16 [4096, 3, 4096], P(None, None, ('row', 'col')), may hold values from -0.09375 to 0.09375
- short_filter: float32 [7, 3, 4096], P(None, None, ('row', 'col')), may hold values from -2 to 2
- mr_filter: float32 [128, 4096], P(None, ('row', 'col')), may hold values from -0.5 to 0.5
- queries: bfloat16 [4096, 4096], P('ctx', ('row', 'col')), may hold values from -6 to 6
- key_rows: bfloat16 [4096, 4096], P('ctx', ('row', 'col')), may hold values from -6 to 6
- cotangent: bfloat16 [4096, 4096], P('ctx', ('row', 'col')), may hold values from -6 to 6
Outputs:
- block_out: bfloat16 [4096, 4096], P('ctx', ('row', 'col'))
- grad_input: bfloat16 [4096, 4096], P('ctx', ('row', 'col'))
- grad_feat: float32 [4096, 3, 4096], P('ctx', None, ('row', 'col'))
- grad_short: float32 [7, 3, 4096], P(None, None, ('row', 'col'))
- grad_mr: float32 [128, 4096], P(None, ('row', 'col'))
- grad_queries: bfloat16 [4096, 4096], P('ctx', ('row', 'col'))
- grad_keys: bfloat16 [4096, 4096], P('ctx', ('row', 'col'))
All inputs are finite; a program needn't handle non-finite values.
Results may differ from a plain program's by a relative error of at most 0.025.
Values may be sent and summed in bfloat16 or wider, within the bound.
A program may use at most 192 MiB of HBM per device.

v0:
```python
import jax
import jax.numpy as jnp
from jax import lax
from jax.sharding import PartitionSpec as P

DH = 128
SHORT = 7
MRLEN = 128


def shifted(block, axis, distance):
    devices = range(lax.axis_size(axis))
    route = [(i - distance, i) for i in devices if i - distance in devices]
    return lax.ppermute(block, axis, route)


def as_sent(array):
    return jax.tree.map(lambda a: a.astype(jnp.bfloat16) if a.dtype == jnp.float32 else a, array)


def causal_mix(padded, filter_taps):
    channels = padded.shape[1]
    kernel = filter_taps[::-1][:, None, :]
    return lax.conv_general_dilated(
        padded[None],
        kernel,
        (1,),
        "VALID",
        dimension_numbers=("NWC", "WIO", "NWC"),
        feature_group_count=channels,
        precision=lax.Precision.HIGHEST,
    )[0]


def anti_mix(padded, filter_taps):
    channels = padded.shape[1]
    kernel = filter_taps[:, None, :]
    return lax.conv_general_dilated(
        padded[None],
        kernel,
        (1,),
        "VALID",
        dimension_numbers=("NWC", "WIO", "NWC"),
        feature_group_count=channels,
        precision=lax.Precision.HIGHEST,
    )[0]


def tap_grads(grad_rows, padded):
    channels = grad_rows.shape[1]
    kernel = grad_rows[:, None, :]
    lagged = lax.conv_general_dilated(
        padded[None],
        kernel,
        (1,),
        "VALID",
        dimension_numbers=("NWC", "WIO", "NWC"),
        feature_group_count=channels,
        precision=lax.Precision.HIGHEST,
    )[0]
    return lagged[::-1]


def score_block(queries, all_keys, first_row, score_scale):
    local_rows, local_width = queries.shape
    head_count = local_width // DH
    query_heads = queries.reshape(local_rows, head_count, DH)
    key_heads = all_keys.reshape(all_keys.shape[0], head_count, DH)
    scores = (
        jnp.einsum("thd,shd->hts", query_heads, key_heads, preferred_element_type=jnp.float32)
        * score_scale
    )
    query_pos = first_row + jnp.arange(local_rows, dtype=jnp.int32)
    key_pos = jnp.arange(all_keys.shape[0], dtype=jnp.int32)
    allowed = query_pos[:, None] >= key_pos[None, :]
    return jnp.where(allowed[None], scores, -jnp.inf)


def local(tokens, w_feat, short_filter, mr_filter, queries, key_rows, cotangent):
    local_rows, local_width = tokens.shape
    ctx_size = lax.axis_size("ctx")
    total_rows = local_rows * ctx_size
    head_count = local_width // DH
    score_scale = DH ** (-0.5)
    first_row = lax.axis_index("ctx") * local_rows
    full_tokens = lax.all_gather(tokens, ("row", "col"), axis=1, tiled=True)
    features = jnp.einsum(
        "tc,cjk->tjk", full_tokens, w_feat, preferred_element_type=jnp.float32
    ).astype(jnp.bfloat16)
    flat_feat = features.reshape(local_rows, 3 * local_width)
    short_taps = short_filter.reshape(SHORT, 3 * local_width)
    feat_rim = shifted(flat_feat[local_rows - (SHORT - 1) :], "ctx", 1)
    feat_pad = jnp.concatenate([feat_rim, flat_feat], axis=0).astype(jnp.float32)
    mixed_feat = causal_mix(feat_pad, short_taps)
    product = (
        mixed_feat[:, local_width : 2 * local_width] * mixed_feat[:, 2 * local_width :]
    ).astype(jnp.bfloat16)
    prod_rim = shifted(product[local_rows - (MRLEN - 1) :], "ctx", 1)
    prod_pad = jnp.concatenate([prod_rim, product], axis=0).astype(jnp.float32)
    query_mix = mixed_feat[:, :local_width]
    key_mix = mixed_feat[:, local_width : 2 * local_width]
    value_mix = mixed_feat[:, 2 * local_width :]
    long_mix = causal_mix(prod_pad, mr_filter)
    hyena_out = query_mix * long_mix
    hyena_stream = (tokens.astype(jnp.float32) + hyena_out).astype(jnp.bfloat16)
    key_pair = (
        lax.all_gather(key_rows, "ctx", axis=0, tiled=True),
        lax.all_gather(hyena_stream, "ctx", axis=0, tiled=True),
    )
    scores = score_block(queries, key_pair[0], first_row, score_scale)
    row_top = jnp.max(scores, axis=2, keepdims=True)
    exponent = jnp.exp(scores - row_top)
    row_total = jnp.sum(exponent, axis=2, keepdims=True)
    probability = exponent / row_total
    prob_half = probability.astype(jnp.bfloat16)
    value_heads = key_pair[1].reshape(total_rows, head_count, DH)
    attended = jnp.einsum(
        "hts,shd->thd", prob_half, value_heads, preferred_element_type=jnp.float32
    ).reshape(local_rows, local_width)
    block_out = (hyena_stream.astype(jnp.float32) + attended).astype(jnp.bfloat16)
    again_pair = (
        lax.all_gather(key_rows, "ctx", axis=0, tiled=True),
        lax.all_gather(hyena_stream, "ctx", axis=0, tiled=True),
    )
    all_keys = again_pair[0]
    all_values = again_pair[1]
    again_scores = score_block(queries, all_keys, first_row, score_scale)
    probability = jnp.exp(again_scores - row_top) / row_total
    prob_half = probability.astype(jnp.bfloat16)
    top_grad = cotangent.astype(jnp.float32)
    key_heads = all_keys.reshape(total_rows, head_count, DH)
    value_again = all_values.reshape(total_rows, head_count, DH)
    grad_heads = cotangent.reshape(local_rows, head_count, DH)
    query_heads = queries.reshape(local_rows, head_count, DH)
    prob_grad = jnp.einsum(
        "thd,shd->hts", grad_heads, value_again, preferred_element_type=jnp.float32
    )
    row_delta = jnp.sum((top_grad * attended).reshape(local_rows, head_count, DH), axis=2).T[
        :, :, None
    ]
    score_grad = (probability * (prob_grad - row_delta)).astype(jnp.bfloat16)
    query_grad = (
        jnp.einsum("hts,shd->thd", score_grad, key_heads, preferred_element_type=jnp.float32)
        * score_scale
    )
    grad_queries = query_grad.reshape(local_rows, local_width).astype(jnp.bfloat16)
    row_count = local_rows * lax.axis_size("ctx")
    key_part = (
        jnp.einsum("hts,thd->shd", score_grad, query_heads, preferred_element_type=jnp.float32)
        * score_scale
    )
    value_part = jnp.einsum(
        "hts,thd->shd", prob_half, grad_heads, preferred_element_type=jnp.float32
    )
    pair_grads = lax.psum_scatter(
        jnp.stack(
            [key_part.reshape(row_count, local_width), value_part.reshape(row_count, local_width)],
            axis=1,
        ).astype(jnp.bfloat16),
        "ctx",
        scatter_dimension=0,
        tiled=True,
    ).astype(jnp.float32)
    grad_keys = pair_grads[:, 0].astype(jnp.bfloat16)
    stream_grad = (top_grad + pair_grads[:, 1]).astype(jnp.bfloat16)
    grad_out = stream_grad.astype(jnp.float32)
    mix_grad = (grad_out * query_mix).astype(jnp.bfloat16)
    mix_rim = shifted(mix_grad[: MRLEN - 1], "ctx", -1)
    mix_pad = jnp.concatenate([mix_grad, mix_rim], axis=0).astype(jnp.float32)
    prod_grad = anti_mix(mix_pad, mr_filter)
    mr_part = tap_grads(mix_grad.astype(jnp.float32), prod_pad)
    stack_grad = jnp.concatenate(
        [grad_out * long_mix, prod_grad * value_mix, prod_grad * key_mix], axis=1
    )
    stack_rim = shifted(as_sent(stack_grad[: SHORT - 1]), "ctx", -1)
    feat_grad = anti_mix(jnp.concatenate([stack_grad, stack_rim], axis=0), short_taps).astype(
        jnp.bfloat16
    )
    short_part = tap_grads(stack_grad, feat_pad)
    grad_mr, short_sum = (
        lax.psum(mr_part.astype(jnp.bfloat16), "ctx").astype(jnp.float32),
        lax.psum(short_part.astype(jnp.bfloat16), "ctx").astype(jnp.float32),
    )
    grad_short = short_sum.reshape(SHORT, 3, local_width)
    feat_grad3 = feat_grad.reshape(local_rows, 3, local_width)
    input_term = jnp.einsum("tjk,cjk->tc", feat_grad3, w_feat, preferred_element_type=jnp.float32)
    input_sum = lax.psum_scatter(
        input_term.astype(jnp.bfloat16), ("row", "col"), scatter_dimension=1, tiled=True
    ).astype(jnp.float32)
    grad_input = (grad_out + input_sum).astype(jnp.bfloat16)
    grad_feat = lax.psum_scatter(
        jnp.einsum(
            "tc,tjk->cjk", full_tokens, feat_grad3, preferred_element_type=jnp.float32
        ).astype(jnp.bfloat16),
        "ctx",
        scatter_dimension=0,
        tiled=True,
    ).astype(jnp.float32)
    return (block_out, grad_input, grad_feat, grad_short, grad_mr, grad_queries, grad_keys)


def solution(mesh):
    placed = (
        P("ctx", ("row", "col")),
        P(None, None, ("row", "col")),
        P(None, None, ("row", "col")),
        P(None, ("row", "col")),
        P("ctx", ("row", "col")),
        P("ctx", ("row", "col")),
        P("ctx", ("row", "col")),
    )
    return jax.shard_map(
        local,
        mesh=mesh,
        in_specs=placed,
        out_specs=(
            P("ctx", ("row", "col")),
            P("ctx", ("row", "col")),
            P("ctx", None, ("row", "col")),
            P(None, None, ("row", "col")),
            P(None, ("row", "col")),
            P("ctx", ("row", "col")),
            P("ctx", ("row", "col")),
        ),
        check_vma=False,
    )
```

profile of v0, /device:TPU:1, one launch (start us, length us, event | category | flops | bytes accessed | tf_op | source)
XLA Modules:
  0.0 652.5 jit_solution(3927335622163083156)
XLA Ops:
  9.8 39.7 %all-gather.4.cloned.1.call-done = bf16[256,4096]{1,0:T(8,128)(2,1)} async-done(((bf16[256,512]{1,0:T(8,128)(2,1)}), bf16[256,4096]{1,0:T(8,128)(2,1)}) %all-gather.4.cloned.1.call-update) | async-done | bytes 2097168 | tf_op jit(solution)/shard_map/all_gather | solution.py:86
  49.6 8.6 %fusion.27 = bf16[256,3,512]{2,0,1:T(8,128)(2,1)S(1)} fusion(bf16[4096,3,512]{2,0,1:T(8,128)(2,1)} %param.8, bf16[256,4096]{1,0:T(8,128)(2,1)} %all-gather.4.cloned.1.call-done), kind=kOutput, calls=%fused_computation.42 | convolution fusion | flops 3221618688 | bytes 15466496 | tf_op jit(solution)/shard_map/tc,cjk->tjk/dot_general | solution.py:87
  58.2 9.9 %collective-permute-start = (bf16[6,1536]{1,0:T(8,128)(2,1)S(1)}, bf16[6,1536]{1,0:T(8,128)(2,1)S(1)}, u32[]{:S(2)}, u32[]{:S(2)}) collective-permute-start(bf16[6,1536]{1,0:T(8,128)(2,1)S(1)} %bitcast.137), channel_id=1, source_target_pairs={{0,8},{8,16},{16,24},{24,32},{32,40},{40,48},{48,56},{56,64},{64,7... | collective-permute-start | bytes 55304 | tf_op jit(solution)/shard_map/ppermute | solution.py:14
  76.3 5.9 collective-permute-start.1
  84.3 5.4 fusion.43
  93.6 20.4 %all-gather.8.cloned.1.call-done = bf16[4096,512]{0,1:T(8,128)(2,1)} async-done(((bf16[256,512]{0,1:T(8,128)(2,1)}), bf16[4096,512]{0,1:T(8,128)(2,1)}) %all-gather.8.cloned.1.call-update) | async-done | bytes 4194320 | tf_op jit(solution)/shard_map/all_gather | solution.py:107
  113.9 11.8 %fusion.64 = (f32[4,256]{1,0:T(4,128)S(1)}, f32[4,256,4096]{2,1,0:T(8,128)}) fusion(pred[256,4096]{1,0:T(8,128)(4,1)} %iota_compare_fusion, bf16[256,4,128]{0,2,1:T(8,128)(2,1)S(1)} %bitcast.124, bf16[4096,4,128]{0,2,1:T(8,128)(2,1)} %bitcast.138), kind=kOutput, calls=%fused_computation.96 | convolution fusion | flops 1090523136 | bytes 22286336 | tf_op jit(solution)/shard_map/sub | solution.py:112
  125.7 6.9 %fusion.6 = bf16[4,256,4096]{2,1,0:T(8,128)(2,1)S(1)} fusion(f32[4,256,4096]{2,1,0:T(8,128)} %get-tuple-element.42, f32[4,256]{1,0:T(4,128)S(1)} %get-tuple-element.41), kind=kLoop, calls=%fused_computation.13 | loop fusion | flops 8388608 | bytes 25169920 | tf_op jit(solution)/shard_map/convert_element_type | solution.py:115
  137.1 6.6 %copy.146 = bf16[4096,1,512]{2,0,1:T(8,128)(2,1)} copy(bf16[4096,1,512]{0,2,1:T(8,128)(2,1)} %bitcast.117) | data formatting | bytes 8388608 | tf_op jit(solution)/shard_map/stack;reshape | solution.py:156
  143.7 26.4 %all-gather.6.cloned.1.call-done = bf16[4096,512]{1,0:T(8,128)(2,1)} async-done(((bf16[256,512]{1,0:T(8,128)(2,1)}), bf16[4096,512]{1,0:T(8,128)(2,1)}) %all-gather.6.cloned.1.call-update) | async-done | bytes 4194320 | tf_op jit(solution)/shard_map/all_gather | solution.py:108
  170.1 7.6 %fusion.8 = f32[4,128,256]{2,1,0:T(8,128)S(1)} fusion(bf16[4,256,4096]{2,1,0:T(8,128)(2,1)} %copy-done, bf16[4096,512]{1,0:T(8,128)(2,1)} %all-gather.6.cloned.1.call-done), kind=kOutput, calls=%fused_computation.17 | convolution fusion | flops 1073741824 | bytes 13107200 | tf_op jit(solution)/shard_map/hts,shd->thd/dot_general | solution.py:117
  179.3 10.6 %fusion.1 = bf16[4,256,4096]{2,1,0:T(8,128)(2,1)} fusion(bf16[256,4,128]{0,2,1:T(8,128)(2,1)} %bitcast.127, f32[4,256]{1,0:T(4,128)S(1)} %copy.120, f32[4,256,4096]{2,1,0:T(8,128)} %get-tuple-element.42, f32[4,256]{1,0:T(4,128)S(1)} %get-tuple-element.41, bf16[4096,512]{1,0:T(8,128)(2,1)} %all-gather.6.cloned.1.call-done), kind=kOutput, calls=%fused_computation.2 | convolution fusion | flops 1090519040 | bytes 29630464 | tf_op jit(solution)/shard_map/thd,shd->hts/dot_general | solution.py:135
  189.9 6.9 %multiply_convert_fusion = bf16[4,4096,128]{1,2,0:T(8,128)(2,1)} fusion(bf16[256,4,128]{0,2,1:T(8,128)(2,1)S(1)} %bitcast.125, bf16[4,256,4096]{2,1,0:T(8,128)(2,1)} %fusion.1), kind=kOutput, calls=%fused_computation.8 | convolution fusion | flops 1077936128 | bytes 12845056 | tf_op jit(solution)/shard_map/hts,thd->shd/dot_general | solution.py:149
  196.8 6.6 %copy.145 = bf16[4096,1,512]{2,0,1:T(8,128)(2,1)} copy(bf16[4096,1,512]{0,2,1:T(8,128)(2,1)} %bitcast.116) | data formatting | bytes 8388608 | tf_op jit(solution)/shard_map/stack;reshape | solution.py:156
  203.4 7.5 %pad_maximum_fusion = bf16[4096,2,512]{2,0,1:T(8,128)(2,1)} fusion(bf16[4096,1,512]{2,0,1:T(8,128)(2,1)} %copy.146, bf16[4096,1,512]{2,0,1:T(8,128)(2,1)} %copy.145), kind=kLoop, calls=%fused_computation.7 | loop fusion | flops 4194304 | bytes 16777216 | tf_op jit(solution)/shard_map/stack | solution.py:156
  211.0 98.8 %reduce-scatter.4.cloned.1.call-done = bf16[256,2,512]{2,0,1:T(8,128)(2,1)} async-done(((bf16[4096,2,512]{2,0,1:T(8,128)(2,1)}), bf16[256,2,512]{2,0,1:T(8,128)(2,1)}) %reduce-scatter.4.cloned.1.call-update) | async-done | bytes 524304 | tf_op jit(solution)/shard_map/reduce_scatter | solution.py:155
  326.4 7.0 %fusion.41 = bf16[1,128,512]{2,0,1:T(2,128)(2,1)S(1)} fusion(bf16[1,383,512]{2,1,0:T(8,128)(2,1)S(1)} %copy-done.11, bf16[256,1,512]{2,0,1:T(8,128)(2,1)S(1)} %bitcast.123), kind=kOutput, calls=%fused_computation.60 | convolution fusion | flops 33554432 | bytes 785408 | tf_op jit(solution)/shard_map/conv_general_dilated | solution.py:52
  346.3 14.2 %fusion.7 = bf16[256,4096]{1,0:T(8,128)(2,1)} fusion(bf16[256,3,512]{0,2,1:T(8,128)(2,1)S(1)} %bitcast.118, bf16[4096,3,512]{2,0,1:T(8,128)(2,1)} %param.8), kind=kOutput, calls=%fused_computation.16 | convolution fusion | flops 3222274048 | bytes 15466496 | tf_op jit(solution)/shard_map/tjk,cjk->tc/dot_general | solution.py:186
  360.5 8.2 %convert_bitcast_fusion = bf16[4096,3,512]{0,2,1:T(8,128)(2,1)} fusion(bf16[256,3,512]{0,2,1:T(8,128)(2,1)S(1)} %bitcast.119, bf16[256,4096]{1,0:T(8,128)(2,1)} %all-gather.4.cloned.1.call-done), kind=kOutput, calls=%fused_computation.6 | convolution fusion | flops 3227516928 | bytes 15466496 | tf_op jit(solution)/shard_map/tc,tjk->cjk/dot_general | solution.py:192
  368.8 8.3 %fusion.30 = bf16[4,256,128]{1,2,0:T(8,128)(2,1)} fusion(bf16[4,256,4096]{2,1,0:T(8,128)(2,1)} %fusion.1, bf16[4096,4,128]{0,2,1:T(8,128)(2,1)} %bitcast.139), kind=kOutput, calls=%fused_computation.44 | convolution fusion | flops 1074003968 | bytes 12845056 | tf_op jit(solution)/shard_map/hts,shd->thd/dot_general | solution.py:143
  383.5 60.3 %psum.14 = bf16[7,3,512]{2,1,0:T(4,128)(2,1)S(1)} all-reduce(bf16[7,3,512]{2,1,0:T(4,128)(2,1)S(1)} %reshape.90), channel_id=1, replica_groups=mesh['ctx'=16,'row'=2,'col'=4] {'ctx'}, use_global_device_ids=true, to_apply=%region_6.7 | all-reduce | flops 10752 | bytes 43008 | tf_op jit(solution)/shard_map/psum | solution.py:182
  444.4 27.1 %all-reduce.2.cloned.1.call-done = bf16[128,512]{1,0:T(8,128)(2,1)} async-done(((bf16[128,512]{1,0:T(8,128)(2,1)}), bf16[128,512]{1,0:T(8,128)(2,1)}) %all-reduce.2.cloned.1.call-update) | async-done | bytes 131088 | tf_op jit(solution)/shard_map/psum | solution.py:181
  473.1 39.3 %reduce-scatter.6.cloned.1.call-done = bf16[256,512]{1,0:T(8,128)(2,1)} async-done(((bf16[256,4096]{1,0:T(8,128)(2,1)}), bf16[256,512]{1,0:T(8,128)(2,1)}) %reduce-scatter.6.cloned.1.call-update) | async-done | bytes 262160 | tf_op jit(solution)/shard_map/reduce_scatter | solution.py:187
  514.1 128.7 %reduce-scatter.8.cloned.1.call-done = bf16[256,3,512]{0,2,1:T(8,128)(2,1)} async-done(((bf16[4096,3,512]{0,2,1:T(8,128)(2,1)}), bf16[256,3,512]{0,2,1:T(8,128)(2,1)}) %reduce-scatter.8.cloned.1.call-update) | async-done | bytes 786448 | tf_op jit(solution)/shard_map/reduce_scatter | solution.py:191
  (114 shorter events, 65.1 us)
Async XLA Ops:
  7.2 42.4 %all-gather.4.cloned.1.call-start = ((), (), s32[]{:S(2)}) async-start(), calls=%async_computation.3 | async-start | bytes 2359296 | tf_op jit(solution)/shard_map/all_gather | solution.py:86
  7.9 106.0 %all-gather.8.cloned.1.call-start = ((), (), s32[]{:S(2)}) async-start(), calls=%async_computation.5 | async-start | bytes 4456448 | tf_op jit(solution)/shard_map/all_gather | solution.py:107
  9.8 58.4 %copy-start.14 = (f32[7,3,512]{2,0,1:T(8,128)S(1)}, f32[7,3,512]{2,0,1:T(8,128)}, u32[]{:S(2)}) copy-start(f32[7,3,512]{2,0,1:T(8,128)} %param.9) | copy-start | bytes 129028
  9.8 160.3 %all-gather.6.cloned.1.call-start = ((), (), s32[]{:S(2)}) async-start(), calls=%async_computation.4 | async-start | bytes 4456448 | tf_op jit(solution)/shard_map/all_gather | solution.py:108
  58.2 10.9 %collective-permute-start = (bf16[6,1536]{1,0:T(8,128)(2,1)S(1)}, bf16[6,1536]{1,0:T(8,128)(2,1)S(1)}, u32[]{:S(2)}, u32[]{:S(2)}) collective-permute-start(bf16[6,1536]{1,0:T(8,128)(2,1)S(1)} %bitcast.137), channel_id=1, source_target_pairs={{0,8},{8,16},{16,24},{24,32},{32,40},{40,48},{48,56},{56,64},{64,7... | collective-permute-start | bytes 55304 | tf_op jit(solution)/shard_map/ppermute | solution.py:14
  73.2 9.1 %copy-start.12 = (f32[128,512]{1,0:T(8,128)S(1)}, f32[128,512]{1,0:T(8,128)}, u32[]{:S(2)}) copy-start(f32[128,512]{1,0:T(8,128)} %param.10) | copy-start | bytes 786436
  76.3 7.9 %collective-permute-start.1 = (bf16[127,512]{1,0:T(8,128)(2,1)S(1)}, bf16[127,512]{1,0:T(8,128)(2,1)S(1)}, u32[]{:S(2)}, u32[]{:S(2)}) collective-permute-start(bf16[127,512]{1,0:T(8,128)(2,1)S(1)} %slice.55), channel_id=1, source_target_pairs={{0,8},{8,16},{16,24},{24,32},{32,40},{40,48},{48,56},{56,64},{64,7... | collective-permute-start | bytes 390152 | tf_op jit(solution)/shard_map/ppermute | solution.py:14
  84.3 5.4 copy-start.10
  84.3 5.4 copy-start.9
  84.3 7.5 %copy-start.1 = (bf16[256,512]{1,0:T(8,128)(2,1)S(1)}, bf16[256,512]{1,0:T(8,128)(2,1)}, u32[]{:S(2)}) copy-start(bf16[256,512]{1,0:T(8,128)(2,1)} %param.13) | copy-start | bytes 786436
  89.7 36.0 %copy-start.5 = (f32[1,256,512]{2,0,1:T(1,128)}, f32[1,256,512]{2,0,1:T(1,128)S(1)}, u32[]{:S(2)}) copy-start(f32[1,256,512]{2,0,1:T(1,128)S(1)} %fusion.43) | copy-start | bytes 1572868
  90.6 219.2 %reduce-scatter.4.cloned.1.call-start = ((), (), s32[]{:S(2)}) async-start(), calls=%async_computation.6 | async-start | bytes 8912896 | tf_op jit(solution)/shard_map/reduce_scatter | solution.py:155
  91.9 40.7 %copy-start.8 = (bf16[256,512]{0,1:T(8,128)(2,1)}, bf16[256,512]{0,1:T(8,128)(2,1)S(1)}, u32[]{:S(2)}) copy-start(bf16[256,512]{0,1:T(8,128)(2,1)S(1)} %copy.152) | copy-start | bytes 786436
  132.6 4.5 copy-start
  143.7 34.2 %copy-start.4 = (bf16[256,512]{1,0:T(8,128)(2,1)S(1)}, bf16[256,512]{1,0:T(8,128)(2,1)}, u32[]{:S(2)}) copy-start(bf16[256,512]{1,0:T(8,128)(2,1)} %fusion.49) | copy-start | bytes 786436
  210.9 98.9 %copy-start.6 = (f32[1,256,512]{2,0,1:T(1,128)S(1)}, f32[1,256,512]{2,0,1:T(1,128)}, u32[]{:S(2)}) copy-start(f32[1,256,512]{2,0,1:T(1,128)} %copy-done.5) | copy-start | bytes 1572868
  210.9 107.9 %copy-start.13 = (f32[128,512]{1,0:T(8,128)S(1)}, f32[128,512]{1,0:T(8,128)}, u32[]{:S(2)}) copy-start(f32[128,512]{1,0:T(8,128)} %param.10) | copy-start | bytes 786436
  210.9 260.5 %all-reduce.2.cloned.1.call-start = ((), (), s32[]{:S(2)}) async-start(), calls=%async_computation.9 | async-start | bytes 262144 | tf_op jit(solution)/shard_map/psum | solution.py:181
  310.9 7.8 %collective-permute-start.2 = (bf16[127,512]{1,0:T(8,128)(2,1)S(1)}, bf16[127,512]{1,0:T(8,128)(2,1)S(1)}, u32[]{:S(2)}, u32[]{:S(2)}) collective-permute-start(bf16[127,512]{1,0:T(8,128)(2,1)S(1)} %slice.57), channel_id=1, source_target_pairs={{8,0},{16,8},{24,16},{32,24},{40,32},{48,40},{56,48},{64,56},{72,6... | collective-permute-start | bytes 390152 | tf_op jit(solution)/shard_map/ppermute | solution.py:14
  324.4 10.4 %collective-permute-start.3 = (bf16[6,1536]{1,0:T(8,128)(2,1)S(1)}, bf16[6,1536]{1,0:T(8,128)(2,1)S(1)}, u32[]{:S(2)}, u32[]{:S(2)}) collective-permute-start(bf16[6,1536]{1,0:T(8,128)(2,1)S(1)} %slice.80), channel_id=1, source_target_pairs={{8,0},{16,8},{24,16},{32,24},{40,32},{48,40},{56,48},{64,56},{72,6... | collective-permute-start | bytes 55304 | tf_op jit(solution)/shard_map/ppermute | solution.py:14
  334.7 177.7 %reduce-scatter.6.cloned.1.call-start = ((), (), s32[]{:S(2)}) async-start(), calls=%async_computation.7 | async-start | bytes 2359296 | tf_op jit(solution)/shard_map/reduce_scatter | solution.py:187
  360.5 282.3 %reduce-scatter.8.cloned.1.call-start = ((), (), s32[]{:S(2)}) async-start(), calls=%async_computation.8 | async-start | bytes 13369344 | tf_op jit(solution)/shard_map/reduce_scatter | solution.py:191
  368.8 10.2 %copy-start.7 = (bf16[256,2,512]{2,0,1:T(8,128)(2,1)S(1)}, bf16[256,2,512]{2,0,1:T(8,128)(2,1)}, u32[]{:S(2)}) copy-start(bf16[256,2,512]{2,0,1:T(8,128)(2,1)} %reduce-scatter.4.cloned.1.call-done) | copy-start | bytes 1572868
  377.0 2.7 copy-start.3
  (3 other events, 4.6 us)
Sparse Core Ops, SparseCore 0:
  9.6 39.8 all-gather.3
  52.5 61.4 all-gather.7
  117.0 53.0 all-gather.5
  211.0 98.7 reduce-scatter.3
  334.8 136.5 all-reduce.1
  473.8 38.4 reduce-scatter.5
  517.3 125.5 reduce-scatter.7
where the time goes:
time: 660 us; the launch traced here: 652 us
  waiting for transfers between devices  387 us (59%)
  matrix products  103 us (16%)
  blocking collectives  60.3 us (9%)
  local copies, waits for them, and re-layouts  41.3 us (6%)
  other arithmetic  23.7 us (4%)
  starting transfers between devices  21.7 us (3%)
  between operations  14.9 us (2%)
    reduce_scatter x1, waiting for transfers between devices, local(): lax.psum_scatter(jnp.einsum('tc,tjk->cjk', full_tokens, feat_grad3, prefe...  129 us
    reduce_scatter x1, waiting for transfers between devices, local(): lax.psum_scatter(jnp.stack([key_part.reshape(row_count, local_width), val...  98.8 us
    psum x1, blocking collectives, local(): lax.psum(short_part.astype(jnp.bfloat16), 'ctx').astype(jnp.float32)  60.3 us
    all_gather x1, waiting for transfers between devices, local(): full_tokens = lax.all_gather(tokens, ('row', 'col'), axis=1, tiled=True)  39.7 us
    reduce_scatter x1, waiting for transfers between devices, local(): lax.psum_scatter(input_term.astype(jnp.bfloat16), ('row', 'col'), scatter...  39.3 us
    psum x1, waiting for transfers between devices, local(): lax.psum(mr_part.astype(jnp.bfloat16), 'ctx').astype(jnp.float32)  27.1 us
    all_gather x1, waiting for transfers between devices, local(): lax.all_gather(hyena_stream, 'ctx', axis=0, tiled=True)  26.4 us
    ppermute x4, starting transfers between devices, shifted(): return lax.ppermute(block, axis, route)  21.4 us
  transfers between devices with their start and end apart: 11, of which 10 were waited for; matrix products, arithmetic and copies ran while one was open for 18% of the time, Pallas kernels for 0%

commit v1 on v0

v1 whole, which is shorter than its diff:
```python
import functools

import jax
import jax.numpy as jnp
from jax import lax
from jax.experimental import pallas as pl
from jax.experimental.pallas import tpu as pltpu
from jax.sharding import PartitionSpec as P

DH = 128
SHORT = 7
MRLEN = 128
HALO = 144
TAIL = 16
ROWS = 256
HEADS = 4
SLABS = 4
SLAB = ROWS * HEADS
EXT = HALO + SLAB + HALO
WIDTH = HEADS * DH
MESH = pl.DeviceIdType.MESH
BF = jnp.bfloat16
F32 = jnp.float32


def place():
    ctx = lax.axis_index("ctx")
    return lax.div(ctx, HEADS), lax.rem(ctx, HEADS)


def turn(index, step, size):
    return lax.rem(index + (step + size), size)


def at_ctx(z, a):
    return {"ctx": z * HEADS + a}


def cols(index, width=DH):
    return pl.ds(pl.multiple_of(index * width, width), width)


def rows(index, height, offset=0):
    return pl.ds(pl.multiple_of(index * height + offset, 16), height)


def greet(devices):
    barrier = pltpu.get_barrier_semaphore()
    for device in devices:
        pl.semaphore_signal(barrier, inc=1, device_id=device, device_id_type=MESH)
    pl.semaphore_wait(barrier, len(devices))


class Courier:
    def __init__(self, send, recv, local):
        self.send, self.recv, self.local = send, recv, local
        self.remote, self.here = [], []
        self.arrived = set()
        self.settled = 0

    def push(self, src, dst, device):
        k = len(self.remote)
        copy = pltpu.make_async_remote_copy(
            src_ref=src,
            dst_ref=dst,
            send_sem=self.send.at[k],
            recv_sem=self.recv.at[k],
            device_id=device,
            device_id_type=MESH,
        )
        copy.start()
        self.remote.append(copy)
        return k

    def keep(self, src, dst):
        copy = pltpu.make_async_copy(src, dst, self.local.at[len(self.here)])
        copy.start()
        self.here.append(copy)

    def arrive(self, k):
        if k not in self.arrived:
            self.arrived.add(k)
            self.remote[k].wait_recv()

    def finish(self):
        for k in range(len(self.remote)):
            self.arrive(k)
        for copy in self.remote:
            copy.wait_send()
        self.settle()

    def settle(self):
        for copy in self.here[self.settled :]:
            copy.wait()
        self.settled = len(self.here)


def exchange(body, collective_id, outs, remotes, locals_, *ins):
    def kernel(*refs):
        body(Courier(*refs[-3:]), *refs[:-3])

    return pl.pallas_call(
        kernel,
        out_shape=outs,
        in_specs=[pl.BlockSpec(memory_space=pl.ANY)] * len(ins),
        out_specs=[pl.BlockSpec(memory_space=pl.ANY)] * len(outs),
        scratch_shapes=[
            pltpu.SemaphoreType.DMA((remotes,)),
            pltpu.SemaphoreType.DMA((remotes,)),
            pltpu.SemaphoreType.DMA((locals_,)),
        ],
        compiler_params=pltpu.CompilerParams(collective_id=collective_id, has_side_effects=True),
    )(*ins)


def shape(*dims, kind=BF):
    return jax.ShapeDtypeStruct(dims, kind)


def inputs_kernel(mail, tokens, queries, keys, cot, full, th, qh, kh, ch, pieces):
    z, a = place()
    row, col = lax.axis_index("row"), lax.axis_index("col")
    other = 1 - row
    right, left = turn(col, 1, 4), turn(col, -1, 4)
    mates = [at_ctx(z, turn(a, d, HEADS)) for d in range(1, HEADS)]
    greet([{"row": other}, {"col": right}, {"col": left}] + mates)

    def block(r, c):
        return full.at[:, cols(r * 4 + c, WIDTH)]

    def half(r, c, h):
        return full.at[pl.ds(h * (ROWS // 2), ROWS // 2), cols(r * 4 + c, WIDTH)]

    up = mail.push(tokens, block(row, col), {"row": other})
    fr = mail.push(tokens, block(row, col), {"col": right})
    fl = mail.push(tokens, block(row, col), {"col": left})
    mail.keep(tokens, block(row, col))
    for src, dst in ((tokens, th), (queries, qh), (keys, kh), (cot, ch)):
        for d in range(1, HEADS):
            to = turn(a, d, HEADS)
            mail.push(src.at[:, cols(to)], dst.at[rows(a, ROWS)], at_ctx(z, to))
        mail.keep(src.at[:, cols(a)], dst.at[rows(a, ROWS)])
    mail.arrive(up)
    gr = mail.push(block(other, col), block(other, col), {"col": right})
    gl = mail.push(block(other, col), block(other, col), {"col": left})
    for r, from_left, from_right in ((row, fr, fl), (other, gr, gl)):
        mail.arrive(from_left)
        mail.push(half(r, left, 0), half(r, left, 0), {"col": right})
        mail.arrive(from_right)
        mail.push(half(r, right, 1), half(r, right, 1), {"col": left})
    mail.finish()
    for d in range(HEADS):
        for s in range(SLABS):
            mail.keep(
                full.at[:, cols(s * HEADS + turn(a, d, HEADS), ROWS)], pieces.at[d, :, pl.ds(s * ROWS, ROWS)]
            )
    mail.settle()


def slab_gather(mail, part, whole, z, a):
    up, down = turn(z, 1, SLABS), turn(z, -1, SLABS)
    mine = whole.at[rows(z, SLAB)]
    mail.keep(part, mine)
    return mail.push(part, mine, at_ctx(up, a)), mail.push(part, mine, at_ctx(down, a))


def slab_relay(mail, whole, z, a, from_down, from_up):
    up, down = turn(z, 1, SLABS), turn(z, -1, SLABS)
    half = SLAB // 2
    mail.arrive(from_down)
    lower = whole.at[pl.ds(pl.multiple_of(down * SLAB, 16), half)]
    mail.push(lower, lower, at_ctx(up, a))
    mail.arrive(from_up)
    upper = whole.at[pl.ds(pl.multiple_of(up * SLAB + half, 16), half)]
    mail.push(upper, upper, at_ctx(down, a))


def features_kernel(mail, feats, cot, kh, fx, chalo, kfull):
    z, a = place()
    up, down = turn(z, 1, SLABS), turn(z, -1, SLABS)
    peers = [at_ctx(z, turn(a, d, HEADS)) for d in range(1, HEADS)]
    peers += [at_ctx(s, b) for s in (up, down) for b in range(HEADS)]
    greet(peers)
    for d in range(1, HEADS):
        to = turn(a, d, HEADS)
        mail.push(feats.at[:, :, cols(to)], fx.at[:, rows(a, ROWS, HALO)], at_ctx(z, to))
    mail.keep(feats.at[:, :, cols(a)], fx.at[:, rows(a, ROWS, HALO)])
    keys = slab_gather(mail, kh, kfull, z, a)

    n = len(mail.remote)

    def edge(src, dst, k, b, device):
        return pltpu.make_async_remote_copy(
            src_ref=src,
            dst_ref=dst,
            send_sem=mail.send.at[k + 3 * b],
            recv_sem=mail.recv.at[k],
            device_id=device,
            device_id_type=MESH,
        )

    def first(b):
        return (
            edge(feats.at[:, pl.ds(0, HALO), pl.ds(b * DH, DH)], fx.at[:, pl.ds(HALO + SLAB, HALO)], n + 2, b, at_ctx(down, b)),
            edge(cot.at[pl.ds(0, HALO), pl.ds(b * DH, DH)], chalo, n + 3, b, at_ctx(down, b)),
        )

    def last(b):
        return (edge(feats.at[:, pl.ds(ROWS - HALO, HALO), pl.ds(b * DH, DH)], fx.at[:, pl.ds(0, HALO)], n + 4, b, at_ctx(up, b)),)

    @pl.when(a == 0)
    def _():
        for b in range(HEADS):
            for copy in first(b):
                copy.start()

    @pl.when(a == HEADS - 1)
    def _():
        for b in range(HEADS):
            for copy in last(b):
                copy.start()

    slab_relay(mail, kfull, z, a, *keys)
    mail.finish()
    for copy in first(0) + last(0):
        copy.wait_recv()

    @pl.when(a == 0)
    def _():
        for b in range(HEADS):
            for copy in first(b):
                copy.wait_send()

    @pl.when(a == HEADS - 1)
    def _():
        for b in range(HEADS):
            for copy in last(b):
                copy.wait_send()


def stream_kernel(mail, part, whole):
    z, a = place()
    greet([at_ctx(turn(z, 1, SLABS), a), at_ctx(turn(z, -1, SLABS), a)])
    slab_relay(mail, whole, z, a, *slab_gather(mail, part, whole, z, a))
    mail.finish()


def around(z, a):
    return [at_ctx(turn(z, d, SLABS), a) for d in range(1, SLABS)] + [
        at_ctx(z, turn(a, d, HEADS)) for d in range(1, HEADS)
    ]


def home(mail, src, dst, z, a):
    for d in range(1, HEADS):
        to = turn(a, d, HEADS)
        mail.push(src.at[rows(to, ROWS)], dst.at[:, cols(a)], at_ctx(z, to))
    mail.keep(src.at[rows(a, ROWS)], dst.at[:, cols(a)])


def values_kernel(mail, dv, dk, block, dq, dvr, dkr, block_home, dq_home):
    z, a = place()
    greet(around(z, a))
    for d in range(1, SLABS):
        to = turn(z, d, SLABS)
        mail.push(dv.at[pl.ds(pl.multiple_of(to * SLAB, 16), SLAB + HALO)], dvr.at[z], at_ctx(to, a))
    mail.keep(dv.at[pl.ds(pl.multiple_of(z * SLAB, 16), SLAB + HALO)], dvr.at[z])
    for d in range(1, SLABS):
        to = turn(z, d, SLABS)
        mail.push(dk.at[rows(to, SLAB)], dkr.at[z], at_ctx(to, a))
    mail.keep(dk.at[rows(z, SLAB)], dkr.at[z])
    home(mail, block, block_home, z, a)
    home(mail, dq, dq_home, z, a)
    mail.finish()


def finale_kernel(
    fg, sg, dk, small, part0, part1, part2, part3, weights,
    grad_input, grad_feat, dk_home, small_home,
    w, tq, tqt, fgall, fgm, wsend, zr1, zr2, tsend, xr1, xr2, yr, ysend, sgh, slots, total,
    send, recv, loc,
):
    mail = Courier(send, recv, loc)
    z, a = place()
    row, col = lax.axis_index("row"), lax.axis_index("col")
    side, core = lax.div(a, 2), lax.rem(a, 2)
    mate, far, far_mate = side * 2 + 1 - core, (1 - side) * 2 + core, (1 - side) * 2 + 1 - core
    up, down = turn(z, 1, SLABS), turn(z, -1, SLABS)
    right, left = turn(col, 1, 4), turn(col, -1, 4)
    half = ROWS // 2
    pair = 2 * ROWS

    mail.keep(fg, fgall.at[a])
    for d, part in enumerate((part0, part1, part2, part3)):
        mail.keep(part, tq.at[rows(turn(a, -d, HEADS), ROWS)])
    for j in range(3):
        mail.keep(weights.at[j], w.at[j])
    greet(around(z, a) + [{"row": 1 - row}, {"col": right}, {"col": left}])

    near_rows, far_rows = rows(side, pair), rows(1 - side, pair)
    to_mate = mail.push(fg, fgall.at[a], at_ctx(z, mate))
    first = mail.push(fg.at[:, far_rows], fgall.at[a, :, far_rows], at_ctx(z, far))
    second = mail.push(fg.at[:, near_rows], fgall.at[a, :, near_rows], at_ctx(z, far))
    small_in = [mail.push(small, slots.at[d - 1], at_ctx(turn(z, d, SLABS), a)) for d in range(1, SLABS)]
    home_sg = []
    for d in range(1, HEADS):
        to = turn(a, d, HEADS)
        home_sg.append(mail.push(sg.at[rows(to, ROWS)], sgh.at[:, cols(a)], at_ctx(z, to)))
        mail.push(dk.at[rows(to, ROWS)], dk_home.at[:, cols(a)], at_ctx(z, to))
    mail.keep(sg.at[rows(a, ROWS)], sgh.at[:, cols(a)])
    mail.keep(dk.at[rows(a, ROWS)], dk_home.at[:, cols(a)])
    mail.settle()

    for b in range(SLABS):
        tqt[pl.ds(b * ROWS, ROWS)] = tq[:, pl.ds(b * ROWS, ROWS)].T

    def weight_block(n, head, dz):
        rhs = jnp.concatenate([fgall[head, j] for j in range(3)], axis=1)
        lhs = tqt[rows(turn(z, dz, SLABS), ROWS)]
        out = jnp.dot(lhs, rhs, preferred_element_type=F32)
        for j in range(3):
            wsend[n, dz, j] = out[:, j * DH : (j + 1) * DH].astype(BF)

    def weight_first(n, head):
        weight_block(n, head, 2)
        keys = (
            mail.push(wsend.at[n, 2, :, pl.ds(0, half)], zr1.at[n, 0], at_ctx(up, a)),
            mail.push(wsend.at[n, 2, :, pl.ds(half, half)], zr1.at[n, 1], at_ctx(down, a)),
        )
        for dz in (1, 3, 0):
            weight_block(n, head, dz)
        return keys

    def weight_second(n, keys):
        top, bottom = pl.ds(0, half), pl.ds(half, half)
        mail.arrive(keys[0])
        wsend[n, 1, :, top] = (wsend[n, 1, :, top].astype(F32) + zr1[n, 0].astype(F32)).astype(BF)
        one = mail.push(wsend.at[n, 1], zr2.at[n, 0], at_ctx(up, a))
        mail.arrive(keys[1])
        wsend[n, 3, :, bottom] = (wsend[n, 3, :, bottom].astype(F32) + zr1[n, 1].astype(F32)).astype(BF)
        return one, mail.push(wsend.at[n, 3], zr2.at[n, 1], at_ctx(down, a))

    def weight_third(n, head, keys):
        for k in keys:
            mail.arrive(k)
        for j in range(3):
            grad_feat[j, :, cols(head)] = (
                wsend[n, 0, j].astype(F32) + zr2[n, 0, j].astype(F32) + zr2[n, 1, j].astype(F32)
            )

    ring = [weight_first(0, a)]
    mail.arrive(to_mate)
    ring.append(weight_first(1, mate))
    mail.arrive(first)
    relay = mail.push(fgall.at[far, :, near_rows], fgall.at[far, :, near_rows], at_ctx(z, mate))
    ring[0] = weight_second(0, ring[0])
    ring[1] = weight_second(1, ring[1])
    mail.arrive(relay)

    for j in range(3):
        for h in range(HEADS):
            fgm[j, :, pl.ds(h * DH, DH)] = fgall[h, j, rows(a, ROWS)]

    def term_block(dc):
        for r in range(2):
            columns = rows(r * 4 + turn(col, dc, 4), WIDTH)
            out = jnp.zeros((ROWS, WIDTH), F32)
            for j in range(3):
                out += lax.dot_general(
                    fgm[j], w[j, columns], (((1,), (1,)), ((), ())), preferred_element_type=F32
                )
            tsend[dc, r] = out.astype(BF)

    top, bottom = pl.ds(0, half), pl.ds(half, half)
    term_block(2)
    from_left = mail.push(tsend.at[2, :, top], xr1.at[0], {"col": right})
    from_right = mail.push(tsend.at[2, :, bottom], xr1.at[1], {"col": left})
    term_block(1)
    term_block(3)
    mail.arrive(from_left)
    tsend[1, :, top] = (tsend[1, :, top].astype(F32) + xr1[0].astype(F32)).astype(BF)
    from_left = mail.push(tsend.at[1], xr2.at[0], {"col": right})
    mail.arrive(from_right)
    tsend[3, :, bottom] = (tsend[3, :, bottom].astype(F32) + xr1[1].astype(F32)).astype(BF)
    from_right = mail.push(tsend.at[3], xr2.at[1], {"col": left})
    term_block(0)

    mail.arrive(second)
    relay = mail.push(fgall.at[far, :, far_rows], fgall.at[far, :, far_rows], at_ctx(z, mate))
    ring.append(weight_first(2, far))
    mail.arrive(relay)
    ring.append(weight_first(3, far_mate))
    ring[2] = weight_second(2, ring[2])
    ring[3] = weight_second(3, ring[3])

    for k in small_in:
        mail.arrive(k)
    total[...] = (small_sum(small, slots)).astype(BF)
    for d in range(1, HEADS):
        mail.push(total, small_home.at[:, cols(a)], at_ctx(z, turn(a, d, HEADS)))
    mail.keep(total, small_home.at[:, cols(a)])

    mail.arrive(from_left)
    mail.arrive(from_right)

    def term_sum(r):
        return tsend[0, r].astype(F32) + xr2[0, r].astype(F32) + xr2[1, r].astype(F32)

    ysend[...] = term_sum(1 - row).astype(BF)
    across = mail.push(ysend, yr, {"row": 1 - row})
    weight_third(0, a, ring[0])
    weight_third(1, mate, ring[1])
    for k in home_sg:
        mail.arrive(k)
    mail.arrive(across)
    grad_input[...] = (sgh[...].astype(F32) + term_sum(row) + yr[...].astype(F32)).astype(BF)
    weight_third(2, far, ring[2])
    weight_third(3, far_mate, ring[3])
    mail.finish()


def small_sum(small, slots):
    return small[...].astype(F32) + sum(slots[d].astype(F32) for d in range(SLABS - 1))


def finale(fg, sg, dk, small, parts, weights):
    lines = small.shape[0]
    any_space, vmem = pl.BlockSpec(memory_space=pl.ANY), pl.BlockSpec(memory_space=pltpu.VMEM)
    remotes = 3 + 3 + 6 + 16 + 2 + 4 + 3 + 1
    return pl.pallas_call(
        finale_kernel,
        out_shape=[
            shape(ROWS, WIDTH),
            shape(3, ROWS, WIDTH, kind=F32),
            shape(ROWS, WIDTH),
            shape(lines, WIDTH),
        ],
        in_specs=[any_space, any_space, any_space, vmem] + [any_space] * 5,
        out_specs=[vmem, vmem, any_space, any_space],
        scratch_shapes=[
            pltpu.VMEM(weights.shape, BF),
            pltpu.VMEM((SLAB, SLABS * ROWS), BF),
            pltpu.VMEM((SLABS * ROWS, SLAB), BF),
            pltpu.VMEM((HEADS, 3, SLAB, DH), BF),
            pltpu.VMEM((3, ROWS, WIDTH), BF),
            pltpu.VMEM((HEADS, SLABS, 3, ROWS, DH), BF),
            pltpu.VMEM((HEADS, 2, 3, ROWS // 2, DH), BF),
            pltpu.VMEM((HEADS, 2, 3, ROWS, DH), BF),
            pltpu.VMEM((4, 2, ROWS, WIDTH), BF),
            pltpu.VMEM((2, 2, ROWS // 2, WIDTH), BF),
            pltpu.VMEM((2, 2, ROWS, WIDTH), BF),
            pltpu.VMEM((ROWS, WIDTH), BF),
            pltpu.VMEM((ROWS, WIDTH), BF),
            pltpu.VMEM((ROWS, WIDTH), BF),
            pltpu.VMEM((SLABS - 1, lines, DH), BF),
            pltpu.VMEM((lines, DH), BF),
            pltpu.SemaphoreType.DMA((remotes,)),
            pltpu.SemaphoreType.DMA((remotes,)),
            pltpu.SemaphoreType.DMA((11,)),
        ],
        compiler_params=pltpu.CompilerParams(
            collective_id=5, has_side_effects=True, vmem_limit_bytes=56 << 20
        ),
    )(fg, sg, dk, small, *parts, weights)


def compute(body, outs, scratch, *ins, vmem=56 << 20):
    z, a = place()
    return pl.pallas_call(
        body,
        out_shape=outs,
        in_specs=[pl.BlockSpec(memory_space=pltpu.SMEM)] + [pl.BlockSpec(memory_space=pltpu.VMEM)] * len(ins),
        out_specs=[pl.BlockSpec(memory_space=pltpu.VMEM)] * len(outs),
        scratch_shapes=scratch,
        compiler_params=pltpu.CompilerParams(vmem_limit_bytes=vmem),
    )(jnp.stack([z, a]).astype(jnp.int32), *ins)


GROUP = 40


def spread_taps(spread, taps, a):
    for i in range(MRLEN):
        spread[i] = jnp.broadcast_to(taps[pl.ds(i, 1), cols(a)], (8, DH))


def hyena_body(where, fx, short, mr, tok, stream, qm, km, vm, lm, pr, feat, spread):
    z, a = where[0], where[1]
    spread_taps(spread, mr, a)
    keep_head = (z > 0).astype(F32)
    keep_tail = (z < SLABS - 1).astype(F32)
    for j in range(3):
        feat[j, pl.ds(0, HALO)] = fx[j, pl.ds(0, HALO)].astype(F32) * keep_head
        feat[j, pl.ds(HALO, SLAB)] = fx[j, pl.ds(HALO, SLAB)].astype(F32)
        feat[j, pl.ds(HALO + SLAB, HALO)] = fx[j, pl.ds(HALO + SLAB, HALO)].astype(F32) * keep_tail

    taps = [[short[j, pl.ds(s, 1), cols(a)] for s in range(SHORT)] for j in range(3)]

    def mixed(j, base, count):
        total = taps[j][0] * feat[j, pl.ds(base, count)]
        for s in range(1, SHORT):
            total += taps[j][s] * feat[j, pl.ds(base - s, count)]
        return total

    pr[pl.ds(0, 16)] = jnp.zeros((16, DH), F32)

    def head_step(g, carry):
        base = pl.multiple_of(16 + g * 16, 16)
        pr[pl.ds(base, 16)] = (mixed(1, base, 16) * mixed(2, base, 16)).astype(BF).astype(F32)
        return carry

    lax.fori_loop(0, (HALO - 16) // 16, head_step, 0)

    def mix_step(g, carry):
        base = pl.multiple_of(HALO + g * GROUP, 8)
        local = pl.multiple_of(g * GROUP, 8)
        key, value = mixed(1, base, GROUP), mixed(2, base, GROUP)
        km[pl.ds(local, GROUP)] = key
        vm[pl.ds(local, GROUP)] = value
        qm[pl.ds(local, GROUP)] = mixed(0, base, GROUP)
        pr[pl.ds(base, GROUP)] = (key * value).astype(BF).astype(F32)
        return carry

    lax.fori_loop(0, (SLAB + TAIL) // GROUP, mix_step, 0)

    def tail_step(g, carry):
        local = pl.multiple_of(SLAB + TAIL + g * 16, 16)
        qm[pl.ds(local, 16)] = mixed(0, local + HALO, 16)
        return carry

    lax.fori_loop(0, (HALO - TAIL) // 16, tail_step, 0)

    def long_step(g, carry):
        base = pl.multiple_of(HALO + g * GROUP, 8)
        local = pl.multiple_of(g * GROUP, 8)
        total = [jnp.zeros((8, DH), F32) for _ in range(GROUP // 8)]
        for i in range(MRLEN):
            tap = spread[i]
            for n in range(GROUP // 8):
                total[n] += tap * pr[pl.ds(base + (n * 8 - i), 8)]
        for n in range(GROUP // 8):
            lm[pl.ds(local + n * 8, 8)] = total[n]
        return carry

    lax.fori_loop(0, (SLAB + TAIL) // GROUP, long_step, 0)
    own = pl.ds(0, SLAB)
    stream[...] = (tok[...].astype(F32) + qm[own] * lm[own]).astype(BF)


def attention_body(where, q, k, v, ct, own_stream, block, dq, dk, dv, st, pt, kt, vt, dka, dva):
    z = where[0]
    scale = DH ** -0.5
    gain = scale * 1.4426950408889634
    dka[...] = jnp.zeros_like(dka)
    dva[...] = jnp.zeros_like(dva)
    kt[...] = k[...].T
    vt[...] = v[...].T

    def dot(x, y):
        return jnp.dot(x, y, preferred_element_type=F32)

    def dot_t(x, y):
        return lax.dot_general(x, y, (((1,), (1,)), ((), ())), preferred_element_type=F32)

    for i in range(HEADS):
        span = ROWS * (i + 1)
        here = pl.ds(i * ROWS, ROWS)
        qb, cb = q[here], ct[here]
        own = pl.ds(pl.multiple_of(z * SLAB, SLAB), span)
        own_lanes = pl.ds(pl.multiple_of(z * SLAB, SLAB), span)
        scores = dot_t(k[own], qb)
        after = lax.broadcasted_iota(jnp.int32, (ROWS, ROWS), 0) > lax.broadcasted_iota(jnp.int32, (ROWS, ROWS), 1)
        corner = jnp.where(after, -1e30, scores[span - ROWS :])
        top = jnp.max(corner, axis=0, keepdims=True)
        if i:
            top = jnp.maximum(top, jnp.max(scores[: span - ROWS], axis=0, keepdims=True))
            st[pl.ds(0, span - ROWS)] = scores[: span - ROWS]
        st[pl.ds(span - ROWS, ROWS)] = corner

        def score_step(s, top):
            past = dot_t(k[pl.ds(pl.multiple_of(s * SLAB, SLAB), SLAB)], qb)
            st[pl.ds(pl.multiple_of((s + 1) * SLAB, SLAB), SLAB)] = past
            return jnp.maximum(top, jnp.max(past, axis=0, keepdims=True))

        top = lax.fori_loop(0, z, score_step, top) * gain

        def weigh(slots, lanes, total, out):
            p = jnp.exp2(st[slots] * gain - top)
            total += jnp.sum(p, axis=0, keepdims=True)
            p = p.astype(BF)
            pt[slots] = p
            return total, out + dot(vt[:, lanes], p)

        carry = weigh(pl.ds(0, span), own_lanes, jnp.zeros((1, ROWS), F32), jnp.zeros((DH, ROWS), F32))

        def weigh_step(s, carry):
            return weigh(
                pl.ds(pl.multiple_of((s + 1) * SLAB, SLAB), SLAB), pl.ds(pl.multiple_of(s * SLAB, SLAB), SLAB), *carry
            )

        total, out = lax.fori_loop(0, z, weigh_step, carry)
        inverse = 1.0 / total
        out = out * inverse
        block[here] = (own_stream[here].astype(F32) + out.T).astype(BF)
        ctt = (cb.astype(F32).T * inverse).astype(BF)
        delta = jnp.sum(ctt.astype(F32) * out, axis=0, keepdims=True)
        cs = ctt.T

        def grads(slots, lanes, dqt):
            p = pt[slots]
            dva[lanes] += dot(p, cs)
            dp = dot(v[lanes], ctt)
            ds = (p.astype(F32) * (dp - delta)).astype(BF)
            dka[lanes] += dot(ds, qb)
            return dqt + dot(kt[:, lanes], ds)

        dqt = grads(pl.ds(0, span), own, jnp.zeros((DH, ROWS), F32))

        def grad_step(s, dqt):
            return grads(
                pl.ds(pl.multiple_of((s + 1) * SLAB, SLAB), SLAB), pl.ds(pl.multiple_of(s * SLAB, SLAB), SLAB), dqt
            )

        dqt = lax.fori_loop(0, z, grad_step, dqt)
        dq[here] = (dqt.T * scale).astype(BF)
    dk[...] = (dka[...] * scale).astype(BF)
    whole = SLABS * SLAB
    dv[pl.ds(0, whole)] = dva[...].astype(BF)
    dv[pl.ds(whole, HALO)] = jnp.zeros((HALO, DH), BF)


def back_body(where, dvr, dkr, ch, chalo, fx, short, mr, qm, km, vm, lm, pr, sg, fg, dk, small, mg, stack, feat, spread):
    z, a = where[0], where[1]
    spread_taps(spread, mr, a)
    keep_head = (z > 0).astype(F32)
    keep_tail = (z < SLABS - 1).astype(F32)
    own, halo = pl.ds(0, SLAB), pl.ds(SLAB, HALO)

    def value_sum(part):
        return sum(dvr[s, part].astype(F32) for s in range(SLABS))

    dk[...] = sum(dkr[s].astype(F32) for s in range(SLABS)).astype(BF)
    grad = (ch[...].astype(F32) + value_sum(own)).astype(BF)
    sg[...] = grad
    mg[own] = (grad.astype(F32) * qm[own]).astype(BF).astype(F32)
    grad_halo = (chalo[...].astype(F32) + value_sum(halo)).astype(BF).astype(F32) * keep_tail
    mg[halo] = (grad_halo * qm[halo]).astype(BF).astype(F32)
    stack[0, own] = grad.astype(F32) * lm[own]
    stack[0, pl.ds(SLAB, TAIL)] = grad_halo[:TAIL] * lm[pl.ds(SLAB, TAIL)]
    for j in range(3):
        feat[j, pl.ds(0, 16)] = fx[j, pl.ds(HALO - 16, 16)].astype(F32) * keep_head
        feat[j, pl.ds(16, SLAB)] = fx[j, pl.ds(HALO, SLAB)].astype(F32)

    def long_step(g, carry):
        local = pl.multiple_of(g * GROUP, 8)
        total = [jnp.zeros((8, DH), F32) for _ in range(GROUP // 8)]
        for i in range(MRLEN):
            tap = spread[i]
            for n in range(GROUP // 8):
                total[n] += tap * mg[pl.ds(local + (n * 8 + i), 8)]
        for n in range(GROUP // 8):
            part = pl.ds(local + n * 8, 8)
            stack[1, part] = total[n] * vm[part]
            stack[2, part] = total[n] * km[part]
        return carry

    lax.fori_loop(0, (SLAB + TAIL) // GROUP, long_step, 0)

    for j in range(3):
        taps = [short[j, pl.ds(s, 1), cols(a)] for s in range(SHORT)]

        def short_step(g, sums):
            base = pl.multiple_of(g * 32, 32)
            total = taps[0] * stack[j, pl.ds(base, 32)]
            for s in range(1, SHORT):
                total += taps[s] * stack[j, pl.ds(base + s, 32)]
            fg[j, pl.ds(base, 32)] = total.astype(BF)
            out = []
            for s in range(SHORT):
                term = stack[j, pl.ds(base, 32)] * feat[j, pl.ds(base + 16 - s, 32)]
                out.append(sums[s] + (term[0:8] + term[8:16] + term[16:24] + term[24:32]))
            return tuple(out)

        sums = lax.fori_loop(0, SLAB // 32, short_step, tuple(jnp.zeros((8, DH), F32) for _ in range(SHORT)))
        lines = [jnp.sum(t, axis=0, keepdims=True) for t in sums]
        small[pl.ds(MRLEN + 16 * j, 16)] = jnp.concatenate(lines + [jnp.zeros((16 - SHORT, DH), F32)], axis=0).astype(BF)

    def tap_step(c, carry):
        first = c * 16

        def row_step(g, sums):
            base = pl.multiple_of(g * 16, 16)
            out = list(sums)
            for n in range(2):
                line = mg[pl.ds(base + n * 8, 8)]
                for s in range(16):
                    out[s] += line * pr[pl.ds(base + (HALO + n * 8 - s) - first, 8)]
            return tuple(out)

        sums = lax.fori_loop(0, SLAB // 16, row_step, tuple(jnp.zeros((8, DH), F32) for _ in range(16)))
        lines = [jnp.sum(t, axis=0, keepdims=True) for t in sums]
        small[pl.ds(pl.multiple_of(first, 16), 16)] = jnp.concatenate(lines, axis=0).astype(BF)
        return carry

    lax.fori_loop(0, MRLEN // 16, tap_step, 0)


def local(tokens, w_feat, short_filter, mr_filter, queries, key_rows, cotangent):
    weights = w_feat.transpose(1, 0, 2)
    short_taps = short_filter.transpose(1, 0, 2)
    head = shape(SLAB, DH)
    full, th, qh, kh, ch, pieces = exchange(
        inputs_kernel, 0, [shape(ROWS, 8 * WIDTH), head, head, head, head, shape(HEADS, ROWS, SLABS * ROWS)], 21, 5 + HEADS * SLABS, tokens, queries, key_rows, cotangent
    )
    feats = jnp.einsum("tc,jck->jtk", full, weights, preferred_element_type=F32).astype(BF)
    fx, chalo, kfull = exchange(
        features_kernel, 1, [shape(3, EXT, DH), shape(HALO, DH), shape(SLABS * SLAB, DH)], 19, 2, feats, cotangent, kh
    )
    pieces, fx = lax.optimization_barrier((pieces, fx))
    token_parts = [pieces[0]]
    for d in range(1, HEADS):
        route = [(s * HEADS + a, s * HEADS + (a + d) % HEADS) for s in range(SLABS) for a in range(HEADS)]
        token_parts.append(lax.ppermute(pieces[d], "ctx", route))
    filters = [pltpu.VMEM((MRLEN, 8, DH), F32)]
    stream, qm, km, vm, lm, pr = compute(
        hyena_body,
        [
            head,
            shape(SLAB + HALO, DH, kind=F32),
            shape(SLAB + TAIL, DH, kind=F32),
            shape(SLAB + TAIL, DH, kind=F32),
            shape(SLAB + TAIL, DH, kind=F32),
            shape(HALO + SLAB + TAIL, DH, kind=F32),
        ],
        [pltpu.VMEM((3, EXT, DH), F32)] + filters,
        fx,
        short_taps,
        mr_filter,
        th,
    )
    (vfull,) = exchange(stream_kernel, 2, [shape(SLABS * SLAB, DH)], 4, 1, stream)
    whole = SLABS * SLAB
    block, dq, dk, dv = compute(
        attention_body,
        [head, head, shape(whole, DH), shape(whole + HALO, DH)],
        [
            pltpu.VMEM((whole + SLAB, ROWS), F32),
            pltpu.VMEM((whole + SLAB, ROWS), BF),
            pltpu.VMEM((DH, whole), BF),
            pltpu.VMEM((DH, whole), BF),
            pltpu.VMEM((whole, DH), F32),
            pltpu.VMEM((whole, DH), F32),
        ],
        qh,
        kfull,
        vfull,
        ch,
        stream,
    )
    mine = shape(ROWS, WIDTH)
    dvr, dkr, block_out, grad_queries = exchange(
        values_kernel,
        3,
        [shape(SLABS, SLAB + HALO, DH), shape(SLABS, SLAB, DH), mine, mine],
        12,
        4,
        dv,
        dk,
        block,
        dq,
    )
    sg, fg, dk_sum, small = compute(
        back_body,
        [head, shape(3, SLAB, DH), head, shape(MRLEN + 3 * 16, DH)],
        [
            pltpu.VMEM((SLAB + HALO, DH), F32),
            pltpu.VMEM((3, SLAB + TAIL, DH), F32),
            pltpu.VMEM((3, SLAB + 16, DH), F32),
        ]
        + filters,
        dvr,
        dkr,
        ch,
        chalo,
        fx,
        short_taps,
        mr_filter,
        qm,
        km,
        vm,
        lm,
        pr,
    )
    grad_input, grad_feat, grad_keys, small_home = finale(fg, sg, dk_sum, small, token_parts, weights)
    sums = small_home.astype(F32)
    grad_short = sums[MRLEN:].reshape(3, 16, WIDTH)[:, :SHORT].transpose(1, 0, 2)
    grad_feat = grad_feat.transpose(1, 0, 2)
    grad_mr = sums[:MRLEN]
    return (block_out, grad_input, grad_feat, grad_short, grad_mr, grad_queries, grad_keys)


def solution(mesh):
    placed = (
        P("ctx", ("row", "col")),
        P(None, None, ("row", "col")),
        P(None, None, ("row", "col")),
        P(None, ("row", "col")),
        P("ctx", ("row", "col")),
        P("ctx", ("row", "col")),
        P("ctx", ("row", "col")),
    )
    return jax.shard_map(
        local,
        mesh=mesh,
        in_specs=placed,
        out_specs=(
            P("ctx", ("row", "col")),
            P("ctx", ("row", "col")),
            P("ctx", None, ("row", "col")),
            P(None, None, ("row", "col")),
            P(None, ("row", "col")),
            P("ctx", ("row", "col")),
            P("ctx", ("row", "col")),
        ),
        check_vma=False,
    )
```

time: 660 us -> 295 us (0.45); the launches traced: 652 us -> 295 us
  waiting for transfers between devices: 387 us -> 0.01 us
  Pallas kernels: 0 us -> 269 us
  matrix products: 103 us -> 9.64 us
  blocking collectives: 60.3 us -> 0 us
  local copies, waits for them, and re-layouts: 41.3 us -> 10.5 us
  other arithmetic: 23.7 us -> 0.58 us
  starting transfers between devices: 21.7 us -> 4.95 us
  between operations: 14.9 us -> 0.75 us
    pallas_call x0 -> x8, Pallas kernels: none -> 269 us  [the longest x4 174 us: exchange(): pl.pallas_call(kernel, out_shape=outs, in_specs=[pl.BlockSpec(memory_spac...]
    reduce_scatter x3 -> x0, waiting for transfers between devices: 267 us -> none  [the longest x1 129 us: local(): lax.psum_scatter(jnp.einsum('tc,tjk->cjk', full_tokens, feat_grad3, prefe...]
    all_gather x3 -> x0, waiting for transfers between devices: 86.5 us -> none  [the longest x1 39.7 us: local(): full_tokens = lax.all_gather(tokens, ('row', 'col'), axis=1, tiled=True)]
    psum x1 -> x0, blocking collectives: 60.3 us -> none  [local(): lax.psum(short_part.astype(jnp.bfloat16), 'ctx').astype(jnp.float32)]
    dot_general x8 -> x1, matrix products: 68 us -> 9.64 us  [local(): jnp.einsum('tc,jck->jtk', full, weights, preferred_element_type=F32)]
    psum x1 -> x0, waiting for transfers between devices: 27.1 us -> none  [local(): lax.psum(mr_part.astype(jnp.bfloat16), 'ctx').astype(jnp.float32)]
    conv_general_dilated x6 -> x0, matrix products: 23.5 us -> none  [the longest x2 10.3 us: tap_grads(): lax.conv_general_dilated(padded[None], kernel, (1,), 'VALID', dimension_n...]
    ppermute x4 -> x3, starting transfers between devices: 21.4 us -> 4.95 us  [local(): token_parts.append(lax.ppermute(pieces[d], 'ctx', route))]
  transfers between devices with their start and end apart: 11 -> 3, of which waited for: 10 -> 0; matrix products, arithmetic and copies ran while one was open for 18% -> 0% of each run, Pallas kernels for 0% -> 37%
where the time goes in v1:
time: 295 us
  Pallas kernels  269 us (91%)
  local copies, waits for them, and re-layouts  10.5 us (4%)
  matrix products  9.64 us (3%)
  starting transfers between devices  4.95 us (2%)
    pallas_call x4, Pallas kernels, exchange(): pl.pallas_call(kernel, out_shape=outs, in_specs=[pl.BlockSpec(memory_spac...  174 us
    pallas_call x1, Pallas kernels, finale(): pl.pallas_call(finale_kernel, out_shape=[shape(ROWS, WIDTH), shape(3, ROW...  47.8 us
    pallas_call x3, Pallas kernels, compute(): pl.pallas_call(body, out_shape=outs, in_specs=[pl.BlockSpec(memory_space=...  47 us
    dot_general x1, matrix products, local(): jnp.einsum('tc,jck->jtk', full, weights, preferred_element_type=F32)  9.64 us
    unnamed x21, local copies, waits for them, and re-layouts  6.12 us
  transfers between devices with their start and end apart: 3, of which 0 were waited for; matrix products, arithmetic and copies ran while one was open for 0% of the time, Pallas kernels for 37%

profile of v1, /device:TPU:1, one launch (start us, length us, event | category | flops | bytes accessed | tf_op | source)
XLA Modules:
  0.0 295.2 jit_solution(5767908280411468213)
XLA Ops:
  0.6 90.5 %shard_map.126 = (bf16[256,4096]{1,0:T(8,128)(2,1)}, bf16[1024,128]{1,0:T(8,128)(2,1)}, bf16[1024,128]{1,0:T(8,128)(2,1)}, bf16[1024,128]{1,0:T(8,128)(2,1)}, bf...) custom-call(bf16[256,512]{1,0:T(8,128)(2,1)} %refs_0_.1, bf16[256,512]{1,0:T(8,128)(2,1)} %refs_1_.2, ...), custom_call_target="tpu_custom_call" | custom-call | tf_op jit(solution)/shard_map/pallas_call | solution.py:102
  91.1 9.6 %fusion.5.refs_0_ = bf16[3,256,512]{2,1,0:T(8,128)(2,1)} fusion(bf16[256,4096]{1,0:T(8,128)(2,1)} %get-tuple-element.41, bf16[4096,3,512]{2,0,1:T(8,128)(2,1)} %param.8), kind=kOutput, calls=%fused_computation.3 | convolution fusion | flops 3221618688 | bytes 15466496 | tf_op jit(solution)/shard_map/tc,jck->jtk/dot_general | solution.py:715
  100.8 22.4 %shard_map.127 = (bf16[3,1312,128]{2,1,0:T(8,128)(2,1)}, bf16[144,128]{1,0:T(8,128)(2,1)}, bf16[4096,128]{1,0:T(8,128)(2,1)}) custom-call(bf16[3,256,512]{2,1,0:T(8,128)(2,1)} %fusion.5.refs_0_, bf16[256,512]{1,0:T(8,128)(2,1)} %refs_1_.3, bf16[1024,128]{1,0:T(8,128)(2,1)} %get-tuple-element.42.refs_2_), custom_call_target="tpu_custom_call" | custom-call | tf_op jit(solution)/shard_map/pallas_call | solution.py:102
  123.1 1.2 slice_bitcast_fusion
  124.3 0.4 collective-permute-start.2
  124.7 2.1 collective-permute-start.1
  126.9 2.4 collective-permute-start
  129.3 0.6 pad_add_fusion.where
  129.9 13.3 %shard_map.128 = (bf16[1024,128]{1,0:T(8,128)(2,1)}, f32[1168,128]{1,0:T(8,128)}, f32[1040,128]{1,0:T(8,128)}, f32[1040,128]{1,0:T(8,128)}, f32[1040,128]{1,0:T(8,128)}, /*index=5*/f32[1184,128]{1,0:T(8,128)}) custom-call(s32[2]{0:T(128)} %pad_add_fusion.where, bf16[3,1312,128]{2,1,0:T(8,128)(2,1)} %get-tuple-element.46.fx, f32[3,7,512]{2,1,0:T(8,128)} %bitcast.30, ...), custom_call_target="tpu_custom_call" | custom-call | tf_op jit(solution)/shard_map/pallas_call | solution.py:469
  143.2 12.4 %shard_map.129.v = bf16[4096,128]{1,0:T(8,128)(2,1)} custom-call(bf16[1024,128]{1,0:T(8,128)(2,1)} %get-tuple-element.48.refs_0_.own_stream), custom_call_target="tpu_custom_call" | custom-call | tf_op jit(solution)/shard_map/pallas_call | solution.py:102
  155.6 9.0 %shard_map.130 = (bf16[1024,128]{1,0:T(8,128)(2,1)}, bf16[1024,128]{1,0:T(8,128)(2,1)}, bf16[4096,128]{1,0:T(8,128)(2,1)}, bf16[4240,128]{1,0:T(8,128)(2,1)}) custom-call(s32[2]{0:T(128)} %pad_add_fusion.where, bf16[1024,128]{1,0:T(8,128)(2,1)} %get-tuple-element.40.q, bf16[4096,128]{1,0:T(8,128)(2,1)} %get-tuple-element.43.k, ...), custom_call_target="tpu_custom_call" | custom-call | tf_op jit(solution)/shard_map/pallas_call | solution.py:469
  164.6 48.7 %shard_map.131 = (bf16[4,1168,128]{2,1,0:T(8,128)(2,1)}, bf16[4,1024,128]{2,1,0:T(8,128)(2,1)}, bf16[256,512]{1,0:T(8,128)(2,1)}, bf16[256,512]{1,0:T(8,128)(2,1)}) custom-call(bf16[4240,128]{1,0:T(8,128)(2,1)} %get-tuple-element.50.refs_0_, bf16[4096,128]{1,0:T(8,128)(2,1)} %get-tuple-element.51.refs_1_, bf16[1024,128]{1,0:T(8,128)(2,1)} %get-tuple-element.52.refs_2_, ...), custom_call_target="tpu_custom_call" | custom-call | tf_op jit(solution)/shard_map/pallas_call | solution.py:102
  213.3 24.7 %shard_map.132 = (bf16[1024,128]{1,0:T(8,128)(2,1)}, bf16[3,1024,128]{2,1,0:T(8,128)(2,1)}, bf16[1024,128]{1,0:T(8,128)(2,1)}, bf16[176,128]{1,0:T(8,128)(2,1)}) custom-call(s32[2]{0:T(128)} %pad_add_fusion.where, bf16[4,1168,128]{2,1,0:T(8,128)(2,1)} %get-tuple-element.55.dvr, bf16[4,1024,128]{2,1,0:T(8,128)(2,1)} %get-tuple-element.56.dkr, ...), custom_call_target="tpu_custom_call" | custom-call | tf_op jit(solution)/shard_map/pallas_call | solution.py:469
  238.1 0.8 copy-done.2
  239.0 0.2 copy-done.4
  239.2 47.8 %shard_map.133 = (bf16[256,512]{1,0:T(8,128)(2,1)}, f32[3,256,512]{2,1,0:T(8,128)}, bf16[256,512]{1,0:T(8,128)(2,1)}, bf16[176,512]{1,0:T(8,128)(2,1)}) custom-call(bf16[3,1024,128]{2,1,0:T(8,128)(2,1)} %get-tuple-element.63.fg, bf16[1024,128]{1,0:T(8,128)(2,1)} %get-tuple-element.64.sg, bf16[1024,128]{1,0:T(8,128)(2,1)} %get-tuple-element.65.dk, ...), custom_call_target="tpu_custom_call" | custom-call | tf_op jit(solution)/shard_map/pallas_call | solution.py:430
  287.0 0.9 slice.28
  287.9 1.6 slice.30
  289.6 0.6 slice_bitcast_fusion.4
  290.2 0.7 copy.19
  290.9 1.7 copy.20
  292.6 1.1 copy.21
  293.8 0.7 copy.22
  294.5 0.7 copy.23
  (17 shorter events, 0.2 us)
Async XLA Ops:
  91.1 32.0 %copy-start = (bf16[4,256,1024]{2,1,0:T(8,128)(2,1)S(1)}, bf16[4,256,1024]{2,1,0:T(8,128)(2,1)}, u32[]{:S(2)}) copy-start(bf16[4,256,1024]{2,1,0:T(8,128)(2,1)} %get-tuple-element.67) | copy-start | bytes 6291460
  124.3 113.7 %collective-permute-start.2 = (bf16[256,1024]{1,0:T(8,128)(2,1)}, bf16[256,1024]{1,0:T(8,128)(2,1)S(1)}, u32[]{:S(2)}, u32[]{:S(2)}) collective-permute-start(bf16[256,1024]{1,0:T(8,128)(2,1)} %get-tuple-element.73), channel_id=1, source_target_pairs={{0,24},{8,0},{16,8},{24,16},{32,56},{40,32},{48,40},{56,48},{64,88... | collective-permute-start | bytes 1572872 | tf_op jit(solution)/shard_map/ppermute | solution.py:723
  124.7 113.3 %collective-permute-start.1 = (bf16[256,1024]{1,0:T(8,128)(2,1)S(1)}, bf16[256,1024]{1,0:T(8,128)(2,1)S(1)}, u32[]{:S(2)}, u32[]{:S(2)}) collective-permute-start(bf16[256,1024]{1,0:T(8,128)(2,1)S(1)} %get-tuple-element.74), channel_id=1, source_target_pairs={{0,16},{8,24},{16,0},{24,8},{32,48},{40,56},{48,32},{56,40},{64,80... | collective-permute-start | bytes 1572872 | tf_op jit(solution)/shard_map/ppermute | solution.py:723
  126.9 111.2 %collective-permute-start = (bf16[256,1024]{1,0:T(8,128)(2,1)S(1)}, bf16[256,1024]{1,0:T(8,128)(2,1)S(1)}, u32[]{:S(2)}, u32[]{:S(2)}) collective-permute-start(bf16[256,1024]{1,0:T(8,128)(2,1)S(1)} %get-tuple-element.75), channel_id=1, source_target_pairs={{0,8},{8,16},{16,24},{24,0},{32,40},{40,48},{48,56},{56,32},{64,72... | collective-permute-start | bytes 1572872 | tf_op jit(solution)/shard_map/ppermute | solution.py:723
  238.0 0.8 copy-start.2
  238.0 1.0 copy-start.3
  238.0 1.1 copy-start.4
  239.2 51.0 %copy-start.6 = (bf16[256,512]{1,0:T(8,128)(2,1)S(1)}, bf16[256,512]{1,0:T(8,128)(2,1)}, u32[]{:S(2)}) copy-start(bf16[256,512]{1,0:T(8,128)(2,1)} %get-tuple-element.84) | copy-start | bytes 786436
  287.0 5.6 %copy-start.1 = (f32[3,256,512]{2,1,0:T(8,128)S(1)}, f32[3,256,512]{2,1,0:T(8,128)}, u32[]{:S(2)}) copy-start(f32[3,256,512]{2,1,0:T(8,128)} %get-tuple-element.69) | copy-start | bytes 4718596
  290.2 3.6 %copy-start.5 = (bf16[256,512]{1,0:T(8,128)(2,1)S(1)}, bf16[256,512]{1,0:T(8,128)(2,1)}, u32[]{:S(2)}) copy-start(bf16[256,512]{1,0:T(8,128)(2,1)} %get-tuple-element.89) | copy-start | bytes 786436
  290.9 3.6 %copy-start.7 = (bf16[256,512]{1,0:T(8,128)(2,1)S(1)}, bf16[256,512]{1,0:T(8,128)(2,1)}, u32[]{:S(2)}) copy-start(bf16[256,512]{1,0:T(8,128)(2,1)} %get-tuple-element.90) | copy-start | bytes 786436

commit v2 on v1

--- a/solution.py
+++ b/solution.py
@@ -117,46 +117,6 @@
     return jax.ShapeDtypeStruct(dims, kind)
 
 
-def inputs_kernel(mail, tokens, queries, keys, cot, full, th, qh, kh, ch, pieces):
-    z, a = place()
-    row, col = lax.axis_index("row"), lax.axis_index("col")
-    other = 1 - row
-    right, left = turn(col, 1, 4), turn(col, -1, 4)
-    mates = [at_ctx(z, turn(a, d, HEADS)) for d in range(1, HEADS)]
-    greet([{"row": other}, {"col": right}, {"col": left}] + mates)
-
-    def block(r, c):
-        return full.at[:, cols(r * 4 + c, WIDTH)]
-
-    def half(r, c, h):
-        return full.at[pl.ds(h * (ROWS // 2), ROWS // 2), cols(r * 4 + c, WIDTH)]
-
-    up = mail.push(tokens, block(row, col), {"row": other})
-    fr = mail.push(tokens, block(row, col), {"col": right})
-    fl = mail.push(tokens, block(row, col), {"col": left})
-    mail.keep(tokens, block(row, col))
-    for src, dst in ((tokens, th), (queries, qh), (keys, kh), (cot, ch)):
-        for d in range(1, HEADS):
-            to = turn(a, d, HEADS)
-            mail.push(src.at[:, cols(to)], dst.at[rows(a, ROWS)], at_ctx(z, to))
-        mail.keep(src.at[:, cols(a)], dst.at[rows(a, ROWS)])
-    mail.arrive(up)
-    gr = mail.push(block(other, col), block(other, col), {"col": right})
-    gl = mail.push(block(other, col), block(other, col), {"col": left})
-    for r, from_left, from_right in ((row, fr, fl), (other, gr, gl)):
-        mail.arrive(from_left)
-        mail.push(half(r, left, 0), half(r, left, 0), {"col": right})
-        mail.arrive(from_right)
-        mail.push(half(r, right, 1), half(r, right, 1), {"col": left})
-    mail.finish()
-    for d in range(HEADS):
-        for s in range(SLABS):
-            mail.keep(
-                full.at[:, cols(s * HEADS + turn(a, d, HEADS), ROWS)], pieces.at[d, :, pl.ds(s * ROWS, ROWS)]
-            )
-    mail.settle()
-
-
 def slab_gather(mail, part, whole, z, a):
     up, down = turn(z, 1, SLABS), turn(z, -1, SLABS)
     mine = whole.at[rows(z, SLAB)]
@@ -175,19 +135,77 @@
     mail.push(upper, upper, at_ctx(down, a))
 
 
-def features_kernel(mail, feats, cot, kh, fx, chalo, kfull):
+def front_kernel(
+    tokens, queries, keys, cot, weights,
+    th, qh, ch, chalo, fx, kfull, pieces,
+    full, w, acc, feats, kh, send, recv, loc,
+):
+    mail = Courier(send, recv, loc)
     z, a = place()
+    row, col = lax.axis_index("row"), lax.axis_index("col")
+    other = 1 - row
+    right, left, across = turn(col, 1, 4), turn(col, -1, 4), turn(col, 2, 4)
     up, down = turn(z, 1, SLABS), turn(z, -1, SLABS)
-    peers = [at_ctx(z, turn(a, d, HEADS)) for d in range(1, HEADS)]
-    peers += [at_ctx(s, b) for s in (up, down) for b in range(HEADS)]
-    greet(peers)
+    for j in range(3):
+        mail.keep(weights.at[j], w.at[j])
+    greet(
+        [{"row": other}, {"col": right}, {"col": left}]
+        + [at_ctx(z, turn(a, d, HEADS)) for d in range(1, HEADS)]
+        + [at_ctx(s, b) for s in (up, down) for b in range(HEADS)]
+    )
+
+    def block(r, c):
+        return full.at[:, cols(r * 4 + c, WIDTH)]
+
+    def half(r, c, h):
+        return full.at[pl.ds(h * (ROWS // 2), ROWS // 2), cols(r * 4 + c, WIDTH)]
+
+    def project(r, c, lhs=None):
+        lhs = full[:, cols(r * 4 + c, WIDTH)] if lhs is None else lhs
+        for j in range(3):
+            acc[j] += jnp.dot(lhs, w[j, rows(r * 4 + c, WIDTH)], preferred_element_type=F32)
+
+    vertical = mail.push(tokens, block(row, col), {"row": other})
+    fr = mail.push(tokens, block(row, col), {"col": right})
+    fl = mail.push(tokens, block(row, col), {"col": left})
+    full[:, cols(row * 4 + col, WIDTH)] = tokens[...]
+    kh[rows(a, ROWS)] = keys[:, cols(a)]
+    acc[...] = jnp.zeros_like(acc)
+    mail.settle()
+    project(row, col, tokens[...])
+    mail.arrive(vertical)
+    gr = mail.push(block(other, col), block(other, col), {"col": right})
+    gl = mail.push(block(other, col), block(other, col), {"col": left})
+    key_parts = []
+    for src, dst in ((keys, kh), (tokens, th), (queries, qh), (cot, ch)):
+        for d in range(1, HEADS):
+            to = turn(a, d, HEADS)
+            k = mail.push(src.at[:, cols(to)], dst.at[rows(a, ROWS)], at_ctx(z, to))
+            if dst is kh:
+                key_parts.append(k)
+        if dst is not kh:
+            mail.keep(src.at[:, cols(a)], dst.at[rows(a, ROWS)])
+    project(other, col)
+    relays = []
+    for r, from_left, from_right in ((row, fr, fl), (other, gr, gl)):
+        mail.arrive(from_left)
+        relays.append(mail.push(half(r, left, 0), half(r, left, 0), {"col": right}))
+        mail.arrive(from_right)
+        relays.append(mail.push(half(r, right, 1), half(r, right, 1), {"col": left}))
+        project(r, left)
+        project(r, right)
+    for r, first in ((row, 0), (other, 2)):
+        mail.arrive(relays[first])
+        mail.arrive(relays[first + 1])
+        project(r, across)
+    feats[...] = acc[...].astype(BF)
+
     for d in range(1, HEADS):
         to = turn(a, d, HEADS)
         mail.push(feats.at[:, :, cols(to)], fx.at[:, rows(a, ROWS, HALO)], at_ctx(z, to))
     mail.keep(feats.at[:, :, cols(a)], fx.at[:, rows(a, ROWS, HALO)])
-    keys = slab_gather(mail, kh, kfull, z, a)
-
-    n = len(mail.remote)
+
+    n = len(mail.remote) + 4
 
     def edge(src, dst, k, b, device):
         return pltpu.make_async_remote_copy(
@@ -199,43 +217,87 @@
             device_id_type=MESH,
         )
 
-    def first(b):
+    def first_rows(b):
+        lanes = pl.ds(b * DH, DH)
         return (
-            edge(feats.at[:, pl.ds(0, HALO), pl.ds(b * DH, DH)], fx.at[:, pl.ds(HALO + SLAB, HALO)], n + 2, b, at_ctx(down, b)),
-            edge(cot.at[pl.ds(0, HALO), pl.ds(b * DH, DH)], chalo, n + 3, b, at_ctx(down, b)),
+            edge(feats.at[:, pl.ds(0, HALO), lanes], fx.at[:, pl.ds(HALO + SLAB, HALO)], n, b, at_ctx(down, b)),
+            edge(cot.at[pl.ds(0, HALO), lanes], chalo, n + 1, b, at_ctx(down, b)),
         )
 
-    def last(b):
-        return (edge(feats.at[:, pl.ds(ROWS - HALO, HALO), pl.ds(b * DH, DH)], fx.at[:, pl.ds(0, HALO)], n + 4, b, at_ctx(up, b)),)
+    def last_rows(b):
+        lanes = pl.ds(b * DH, DH)
+        return (edge(feats.at[:, pl.ds(ROWS - HALO, HALO), lanes], fx.at[:, pl.ds(0, HALO)], n + 2, b, at_ctx(up, b)),)
 
     @pl.when(a == 0)
     def _():
         for b in range(HEADS):
-            for copy in first(b):
+            for copy in first_rows(b):
                 copy.start()
 
     @pl.when(a == HEADS - 1)
     def _():
         for b in range(HEADS):
-            for copy in last(b):
+            for copy in last_rows(b):
                 copy.start()
 
-    slab_relay(mail, kfull, z, a, *keys)
+    for k in key_parts:
+        mail.arrive(k)
+    gathered = slab_gather(mail, kh, kfull, z, a)
+    for d in range(HEADS):
+        for s in range(SLABS):
+            mail.keep(
+                full.at[:, cols(s * HEADS + turn(a, d, HEADS), ROWS)], pieces.at[d, :, pl.ds(s * ROWS, ROWS)]
+            )
+    slab_relay(mail, kfull, z, a, *gathered)
     mail.finish()
-    for copy in first(0) + last(0):
+    for copy in first_rows(0) + last_rows(0):
         copy.wait_recv()
 
     @pl.when(a == 0)
     def _():
         for b in range(HEADS):
-            for copy in first(b):
+            for copy in first_rows(b):
                 copy.wait_send()
 
     @pl.when(a == HEADS - 1)
     def _():
         for b in range(HEADS):
-            for copy in last(b):
+            for copy in last_rows(b):
                 copy.wait_send()
+
+
+def front(tokens, queries, keys, cot, weights):
+    any_space, vmem = pl.BlockSpec(memory_space=pl.ANY), pl.BlockSpec(memory_space=pltpu.VMEM)
+    head = shape(SLAB, DH)
+    outs = [
+        head,
+        head,
+        head,
+        shape(HALO, DH),
+        shape(3, EXT, DH),
+        shape(SLABS * SLAB, DH),
+        shape(HEADS, ROWS, SLABS * ROWS),
+    ]
+    remotes = 3 + 2 + 12 + 4 + 3 + 4 + 12
+    return pl.pallas_call(
+        front_kernel,
+        out_shape=outs,
+        in_specs=[vmem] * 4 + [any_space],
+        out_specs=[any_space] * len(outs),
+        scratch_shapes=[
+            pltpu.VMEM((ROWS, 8 * WIDTH), BF),
+            pltpu.VMEM(weights.shape, BF),
+            pltpu.VMEM((3, ROWS, WIDTH), F32),
+            pltpu.VMEM((3, ROWS, WIDTH), BF),
+            pltpu.VMEM((SLAB, DH), BF),
+            pltpu.SemaphoreType.DMA((remotes,)),
+            pltpu.SemaphoreType.DMA((remotes,)),
+            pltpu.SemaphoreType.DMA((3 + 3 + 1 + 1 + HEADS * SLABS,)),
+        ],
+        compiler_params=pltpu.CompilerParams(
+            collective_id=0, has_side_effects=True, vmem_limit_bytes=56 << 20
+        ),
+    )(tokens, queries, keys, cot, weights)
 
 
 def stream_kernel(mail, part, whole):
@@ -709,14 +771,7 @@
     weights = w_feat.transpose(1, 0, 2)
     short_taps = short_filter.transpose(1, 0, 2)
     head = shape(SLAB, DH)
-    full, th, qh, kh, ch, pieces = exchange(
-        inputs_kernel, 0, [shape(ROWS, 8 * WIDTH), head, head, head, head, shape(HEADS, ROWS, SLABS * ROWS)], 21, 5 + HEADS * SLABS, tokens, queries, key_rows, cotangent
-    )
-    feats = jnp.einsum("tc,jck->jtk", full, weights, preferred_element_type=F32).astype(BF)
-    fx, chalo, kfull = exchange(
-        features_kernel, 1, [shape(3, EXT, DH), shape(HALO, DH), shape(SLABS * SLAB, DH)], 19, 2, feats, cotangent, kh
-    )
-    pieces, fx = lax.optimization_barrier((pieces, fx))
+    th, qh, ch, chalo, fx, kfull, pieces = front(tokens, queries, key_rows, cotangent, weights)
     token_parts = [pieces[0]]
     for d in range(1, HEADS):
         route = [(s * HEADS + a, s * HEADS + (a + d) % HEADS) for s in range(SLABS) for a in range(HEADS)]

time: 295 us -> 221 us (0.75)
  Pallas kernels: 269 us -> 200 us
  matrix products: 9.64 us -> 0 us
  starting transfers between devices: 4.95 us -> 8.04 us
    pallas_call x4 -> x2, Pallas kernels: 174 us -> 61 us  [exchange(): pl.pallas_call(kernel, out_shape=outs, in_specs=[pl.BlockSpec(memory_spac...]
    pallas_call x0 -> x1, Pallas kernels: none -> 44.8 us  [front(): pl.pallas_call(front_kernel, out_shape=outs, in_specs=[vmem] * 4 + [any_s...]
    dot_general x1 -> x0, matrix products: 9.64 us -> none  [local(): jnp.einsum('tc,jck->jtk', full, weights, preferred_element_type=F32)]
    ppermute x3, starting transfers between devices: 4.95 us -> 8.04 us  [local(): token_parts.append(lax.ppermute(pieces[d], 'ctx', route))]
    unnamed x21 -> x19, local copies, waits for them, and re-layouts: 6.12 us -> 6.09 us
  transfers between devices with their start and end apart: 3 -> 3, of which waited for: 0 -> 0; matrix products, arithmetic and copies ran while one was open for 0% -> 0% of each run, Pallas kernels for 37% -> 49%
where the time goes in v2:
time: 221 us
  Pallas kernels  200 us (90%)
  local copies, waits for them, and re-layouts  11.7 us (5%)
  starting transfers between devices  8.04 us (4%)
    pallas_call x2, Pallas kernels, exchange(): pl.pallas_call(kernel, out_shape=outs, in_specs=[pl.BlockSpec(memory_spac...  61 us
    pallas_call x1, Pallas kernels, finale(): pl.pallas_call(finale_kernel, out_shape=[shape(ROWS, WIDTH), shape(3, ROW...  47.3 us
    pallas_call x3, Pallas kernels, compute(): pl.pallas_call(body, out_shape=outs, in_specs=[pl.BlockSpec(memory_space=...  47 us
    pallas_call x1, Pallas kernels, front(): pl.pallas_call(front_kernel, out_shape=outs, in_specs=[vmem] * 4 + [any_s...  44.8 us
    ppermute x3, starting transfers between devices, local(): token_parts.append(lax.ppermute(pieces[d], 'ctx', route))  8.04 us
    unnamed x19, local copies, waits for them, and re-layouts  6.09 us
  transfers between devices with their start and end apart: 3, of which 0 were waited for; matrix products, arithmetic and copies ran while one was open for 0% of the time, Pallas kernels for 49%

profile of v2, /device:TPU:1, one launch (start us, length us, event | category | flops | bytes accessed | tf_op | source)
XLA Modules:
  0.0 221.1 jit_solution(17416570216531010002)
XLA Ops:
  0.6 44.8 %shard_map.126 = (bf16[1024,128]{1,0:T(8,128)(2,1)}, bf16[1024,128]{1,0:T(8,128)(2,1)}, bf16[1024,128]{1,0:T(8,128)(2,1)}, bf16[144,128]{1,0:T(8,128)(2,1)}, bf1...) custom-call(bf16[256,512]{1,0:T(8,128)(2,1)} %tokens.1, ...), custom_call_target="tpu_custom_call" | custom-call | tf_op jit(solution)/shard_map/pallas_call | solution.py:282
  45.4 2.5 %slice_bitcast_fusion = (bf16[256,1024]{1,0:T(8,128)(2,1)S(1)}, bf16[256,1024]{1,0:T(8,128)(2,1)S(1)}, bf16[256,1024]{1,0:T(8,128)(2,1)S(1)}, bf16[256,1024]{1,0:T(8,128)(2,1)}) fusion(bf16[4,256,1024]{2,1,0:T(8,128)(2,1)} %get-tuple-element.59), kind=kLoop, calls=%fused_computation | loop fusion | bytes 4194304 | tf_op jit(solution)/shard_map/squeeze | solution.py:778
  47.9 3.0 %collective-permute-start.2 = (bf16[256,1024]{1,0:T(8,128)(2,1)S(1)}, bf16[256,1024]{1,0:T(8,128)(2,1)S(1)}, u32[]{:S(2)}, u32[]{:S(2)}) collective-permute-start(bf16[256,1024]{1,0:T(8,128)(2,1)S(1)} %get-tuple-element.65), channel_id=1, source_target_pairs={{0,24},{8,0},{16,8},{24,16},{32,56},{40,32},{48,40},{56,48},{64,88... | collective-permute-start | bytes 1572872 | tf_op jit(solution)/shard_map/ppermute | solution.py:778
  50.9 1.9 collective-permute-start.1
  52.8 3.1 %collective-permute-start = (bf16[256,1024]{1,0:T(8,128)(2,1)S(1)}, bf16[256,1024]{1,0:T(8,128)(2,1)S(1)}, u32[]{:S(2)}, u32[]{:S(2)}) collective-permute-start(bf16[256,1024]{1,0:T(8,128)(2,1)S(1)} %get-tuple-element.67), channel_id=1, source_target_pairs={{0,8},{8,16},{16,24},{24,0},{32,40},{40,48},{48,56},{56,32},{64,72... | collective-permute-start | bytes 1572872 | tf_op jit(solution)/shard_map/ppermute | solution.py:778
  55.9 0.6 pad_add_fusion.where
  56.5 13.3 %shard_map.127 = (bf16[1024,128]{1,0:T(8,128)(2,1)}, f32[1168,128]{1,0:T(8,128)}, f32[1040,128]{1,0:T(8,128)}, f32[1040,128]{1,0:T(8,128)}, f32[1040,128]{1,0:T(8,128)}, /*index=5*/f32[1184,128]{1,0:T(8,128)}) custom-call(s32[2]{0:T(128)} %pad_add_fusion.where, bf16[3,1312,128]{2,1,0:T(8,128)(2,1)} %get-tuple-element.38.fx, f32[3,7,512]{2,1,0:T(8,128)} %bitcast.20, ...), custom_call_target="tpu_custom_call" | custom-call | tf_op jit(solution)/shard_map/pallas_call | solution.py:531
  69.8 13.4 %shard_map.128.v = bf16[4096,128]{1,0:T(8,128)(2,1)} custom-call(bf16[1024,128]{1,0:T(8,128)(2,1)} %get-tuple-element.40.refs_0_.own_stream), custom_call_target="tpu_custom_call" | custom-call | tf_op jit(solution)/shard_map/pallas_call | solution.py:102
  83.2 9.0 %shard_map.129 = (bf16[1024,128]{1,0:T(8,128)(2,1)}, bf16[1024,128]{1,0:T(8,128)(2,1)}, bf16[4096,128]{1,0:T(8,128)(2,1)}, bf16[4240,128]{1,0:T(8,128)(2,1)}) custom-call(s32[2]{0:T(128)} %pad_add_fusion.where, bf16[1024,128]{1,0:T(8,128)(2,1)} %get-tuple-element.36.q, bf16[4096,128]{1,0:T(8,128)(2,1)} %get-tuple-element.37.k, ...), custom_call_target="tpu_custom_call" | custom-call | tf_op jit(solution)/shard_map/pallas_call | solution.py:531
  92.2 47.7 %shard_map.130 = (bf16[4,1168,128]{2,1,0:T(8,128)(2,1)}, bf16[4,1024,128]{2,1,0:T(8,128)(2,1)}, bf16[256,512]{1,0:T(8,128)(2,1)}, bf16[256,512]{1,0:T(8,128)(2,1)}) custom-call(bf16[4240,128]{1,0:T(8,128)(2,1)} %get-tuple-element.42.refs_0_, bf16[4096,128]{1,0:T(8,128)(2,1)} %get-tuple-element.43.refs_1_, bf16[1024,128]{1,0:T(8,128)(2,1)} %get-tuple-element.44.refs_2_, ...), custom_call_target="tpu_custom_call" | custom-call | tf_op jit(solution)/shard_map/pallas_call | solution.py:102
  139.9 24.7 %shard_map.131 = (bf16[1024,128]{1,0:T(8,128)(2,1)}, bf16[3,1024,128]{2,1,0:T(8,128)(2,1)}, bf16[1024,128]{1,0:T(8,128)(2,1)}, bf16[176,128]{1,0:T(8,128)(2,1)}) custom-call(s32[2]{0:T(128)} %pad_add_fusion.where, bf16[4,1168,128]{2,1,0:T(8,128)(2,1)} %get-tuple-element.47.dvr, bf16[4,1024,128]{2,1,0:T(8,128)(2,1)} %get-tuple-element.48.dkr, ...), custom_call_target="tpu_custom_call" | custom-call | tf_op jit(solution)/shard_map/pallas_call | solution.py:531
  164.5 0.0 collective-permute-done.2.part3
  164.6 0.8 copy-done.1
  165.3 0.2 copy-done.2
  165.5 0.2 copy-done.3
  165.7 47.3 %shard_map.132 = (bf16[256,512]{1,0:T(8,128)(2,1)}, f32[3,256,512]{2,1,0:T(8,128)}, bf16[256,512]{1,0:T(8,128)(2,1)}, bf16[176,512]{1,0:T(8,128)(2,1)}) custom-call(bf16[3,1024,128]{2,1,0:T(8,128)(2,1)} %get-tuple-element.55.fg, bf16[1024,128]{1,0:T(8,128)(2,1)} %get-tuple-element.56.sg, bf16[1024,128]{1,0:T(8,128)(2,1)} %get-tuple-element.57.dk, ...), custom_call_target="tpu_custom_call" | custom-call | tf_op jit(solution)/shard_map/pallas_call | solution.py:492
  213.0 0.9 slice.28
  213.9 1.6 slice.30
  215.6 0.6 slice_bitcast_fusion.4
  216.2 0.7 copy.19
  216.9 1.7 copy.20
  218.6 1.1 copy.21
  219.7 0.7 copy.22
  220.4 0.7 copy.23
  (13 shorter events, 0.0 us)
Async XLA Ops:
  47.9 116.6 %collective-permute-start.2 = (bf16[256,1024]{1,0:T(8,128)(2,1)S(1)}, bf16[256,1024]{1,0:T(8,128)(2,1)S(1)}, u32[]{:S(2)}, u32[]{:S(2)}) collective-permute-start(bf16[256,1024]{1,0:T(8,128)(2,1)S(1)} %get-tuple-element.65), channel_id=1, source_target_pairs={{0,24},{8,0},{16,8},{24,16},{32,56},{40,32},{48,40},{56,48},{64,88... | collective-permute-start | bytes 1572872 | tf_op jit(solution)/shard_map/ppermute | solution.py:778
  50.9 113.7 %collective-permute-start.1 = (bf16[256,1024]{1,0:T(8,128)(2,1)S(1)}, bf16[256,1024]{1,0:T(8,128)(2,1)S(1)}, u32[]{:S(2)}, u32[]{:S(2)}) collective-permute-start(bf16[256,1024]{1,0:T(8,128)(2,1)S(1)} %get-tuple-element.66), channel_id=1, source_target_pairs={{0,16},{8,24},{16,0},{24,8},{32,48},{40,56},{48,32},{56,40},{64,80... | collective-permute-start | bytes 1572872 | tf_op jit(solution)/shard_map/ppermute | solution.py:778
  52.8 111.7 %collective-permute-start = (bf16[256,1024]{1,0:T(8,128)(2,1)S(1)}, bf16[256,1024]{1,0:T(8,128)(2,1)S(1)}, u32[]{:S(2)}, u32[]{:S(2)}) collective-permute-start(bf16[256,1024]{1,0:T(8,128)(2,1)S(1)} %get-tuple-element.67), channel_id=1, source_target_pairs={{0,8},{8,16},{16,24},{24,0},{32,40},{40,48},{48,56},{56,32},{64,72... | collective-permute-start | bytes 1572872 | tf_op jit(solution)/shard_map/ppermute | solution.py:778
  164.5 0.8 copy-start.1
  164.6 1.0 copy-start.2
  164.6 1.2 copy-start.3
  165.7 50.5 %copy-start.5 = (bf16[256,512]{1,0:T(8,128)(2,1)S(1)}, bf16[256,512]{1,0:T(8,128)(2,1)}, u32[]{:S(2)}) copy-start(bf16[256,512]{1,0:T(8,128)(2,1)} %get-tuple-element.76) | copy-start | bytes 786436
  213.0 5.6 %copy-start = (f32[3,256,512]{2,1,0:T(8,128)S(1)}, f32[3,256,512]{2,1,0:T(8,128)}, u32[]{:S(2)}) copy-start(f32[3,256,512]{2,1,0:T(8,128)} %get-tuple-element.61) | copy-start | bytes 4718596
  218.6 1.1 copy-start.4
  218.6 1.9 copy-start.6

commit v3 on v2

--- a/solution.py
+++ b/solution.py
@@ -93,24 +93,6 @@
         for copy in self.here[self.settled :]:
             copy.wait()
         self.settled = len(self.here)
-
-
-def exchange(body, collective_id, outs, remotes, locals_, *ins):
-    def kernel(*refs):
-        body(Courier(*refs[-3:]), *refs[:-3])
-
-    return pl.pallas_call(
-        kernel,
-        out_shape=outs,
-        in_specs=[pl.BlockSpec(memory_space=pl.ANY)] * len(ins),
-        out_specs=[pl.BlockSpec(memory_space=pl.ANY)] * len(outs),
-        scratch_shapes=[
-            pltpu.SemaphoreType.DMA((remotes,)),
-            pltpu.SemaphoreType.DMA((remotes,)),
-            pltpu.SemaphoreType.DMA((locals_,)),
-        ],
-        compiler_params=pltpu.CompilerParams(collective_id=collective_id, has_side_effects=True),
-    )(*ins)
 
 
 def shape(*dims, kind=BF):
@@ -300,13 +282,6 @@
     )(tokens, queries, keys, cot, weights)
 
 
-def stream_kernel(mail, part, whole):
-    z, a = place()
-    greet([at_ctx(turn(z, 1, SLABS), a), at_ctx(turn(z, -1, SLABS), a)])
-    slab_relay(mail, whole, z, a, *slab_gather(mail, part, whole, z, a))
-    mail.finish()
-
-
 def around(z, a):
     return [at_ctx(turn(z, d, SLABS), a) for d in range(1, SLABS)] + [
         at_ctx(z, turn(a, d, HEADS)) for d in range(1, HEADS)
@@ -320,20 +295,236 @@
     mail.keep(src.at[rows(a, ROWS)], dst.at[:, cols(a)])
 
 
-def values_kernel(mail, dv, dk, block, dq, dvr, dkr, block_home, dq_home):
+CHUNK = 512
+
+
+def dot(x, y):
+    return jnp.dot(x, y, preferred_element_type=F32)
+
+
+def dot_t(x, y):
+    return lax.dot_general(x, y, (((1,), (1,)), ((), ())), preferred_element_type=F32)
+
+
+def attention_kernel(
+    q, k, stream, ct,
+    block_home, dq_home, dv, dk,
+    v, kt, vt, st, pt, tops, outs, ctt, cs, delta, block, dq, dqt, dva, dka, edge, dv_out, dk_out, dv_in, dk_in,
+    dv_send, dv_recv, dk_send, dk_recv, send, recv, loc,
+):
+    mail = Courier(send, recv, loc)
     z, a = place()
+    scale = DH ** -0.5
+    gain = scale * 1.4426950408889634
     greet(around(z, a))
-    for d in range(1, SLABS):
-        to = turn(z, d, SLABS)
-        mail.push(dv.at[pl.ds(pl.multiple_of(to * SLAB, 16), SLAB + HALO)], dvr.at[z], at_ctx(to, a))
-    mail.keep(dv.at[pl.ds(pl.multiple_of(z * SLAB, 16), SLAB + HALO)], dvr.at[z])
-    for d in range(1, SLABS):
-        to = turn(z, d, SLABS)
-        mail.push(dk.at[rows(to, SLAB)], dkr.at[z], at_ctx(to, a))
-    mail.keep(dk.at[rows(z, SLAB)], dkr.at[z])
+    mine = rows(z, SLAB)
+    up, down = at_ctx(turn(z, 1, SLABS), a), at_ctx(turn(z, -1, SLABS), a)
+    from_down = mail.push(stream, v.at[mine], up)
+    from_up = mail.push(stream, v.at[mine], down)
+    v[mine] = stream[...]
+
+    def lanes_of(i):
+        return pl.ds(i * ROWS, ROWS)
+
+    def slots(c):
+        return pl.ds(pl.multiple_of(SLAB + c * CHUNK, CHUNK), CHUNK)
+
+    def keys_of(c):
+        return pl.ds(pl.multiple_of(c * CHUNK, CHUNK), CHUNK)
+
+    def turn_keys(s, carry):
+        kt[:, cols(s, SLAB)] = k[rows(s, SLAB)].T
+        return carry
+
+    lax.fori_loop(0, z + 1, turn_keys, 0)
+    after = lax.broadcasted_iota(jnp.int32, (ROWS, ROWS), 0) > lax.broadcasted_iota(jnp.int32, (ROWS, ROWS), 1)
+    for i in range(HEADS):
+        span = ROWS * (i + 1)
+        scores = dot_t(k[pl.ds(pl.multiple_of(z * SLAB, SLAB), span)], q[lanes_of(i)])
+        corner = jnp.where(after, -1e30, scores[span - ROWS :])
+        top = jnp.max(corner, axis=0, keepdims=True)
+        if i:
+            top = jnp.maximum(top, jnp.max(scores[: span - ROWS], axis=0, keepdims=True))
+            st[pl.ds(0, span - ROWS), lanes_of(i)] = scores[: span - ROWS]
+        st[pl.ds(span - ROWS, ROWS), lanes_of(i)] = corner
+        tops[:, lanes_of(i)] = top
+
+    def score_step(c, top):
+        past = dot_t(k[keys_of(c)], q[...])
+        st[slots(c)] = past
+        return jnp.maximum(top, jnp.max(past, axis=0, keepdims=True))
+
+    half = SLAB // 2
+    mail.arrive(from_down)
+    lower = v.at[pl.ds(pl.multiple_of(turn(z, -1, SLABS) * SLAB, SLAB), half)]
+    mail.push(lower, lower, up)
+    mail.arrive(from_up)
+    upper = v.at[pl.ds(pl.multiple_of(turn(z, 1, SLABS) * SLAB + half, half), half)]
+    mail.push(upper, upper, down)
+
+    top = lax.fori_loop(0, z * (SLAB // CHUNK), score_step, tops[...]) * gain
+    mail.arrive(2)
+    mail.arrive(3)
+
+    def turn_values(s, carry):
+        vt[:, cols(s, SLAB)] = v[rows(s, SLAB)].T
+        return carry
+
+    lax.fori_loop(0, z + 1, turn_values, 0)
+
+    for i in range(HEADS):
+        span = ROWS * (i + 1)
+        p = jnp.exp2(st[pl.ds(0, span), lanes_of(i)] * gain - top[:, i * ROWS : (i + 1) * ROWS])
+        tops[:, lanes_of(i)] = jnp.sum(p, axis=0, keepdims=True)
+        p = p.astype(BF)
+        pt[pl.ds(0, span), lanes_of(i)] = p
+        outs[:, lanes_of(i)] = dot(vt[:, pl.ds(pl.multiple_of(z * SLAB, SLAB), span)], p)
+
+    def weigh_step(c, total):
+        p = jnp.exp2(st[slots(c)] * gain - top)
+        total += jnp.sum(p, axis=0, keepdims=True)
+        p = p.astype(BF)
+        pt[slots(c)] = p
+        outs[...] += dot(vt[:, keys_of(c)], p)
+        return total
+
+    inverse = 1.0 / lax.fori_loop(0, z * (SLAB // CHUNK), weigh_step, tops[...])
+    out = outs[...] * inverse
+    block[...] = (stream[...].astype(F32) + out.T).astype(BF)
+    ctt[...] = (ct[...].astype(F32).T * inverse).astype(BF)
+    cs[...] = ctt[...].T
+    delta[...] = jnp.sum(ctt[...].astype(F32) * out, axis=0, keepdims=True)
     home(mail, block, block_home, z, a)
+
+    for i in reversed(range(HEADS)):
+        span = ROWS * (i + 1)
+        here = pl.ds(pl.multiple_of(z * SLAB, SLAB), span)
+        p = pt[pl.ds(0, span), lanes_of(i)]
+        value_part = dot(p, cs[lanes_of(i)])
+        dp = dot(v[here], ctt[:, lanes_of(i)])
+        ds = (p.astype(F32) * (dp - delta[:, lanes_of(i)])).astype(BF)
+        key_part = dot(ds, q[lanes_of(i)])
+        dqt[:, lanes_of(i)] = dot(kt[:, here], ds)
+        if i == HEADS - 1:
+            dva[...] = value_part
+            dka[...] = key_part
+        else:
+            dva[pl.ds(0, span)] += value_part
+            dka[pl.ds(0, span)] += key_part
+    edge[...] = dva[pl.ds(0, HALO)].astype(BF)
+
+    def parcels(d, to):
+        return (
+            pltpu.make_async_remote_copy(
+                src_ref=dv_out.at[d - 1],
+                dst_ref=dv_in.at[d - 1],
+                send_sem=dv_send.at[d - 1],
+                recv_sem=dv_recv.at[d - 1],
+                device_id=at_ctx(to, a),
+                device_id_type=MESH,
+            ),
+            pltpu.make_async_remote_copy(
+                src_ref=dk_out.at[d - 1],
+                dst_ref=dk_in.at[d - 1],
+                send_sem=dk_send.at[d - 1],
+                recv_sem=dk_recv.at[d - 1],
+                device_id=at_ctx(to, a),
+                device_id_type=MESH,
+            ),
+        )
+
+    def grad_step(d, carry):
+        s = z - d
+        dv_out[d - 1, pl.ds(SLAB, HALO)] = edge[...]
+        for n in range(SLAB // CHUNK):
+            c = s * (SLAB // CHUNK) + n
+            p = pt[slots(c)]
+            value_part = dot(p, cs[...]).astype(BF)
+            dv_out[d - 1, pl.ds(n * CHUNK, CHUNK)] = value_part
+            if n == 0:
+                edge[...] = value_part[:HALO]
+            dp = dot(v[keys_of(c)], ctt[...])
+            ds = (p.astype(F32) * (dp - delta[...])).astype(BF)
+            dk_out[d - 1, pl.ds(n * CHUNK, CHUNK)] = (dot(ds, q[...]) * scale).astype(BF)
+            dqt[...] += dot(kt[:, keys_of(c)], ds)
+        for copy in parcels(d, s):
+            copy.start()
+        return carry
+
+    lax.fori_loop(1, z + 1, grad_step, 0)
+    dq[...] = (dqt[...].T * scale).astype(BF)
     home(mail, dq, dq_home, z, a)
+
+    dv[pl.ds(0, SLAB)] = dva[...]
+    dv[pl.ds(SLAB, HALO)] = jnp.zeros((HALO, DH), F32)
+    dka[...] = dka[...] * scale
+
+    def value_step(d, carry):
+        parcels(d, turn(z, d, SLABS))[0].wait_recv()
+        dv[...] += dv_in[d - 1].astype(F32)
+        return carry
+
+    def key_step(d, carry):
+        parcels(d, turn(z, d, SLABS))[1].wait_recv()
+        dka[...] += dk_in[d - 1].astype(F32)
+        return carry
+
+    lax.fori_loop(1, SLABS - z, value_step, 0)
+    lax.fori_loop(1, SLABS - z, key_step, 0)
+    dk[...] = dka[...].astype(BF)
     mail.finish()
+
+    def sent_step(d, carry):
+        for copy in parcels(d, turn(z, -d, SLABS)):
+            copy.wait_send()
+        return carry
+
+    lax.fori_loop(1, z + 1, sent_step, 0)
+
+
+def attention(q, k, stream, ct):
+    any_space, vmem = pl.BlockSpec(memory_space=pl.ANY), pl.BlockSpec(memory_space=pltpu.VMEM)
+    whole = SLABS * SLAB
+    mine = shape(ROWS, WIDTH)
+    dma = pltpu.SemaphoreType.DMA
+    return pl.pallas_call(
+        attention_kernel,
+        out_shape=[mine, mine, shape(SLAB + HALO, DH, kind=F32), shape(SLAB, DH)],
+        in_specs=[vmem] * 4,
+        out_specs=[any_space, any_space, vmem, vmem],
+        scratch_shapes=[
+            pltpu.VMEM((whole, DH), BF),
+            pltpu.VMEM((DH, whole), BF),
+            pltpu.VMEM((DH, whole), BF),
+            pltpu.VMEM((whole, SLAB), F32),
+            pltpu.VMEM((whole, SLAB), BF),
+            pltpu.VMEM((1, SLAB), F32),
+            pltpu.VMEM((DH, SLAB), F32),
+            pltpu.VMEM((DH, SLAB), BF),
+            pltpu.VMEM((SLAB, DH), BF),
+            pltpu.VMEM((1, SLAB), F32),
+            pltpu.VMEM((SLAB, DH), BF),
+            pltpu.VMEM((SLAB, DH), BF),
+            pltpu.VMEM((DH, SLAB), F32),
+            pltpu.VMEM((SLAB, DH), F32),
+            pltpu.VMEM((SLAB, DH), F32),
+            pltpu.VMEM((HALO, DH), BF),
+            pltpu.VMEM((SLABS - 1, SLAB + HALO, DH), BF),
+            pltpu.VMEM((SLABS - 1, SLAB, DH), BF),
+            pltpu.VMEM((SLABS - 1, SLAB + HALO, DH), BF),
+            pltpu.VMEM((SLABS - 1, SLAB, DH), BF),
+            dma((SLABS - 1,)),
+            dma((SLABS - 1,)),
+            dma((SLABS - 1,)),
+            dma((SLABS - 1,)),
+            dma((10,)),
+            dma((10,)),
+            dma((2,)),
+        ],
+        compiler_params=pltpu.CompilerParams(
+            collective_id=2, has_side_effects=True, vmem_limit_bytes=58 << 20
+        ),
+    )(q, k, stream, ct)
 
 
 def finale_kernel(
@@ -609,103 +800,17 @@
     stream[...] = (tok[...].astype(F32) + qm[own] * lm[own]).astype(BF)
 
 
-def attention_body(where, q, k, v, ct, own_stream, block, dq, dk, dv, st, pt, kt, vt, dka, dva):
-    z = where[0]
-    scale = DH ** -0.5
-    gain = scale * 1.4426950408889634
-    dka[...] = jnp.zeros_like(dka)
-    dva[...] = jnp.zeros_like(dva)
-    kt[...] = k[...].T
-    vt[...] = v[...].T
-
-    def dot(x, y):
-        return jnp.dot(x, y, preferred_element_type=F32)
-
-    def dot_t(x, y):
-        return lax.dot_general(x, y, (((1,), (1,)), ((), ())), preferred_element_type=F32)
-
-    for i in range(HEADS):
-        span = ROWS * (i + 1)
-        here = pl.ds(i * ROWS, ROWS)
-        qb, cb = q[here], ct[here]
-        own = pl.ds(pl.multiple_of(z * SLAB, SLAB), span)
-        own_lanes = pl.ds(pl.multiple_of(z * SLAB, SLAB), span)
-        scores = dot_t(k[own], qb)
-        after = lax.broadcasted_iota(jnp.int32, (ROWS, ROWS), 0) > lax.broadcasted_iota(jnp.int32, (ROWS, ROWS), 1)
-        corner = jnp.where(after, -1e30, scores[span - ROWS :])
-        top = jnp.max(corner, axis=0, keepdims=True)
-        if i:
-            top = jnp.maximum(top, jnp.max(scores[: span - ROWS], axis=0, keepdims=True))
-            st[pl.ds(0, span - ROWS)] = scores[: span - ROWS]
-        st[pl.ds(span - ROWS, ROWS)] = corner
-
-        def score_step(s, top):
-            past = dot_t(k[pl.ds(pl.multiple_of(s * SLAB, SLAB), SLAB)], qb)
-            st[pl.ds(pl.multiple_of((s + 1) * SLAB, SLAB), SLAB)] = past
-            return jnp.maximum(top, jnp.max(past, axis=0, keepdims=True))
-
-        top = lax.fori_loop(0, z, score_step, top) * gain
-
-        def weigh(slots, lanes, total, out):
-            p = jnp.exp2(st[slots] * gain - top)
-            total += jnp.sum(p, axis=0, keepdims=True)
-            p = p.astype(BF)
-            pt[slots] = p
-            return total, out + dot(vt[:, lanes], p)
-
-        carry = weigh(pl.ds(0, span), own_lanes, jnp.zeros((1, ROWS), F32), jnp.zeros((DH, ROWS), F32))
-
-        def weigh_step(s, carry):
-            return weigh(
-                pl.ds(pl.multiple_of((s + 1) * SLAB, SLAB), SLAB), pl.ds(pl.multiple_of(s * SLAB, SLAB), SLAB), *carry
-            )
-
-        total, out = lax.fori_loop(0, z, weigh_step, carry)
-        inverse = 1.0 / total
-        out = out * inverse
-        block[here] = (own_stream[here].astype(F32) + out.T).astype(BF)
-        ctt = (cb.astype(F32).T * inverse).astype(BF)
-        delta = jnp.sum(ctt.astype(F32) * out, axis=0, keepdims=True)
-        cs = ctt.T
-
-        def grads(slots, lanes, dqt):
-            p = pt[slots]
-            dva[lanes] += dot(p, cs)
-            dp = dot(v[lanes], ctt)
-            ds = (p.astype(F32) * (dp - delta)).astype(BF)
-            dka[lanes] += dot(ds, qb)
-            return dqt + dot(kt[:, lanes], ds)
-
-        dqt = grads(pl.ds(0, span), own, jnp.zeros((DH, ROWS), F32))
-
-        def grad_step(s, dqt):
-            return grads(
-                pl.ds(pl.multiple_of((s + 1) * SLAB, SLAB), SLAB), pl.ds(pl.multiple_of(s * SLAB, SLAB), SLAB), dqt
-            )
-
-        dqt = lax.fori_loop(0, z, grad_step, dqt)
-        dq[here] = (dqt.T * scale).astype(BF)
-    dk[...] = (dka[...] * scale).astype(BF)
-    whole = SLABS * SLAB
-    dv[pl.ds(0, whole)] = dva[...].astype(BF)
-    dv[pl.ds(whole, HALO)] = jnp.zeros((HALO, DH), BF)
-
-
-def back_body(where, dvr, dkr, ch, chalo, fx, short, mr, qm, km, vm, lm, pr, sg, fg, dk, small, mg, stack, feat, spread):
+def back_body(where, dv, ch, chalo, fx, short, mr, qm, km, vm, lm, pr, sg, fg, small, mg, stack, feat, spread):
     z, a = where[0], where[1]
     spread_taps(spread, mr, a)
     keep_head = (z > 0).astype(F32)
     keep_tail = (z < SLABS - 1).astype(F32)
     own, halo = pl.ds(0, SLAB), pl.ds(SLAB, HALO)
 
-    def value_sum(part):
-        return sum(dvr[s, part].astype(F32) for s in range(SLABS))
-
-    dk[...] = sum(dkr[s].astype(F32) for s in range(SLABS)).astype(BF)
-    grad = (ch[...].astype(F32) + value_sum(own)).astype(BF)
+    grad = (ch[...].astype(F32) + dv[own]).astype(BF)
     sg[...] = grad
     mg[own] = (grad.astype(F32) * qm[own]).astype(BF).astype(F32)
-    grad_halo = (chalo[...].astype(F32) + value_sum(halo)).astype(BF).astype(F32) * keep_tail
+    grad_halo = (chalo[...].astype(F32) + dv[halo]).astype(BF).astype(F32) * keep_tail
     mg[halo] = (grad_halo * qm[halo]).astype(BF).astype(F32)
     stack[0, own] = grad.astype(F32) * lm[own]
     stack[0, pl.ds(SLAB, TAIL)] = grad_halo[:TAIL] * lm[pl.ds(SLAB, TAIL)]
@@ -793,48 +898,17 @@
         mr_filter,
         th,
     )
-    (vfull,) = exchange(stream_kernel, 2, [shape(SLABS * SLAB, DH)], 4, 1, stream)
-    whole = SLABS * SLAB
-    block, dq, dk, dv = compute(
-        attention_body,
-        [head, head, shape(whole, DH), shape(whole + HALO, DH)],
-        [
-            pltpu.VMEM((whole + SLAB, ROWS), F32),
-            pltpu.VMEM((whole + SLAB, ROWS), BF),
-            pltpu.VMEM((DH, whole), BF),
-            pltpu.VMEM((DH, whole), BF),
-            pltpu.VMEM((whole, DH), F32),
-            pltpu.VMEM((whole, DH), F32),
-        ],
-        qh,
-        kfull,
-        vfull,
-        ch,
-        stream,
-    )
-    mine = shape(ROWS, WIDTH)
-    dvr, dkr, block_out, grad_queries = exchange(
-        values_kernel,
-        3,
-        [shape(SLABS, SLAB + HALO, DH), shape(SLABS, SLAB, DH), mine, mine],
-        12,
-        4,
-        dv,
-        dk,
-        block,
-        dq,
-    )
-    sg, fg, dk_sum, small = compute(
+    block_out, grad_queries, dv, dk = attention(qh, kfull, stream, ch)
+    sg, fg, small = compute(
         back_body,
-        [head, shape(3, SLAB, DH), head, shape(MRLEN + 3 * 16, DH)],
+        [head, shape(3, SLAB, DH), shape(MRLEN + 3 * 16, DH)],
         [
             pltpu.VMEM((SLAB + HALO, DH), F32),
             pltpu.VMEM((3, SLAB + TAIL, DH), F32),
             pltpu.VMEM((3, SLAB + 16, DH), F32),
         ]
         + filters,
-        dvr,
-        dkr,
+        dv,
         ch,
         chalo,
         fx,
@@ -846,7 +920,7 @@
         lm,
         pr,
     )
-    grad_input, grad_feat, grad_keys, small_home = finale(fg, sg, dk_sum, small, token_parts, weights)
+    grad_input, grad_feat, grad_keys, small_home = finale(fg, sg, dk, small, token_parts, weights)
     sums = small_home.astype(F32)
     grad_short = sums[MRLEN:].reshape(3, 16, WIDTH)[:, :SHORT].transpose(1, 0, 2)
     grad_feat = grad_feat.transpose(1, 0, 2)

time: 221 us -> 203 us (0.919)
  Pallas kernels: 200 us -> 182 us
    pallas_call x3 -> x2, Pallas kernels: 47 us -> 37.1 us  [compute(): pl.pallas_call(body, out_shape=outs, in_specs=[pl.BlockSpec(memory_space=...]
    pallas_call x2 -> x1, Pallas kernels: 61 us -> 51.3 us  [attention(): pl.pallas_call(attention_kernel, out_shape=[mine, mine, shape(SLAB + HALO...]
  transfers between devices with their start and end apart: 3 -> 3, of which waited for: 0 -> 0; matrix products, arithmetic and copies ran while one was open for 0% -> 0% of each run, Pallas kernels for 49% -> 44%
where the time goes in v3:
time: 203 us
  Pallas kernels  182 us (90%)
  local copies, waits for them, and re-layouts  11.8 us (6%)
  starting transfers between devices  8.04 us (4%)
    pallas_call x1, Pallas kernels, attention(): pl.pallas_call(attention_kernel, out_shape=[mine, mine, shape(SLAB + HALO...  51.3 us
    pallas_call x1, Pallas kernels, finale(): pl.pallas_call(finale_kernel, out_shape=[shape(ROWS, WIDTH), shape(3, ROW...  48.4 us
    pallas_call x1, Pallas kernels, front(): pl.pallas_call(front_kernel, out_shape=outs, in_specs=[vmem] * 4 + [any_s...  44.8 us
    pallas_call x2, Pallas kernels, compute(): pl.pallas_call(body, out_shape=outs, in_specs=[pl.BlockSpec(memory_space=...  37.1 us
    ppermute x3, starting transfers between devices, local(): token_parts.append(lax.ppermute(pieces[d], 'ctx', route))  8.04 us
    unnamed x19, local copies, waits for them, and re-layouts  6.11 us
  transfers between devices with their start and end apart: 3, of which 0 were waited for; matrix products, arithmetic and copies ran while one was open for 0% of the time, Pallas kernels for 44%

profile of v3, /device:TPU:1, one launch (start us, length us, event | category | flops | bytes accessed | tf_op | source)
XLA Modules:
  0.0 202.7 jit_solution(17744130266637976906)
XLA Ops:
  0.6 44.8 %shard_map.126 = (bf16[1024,128]{1,0:T(8,128)(2,1)}, bf16[1024,128]{1,0:T(8,128)(2,1)}, bf16[1024,128]{1,0:T(8,128)(2,1)}, bf16[144,128]{1,0:T(8,128)(2,1)}, bf1...) custom-call(bf16[256,512]{1,0:T(8,128)(2,1)} %tokens.1, ...), custom_call_target="tpu_custom_call" | custom-call | tf_op jit(solution)/shard_map/pallas_call | solution.py:264
  45.4 2.5 %slice_bitcast_fusion = (bf16[256,1024]{1,0:T(8,128)(2,1)S(1)}, bf16[256,1024]{1,0:T(8,128)(2,1)S(1)}, bf16[256,1024]{1,0:T(8,128)(2,1)S(1)}, bf16[256,1024]{1,0:T(8,128)(2,1)}) fusion(bf16[4,256,1024]{2,1,0:T(8,128)(2,1)} %get-tuple-element.49), kind=kLoop, calls=%fused_computation | loop fusion | bytes 4194304 | tf_op jit(solution)/shard_map/squeeze | solution.py:883
  47.9 3.0 %collective-permute-start.2 = (bf16[256,1024]{1,0:T(8,128)(2,1)S(1)}, bf16[256,1024]{1,0:T(8,128)(2,1)S(1)}, u32[]{:S(2)}, u32[]{:S(2)}) collective-permute-start(bf16[256,1024]{1,0:T(8,128)(2,1)S(1)} %get-tuple-element.55), channel_id=1, source_target_pairs={{0,24},{8,0},{16,8},{24,16},{32,56},{40,32},{48,40},{56,48},{64,88... | collective-permute-start | bytes 1572872 | tf_op jit(solution)/shard_map/ppermute | solution.py:883
  50.9 1.9 collective-permute-start.1
  52.8 3.1 %collective-permute-start = (bf16[256,1024]{1,0:T(8,128)(2,1)S(1)}, bf16[256,1024]{1,0:T(8,128)(2,1)S(1)}, u32[]{:S(2)}, u32[]{:S(2)}) collective-permute-start(bf16[256,1024]{1,0:T(8,128)(2,1)S(1)} %get-tuple-element.57), channel_id=1, source_target_pairs={{0,8},{8,16},{16,24},{24,0},{32,40},{40,48},{48,56},{56,32},{64,72... | collective-permute-start | bytes 1572872 | tf_op jit(solution)/shard_map/ppermute | solution.py:883
  55.9 0.6 pad_add_fusion.where
  56.5 13.3 %shard_map.127 = (bf16[1024,128]{1,0:T(8,128)(2,1)}, f32[1168,128]{1,0:T(8,128)}, f32[1040,128]{1,0:T(8,128)}, f32[1040,128]{1,0:T(8,128)}, f32[1040,128]{1,0:T(8,128)}, /*index=5*/f32[1184,128]{1,0:T(8,128)}) custom-call(s32[2]{0:T(128)} %pad_add_fusion.where, bf16[3,1312,128]{2,1,0:T(8,128)(2,1)} %get-tuple-element.33.fx, f32[3,7,512]{2,1,0:T(8,128)} %bitcast.20, ...), custom_call_target="tpu_custom_call" | custom-call | tf_op jit(solution)/shard_map/pallas_call | solution.py:722
  69.8 51.3 %shard_map.128 = (bf16[256,512]{1,0:T(8,128)(2,1)}, bf16[256,512]{1,0:T(8,128)(2,1)}, f32[1168,128]{1,0:T(8,128)}, bf16[1024,128]{1,0:T(8,128)(2,1)}) custom-call(bf16[1024,128]{1,0:T(8,128)(2,1)} %get-tuple-element.31.q, bf16[4096,128]{1,0:T(8,128)(2,1)} %get-tuple-element.32.k, bf16[1024,128]{1,0:T(8,128)(2,1)} %get-tuple-element.35.stream, ...), custom_call_target="tpu_custom_call" | custom-call | tf_op jit(solution)/shard_map/pallas_call | solution.py:490
  121.1 23.8 %shard_map.129 = (bf16[1024,128]{1,0:T(8,128)(2,1)}, bf16[3,1024,128]{2,1,0:T(8,128)(2,1)}, bf16[176,128]{1,0:T(8,128)(2,1)}) custom-call(s32[2]{0:T(128)} %pad_add_fusion.where, f32[1168,128]{1,0:T(8,128)} %get-tuple-element.38.dv, bf16[1024,128]{1,0:T(8,128)(2,1)} %get-tuple-element.36.ct.ch, bf16[144,128]{1,0:T(8,128)(2,1)} %get-tuple-element.39.chalo, ...), custom_call_target="tpu_custom_call" | custom-call | tf_op jit(solution)/shard_map/pallas_call | solution.py:722
  144.9 0.0 collective-permute-done.2.part3
  144.9 0.0 collective-permute-done.1.part2
  145.0 0.0 collective-permute-done.part1
  145.0 0.8 copy-done.1
  145.7 0.2 copy-done.2
  145.9 0.2 copy-done.3
  146.1 48.4 %shard_map.130 = (bf16[256,512]{1,0:T(8,128)(2,1)}, f32[3,256,512]{2,1,0:T(8,128)}, bf16[256,512]{1,0:T(8,128)(2,1)}, bf16[176,512]{1,0:T(8,128)(2,1)}) custom-call(bf16[3,1024,128]{2,1,0:T(8,128)(2,1)} %get-tuple-element.45.fg, bf16[1024,128]{1,0:T(8,128)(2,1)} %get-tuple-element.46.sg, bf16[1024,128]{1,0:T(8,128)(2,1)} %get-tuple-element.47.dk, ...), custom_call_target="tpu_custom_call" | custom-call | tf_op jit(solution)/shard_map/pallas_call | solution.py:683
  194.6 0.9 slice.28
  195.5 1.6 slice.30
  197.1 0.6 slice_bitcast_fusion.4
  197.8 0.7 copy.19
  198.5 1.7 copy.20
  200.2 1.1 copy.21
  201.3 0.7 copy.22
  202.0 0.7 copy.23
  (11 shorter events, 0.0 us)
Async XLA Ops:
  47.9 97.0 %collective-permute-start.2 = (bf16[256,1024]{1,0:T(8,128)(2,1)S(1)}, bf16[256,1024]{1,0:T(8,128)(2,1)S(1)}, u32[]{:S(2)}, u32[]{:S(2)}) collective-permute-start(bf16[256,1024]{1,0:T(8,128)(2,1)S(1)} %get-tuple-element.55), channel_id=1, source_target_pairs={{0,24},{8,0},{16,8},{24,16},{32,56},{40,32},{48,40},{56,48},{64,88... | collective-permute-start | bytes 1572872 | tf_op jit(solution)/shard_map/ppermute | solution.py:883
  50.9 94.1 %collective-permute-start.1 = (bf16[256,1024]{1,0:T(8,128)(2,1)S(1)}, bf16[256,1024]{1,0:T(8,128)(2,1)S(1)}, u32[]{:S(2)}, u32[]{:S(2)}) collective-permute-start(bf16[256,1024]{1,0:T(8,128)(2,1)S(1)} %get-tuple-element.56), channel_id=1, source_target_pairs={{0,16},{8,24},{16,0},{24,8},{32,48},{40,56},{48,32},{56,40},{64,80... | collective-permute-start | bytes 1572872 | tf_op jit(solution)/shard_map/ppermute | solution.py:883
  52.8 92.2 %collective-permute-start = (bf16[256,1024]{1,0:T(8,128)(2,1)S(1)}, bf16[256,1024]{1,0:T(8,128)(2,1)S(1)}, u32[]{:S(2)}, u32[]{:S(2)}) collective-permute-start(bf16[256,1024]{1,0:T(8,128)(2,1)S(1)} %get-tuple-element.57), channel_id=1, source_target_pairs={{0,8},{8,16},{16,24},{24,0},{32,40},{40,48},{48,56},{56,32},{64,72... | collective-permute-start | bytes 1572872 | tf_op jit(solution)/shard_map/ppermute | solution.py:883
  144.9 0.8 copy-start.1
  145.0 1.0 copy-start.2
  145.0 1.1 copy-start.3
  146.1 51.6 %copy-start.5 = (bf16[256,512]{1,0:T(8,128)(2,1)S(1)}, bf16[256,512]{1,0:T(8,128)(2,1)}, u32[]{:S(2)}) copy-start(bf16[256,512]{1,0:T(8,128)(2,1)} %get-tuple-element.66) | copy-start | bytes 786436
  194.6 5.6 %copy-start = (f32[3,256,512]{2,1,0:T(8,128)S(1)}, f32[3,256,512]{2,1,0:T(8,128)}, u32[]{:S(2)}) copy-start(f32[3,256,512]{2,1,0:T(8,128)} %get-tuple-element.51) | copy-start | bytes 4718596
  197.8 3.6 %copy-start.4 = (bf16[256,512]{1,0:T(8,128)(2,1)S(1)}, bf16[256,512]{1,0:T(8,128)(2,1)}, u32[]{:S(2)}) copy-start(bf16[256,512]{1,0:T(8,128)(2,1)} %get-tuple-element.71) | copy-start | bytes 786436
  198.5 3.6 %copy-start.6 = (bf16[256,512]{1,0:T(8,128)(2,1)S(1)}, bf16[256,512]{1,0:T(8,128)(2,1)}, u32[]{:S(2)}) copy-start(bf16[256,512]{1,0:T(8,128)(2,1)} %get-tuple-element.72) | copy-start | bytes 786436

commit v4 on v3

--- a/solution.py
+++ b/solution.py
@@ -119,7 +119,7 @@
 
 def front_kernel(
     tokens, queries, keys, cot, weights,
-    th, qh, ch, chalo, fx, kfull, pieces,
+    th, qh, ch, chalo, fx, kfull, piece0, piece1, piece2, piece3,
     full, w, acc, feats, kh, send, recv, loc,
 ):
     mail = Courier(send, recv, loc)
@@ -176,10 +176,15 @@
         relays.append(mail.push(half(r, right, 1), half(r, right, 1), {"col": left}))
         project(r, left)
         project(r, right)
+        if r is row:
+            for k in key_parts:
+                mail.arrive(k)
+            gathered = slab_gather(mail, kh, kfull, z, a)
     for r, first in ((row, 0), (other, 2)):
         mail.arrive(relays[first])
         mail.arrive(relays[first + 1])
         project(r, across)
+    slab_relay(mail, kfull, z, a, *gathered)
     feats[...] = acc[...].astype(BF)
 
     for d in range(1, HEADS):
@@ -187,7 +192,7 @@
         mail.push(feats.at[:, :, cols(to)], fx.at[:, rows(a, ROWS, HALO)], at_ctx(z, to))
     mail.keep(feats.at[:, :, cols(a)], fx.at[:, rows(a, ROWS, HALO)])
 
-    n = len(mail.remote) + 4
+    n = len(mail.remote)
 
     def edge(src, dst, k, b, device):
         return pltpu.make_async_remote_copy(
@@ -222,15 +227,9 @@
             for copy in last_rows(b):
                 copy.start()
 
-    for k in key_parts:
-        mail.arrive(k)
-    gathered = slab_gather(mail, kh, kfull, z, a)
-    for d in range(HEADS):
+    for d, piece in enumerate((piece0, piece1, piece2, piece3)):
         for s in range(SLABS):
-            mail.keep(
-                full.at[:, cols(s * HEADS + turn(a, d, HEADS), ROWS)], pieces.at[d, :, pl.ds(s * ROWS, ROWS)]
-            )
-    slab_relay(mail, kfull, z, a, *gathered)
+            mail.keep(full.at[:, cols(s * HEADS + turn(a, d, HEADS), ROWS)], piece.at[:, pl.ds(s * ROWS, ROWS)])
     mail.finish()
     for copy in first_rows(0) + last_rows(0):
         copy.wait_recv()
@@ -258,8 +257,7 @@
         shape(HALO, DH),
         shape(3, EXT, DH),
         shape(SLABS * SLAB, DH),
-        shape(HEADS, ROWS, SLABS * ROWS),
-    ]
+    ] + [shape(ROWS, SLABS * ROWS)] * HEADS
     remotes = 3 + 2 + 12 + 4 + 3 + 4 + 12
     return pl.pallas_call(
         front_kernel,
@@ -306,19 +304,183 @@
     return lax.dot_general(x, y, (((1,), (1,)), ((), ())), preferred_element_type=F32)
 
 
-def attention_kernel(
-    q, k, stream, ct,
-    block_home, dq_home, dv, dk,
-    v, kt, vt, st, pt, tops, outs, ctt, cs, delta, block, dq, dqt, dva, dka, edge, dv_out, dk_out, dv_in, dk_in,
+GROUP = 40
+TILE = 8
+TAPS = MRLEN // TILE
+SPAN = 13
+
+
+def spread_taps(spread, taps, a):
+    for i in range(MRLEN):
+        spread[i % TILE, i // TILE] = jnp.broadcast_to(taps[pl.ds(i, 1), cols(a)], (TILE, DH))
+
+
+def spread_shifts(shifts, rows_of, first, sign):
+    count = shifts.shape[1]
+    for r in range(TILE):
+        shifts[r] = rows_of[pl.ds(first + sign * r, count)]
+
+
+def long_filter(shifts, spread, backward, store):
+    def step(g, carry):
+        base = pl.multiple_of(g * (SPAN * TILE), TILE)
+
+        def shift(r, totals):
+            totals = list(totals)
+            taps = [spread[r, m] for m in range(TAPS)]
+            for t in range(SPAN + TAPS - 1):
+                tile = shifts[r, pl.ds(base + t * TILE, TILE)]
+                for n in range(SPAN):
+                    m = t - n if backward else n + TAPS - 1 - t
+                    if 0 <= m < TAPS:
+                        totals[n] += taps[m] * tile
+            return tuple(totals)
+
+        totals = lax.fori_loop(0, TILE, shift, tuple(jnp.zeros((TILE, DH), F32) for _ in range(SPAN)))
+        for n in range(SPAN):
+            store(pl.ds(base + n * TILE, TILE), totals[n])
+        return carry
+
+    lax.fori_loop(0, (SLAB + TAIL) // (SPAN * TILE), step, 0)
+
+
+def tap_grads(shifts, grads, lines):
+    count = 16
+
+    def shift(r, carry):
+        def step(g, sums):
+            sums = list(sums)
+            base = pl.multiple_of(g * (count * TILE), TILE)
+            own = [grads[pl.ds(base + n * TILE, TILE)] for n in range(count)]
+            for t in range(count + TAPS - 1):
+                tile = shifts[r, pl.ds(base + t * TILE, TILE)]
+                for n in range(count):
+                    m = n + TAPS - 1 - t
+                    if 0 <= m < TAPS:
+                        sums[m] += own[n] * tile
+            return tuple(sums)
+
+        zero = tuple(jnp.zeros((TILE, DH), F32) for _ in range(TAPS))
+        sums = lax.fori_loop(0, SLAB // (count * TILE), step, zero)
+        for m in range(TAPS):
+            lines[m, pl.ds(r, 1)] = jnp.sum(sums[m], axis=0, keepdims=True)
+        return carry
+
+    lax.fori_loop(0, TILE, shift, 0)
+
+
+def hyena(z, a, fx, short, tok, stream, qm, km, vm, lm, pr, feat, shifts, spread):
+    keep_head = (z > 0).astype(F32)
+    keep_tail = (z < SLABS - 1).astype(F32)
+    for j in range(3):
+        feat[j, pl.ds(0, HALO)] = fx[j, pl.ds(0, HALO)].astype(F32) * keep_head
+        feat[j, pl.ds(HALO, SLAB)] = fx[j, pl.ds(HALO, SLAB)].astype(F32)
+        feat[j, pl.ds(HALO + SLAB, HALO)] = fx[j, pl.ds(HALO + SLAB, HALO)].astype(F32) * keep_tail
+
+    taps = [[short[j, pl.ds(s, 1), cols(a)] for s in range(SHORT)] for j in range(3)]
+
+    def mixed(j, base, count):
+        total = taps[j][0] * feat[j, pl.ds(base, count)]
+        for s in range(1, SHORT):
+            total += taps[j][s] * feat[j, pl.ds(base - s, count)]
+        return total
+
+    pr[pl.ds(0, 16)] = jnp.zeros((16, DH), F32)
+
+    def head_step(g, carry):
+        base = pl.multiple_of(16 + g * 16, 16)
+        pr[pl.ds(base, 16)] = (mixed(1, base, 16) * mixed(2, base, 16)).astype(BF).astype(F32)
+        return carry
+
+    lax.fori_loop(0, (HALO - 16) // 16, head_step, 0)
+
+    def mix_step(g, carry):
+        base = pl.multiple_of(HALO + g * GROUP, 8)
+        here = pl.ds(pl.multiple_of(g * GROUP, 8), GROUP)
+        key, value = mixed(1, base, GROUP), mixed(2, base, GROUP)
+        km[here] = key
+        vm[here] = value
+        qm[here] = mixed(0, base, GROUP)
+        pr[pl.ds(base, GROUP)] = (key * value).astype(BF).astype(F32)
+        return carry
+
+    lax.fori_loop(0, (SLAB + TAIL) // GROUP, mix_step, 0)
+
+    def tail_step(g, carry):
+        here = pl.multiple_of(SLAB + TAIL + g * 16, 16)
+        qm[pl.ds(here, 16)] = mixed(0, here + HALO, 16)
+        return carry
+
+    lax.fori_loop(0, (HALO - TAIL) // 16, tail_step, 0)
+    spread_shifts(shifts, pr, HALO - MRLEN + TILE, -1)
+
+    def store(here, total):
+        lm[here] = total
+
+    long_filter(shifts, spread, False, store)
+    own = pl.ds(0, SLAB)
+    stream[...] = (tok[...].astype(F32) + qm[own] * lm[own]).astype(BF)
+
+
+def back(z, a, dv, ch, chalo, short, qm, km, vm, lm, feat, sg, fg, short_part, mg, stack, shifts, spread):
+    keep_tail = (z < SLABS - 1).astype(F32)
+    own, halo = pl.ds(0, SLAB), pl.ds(SLAB, HALO)
+    grad = (ch[...].astype(F32) + dv[own]).astype(BF)
+    sg[...] = grad
+    mg[own] = (grad.astype(F32) * qm[own]).astype(BF).astype(F32)
+    grad_halo = (chalo[...].astype(F32) + dv[halo]).astype(BF).astype(F32) * keep_tail
+    mg[halo] = (grad_halo * qm[halo]).astype(BF).astype(F32)
+    stack[0, own] = grad.astype(F32) * lm[own]
+    stack[0, pl.ds(SLAB, TAIL)] = grad_halo[:TAIL] * lm[pl.ds(SLAB, TAIL)]
+    spread_shifts(shifts, mg, 0, 1)
+
+    def store(here, total):
+        stack[1, here] = total * vm[here]
+        stack[2, here] = total * km[here]
+
+    long_filter(shifts, spread, True, store)
+    for j in range(3):
+        taps = [short[j, pl.ds(s, 1), cols(a)] for s in range(SHORT)]
+
+        def short_step(g, sums):
+            base = pl.multiple_of(g * 32, 32)
+            line = stack[j, pl.ds(base, 32)]
+            total = taps[0] * line
+            for s in range(1, SHORT):
+                total += taps[s] * stack[j, pl.ds(base + s, 32)]
+            fg[j, pl.ds(base, 32)] = total.astype(BF)
+            out = []
+            for s in range(SHORT):
+                term = line * feat[j, pl.ds(base + HALO - s, 32)]
+                out.append(sums[s] + (term[0:8] + term[8:16] + term[16:24] + term[24:32]))
+            return tuple(out)
+
+        sums = lax.fori_loop(0, SLAB // 32, short_step, tuple(jnp.zeros((8, DH), F32) for _ in range(SHORT)))
+        lines = [jnp.sum(t, axis=0, keepdims=True) for t in sums]
+        short_part[pl.ds(16 * j, 16)] = jnp.concatenate(lines + [jnp.zeros((16 - SHORT, DH), F32)], axis=0).astype(BF)
+
+
+def middle_kernel(
+    fx, tok, q, k, ct, chalo, short, mr,
+    block_home, dq_home, sg, fg, dk, short_part, mg, pr,
+    stream, v, kt, vt, st, pt, tops, outs, ctt, cs, delta, block, dq, dqt, dv, dka, edge, dv_out, dk_out, dv_in, dk_in,
+    qm, km, vm, lm, feat, stack, shifts, spread,
     dv_send, dv_recv, dk_send, dk_recv, send, recv, loc,
 ):
     mail = Courier(send, recv, loc)
     z, a = place()
     scale = DH ** -0.5
     gain = scale * 1.4426950408889634
-    greet(around(z, a))
     mine = rows(z, SLAB)
     up, down = at_ctx(turn(z, 1, SLABS), a), at_ctx(turn(z, -1, SLABS), a)
+    spread_taps(spread, mr, a)
+
+    def turn_keys(s, carry):
+        kt[:, cols(s, SLAB)] = k[rows(s, SLAB)].T
+        return carry
+
+    hyena(z, a, fx, short, tok, stream, qm, km, vm, lm, pr, feat, shifts, spread)
+    greet(around(z, a))
     from_down = mail.push(stream, v.at[mine], up)
     from_up = mail.push(stream, v.at[mine], down)
     v[mine] = stream[...]
@@ -332,11 +494,6 @@
     def keys_of(c):
         return pl.ds(pl.multiple_of(c * CHUNK, CHUNK), CHUNK)
 
-    def turn_keys(s, carry):
-        kt[:, cols(s, SLAB)] = k[rows(s, SLAB)].T
-        return carry
-
-    lax.fori_loop(0, z + 1, turn_keys, 0)
     after = lax.broadcasted_iota(jnp.int32, (ROWS, ROWS), 0) > lax.broadcasted_iota(jnp.int32, (ROWS, ROWS), 1)
     for i in range(HEADS):
         span = ROWS * (i + 1)
@@ -354,6 +511,8 @@
         st[slots(c)] = past
         return jnp.maximum(top, jnp.max(past, axis=0, keepdims=True))
 
+    top = lax.fori_loop(0, z * (SLAB // CHUNK), score_step, tops[...]) * gain
+
     half = SLAB // 2
     mail.arrive(from_down)
     lower = v.at[pl.ds(pl.multiple_of(turn(z, -1, SLABS) * SLAB, SLAB), half)]
@@ -362,137 +521,152 @@
     upper = v.at[pl.ds(pl.multiple_of(turn(z, 1, SLABS) * SLAB + half, half), half)]
     mail.push(upper, upper, down)
 
-    top = lax.fori_loop(0, z * (SLAB // CHUNK), score_step, tops[...]) * gain
-    mail.arrive(2)
-    mail.arrive(3)
-
-    def turn_values(s, carry):
-        vt[:, cols(s, SLAB)] = v[rows(s, SLAB)].T
-        return carry
-
-    lax.fori_loop(0, z + 1, turn_values, 0)
-
     for i in range(HEADS):
         span = ROWS * (i + 1)
         p = jnp.exp2(st[pl.ds(0, span), lanes_of(i)] * gain - top[:, i * ROWS : (i + 1) * ROWS])
         tops[:, lanes_of(i)] = jnp.sum(p, axis=0, keepdims=True)
-        p = p.astype(BF)
-        pt[pl.ds(0, span), lanes_of(i)] = p
-        outs[:, lanes_of(i)] = dot(vt[:, pl.ds(pl.multiple_of(z * SLAB, SLAB), span)], p)
+        pt[pl.ds(0, span), lanes_of(i)] = p.astype(BF)
 
     def weigh_step(c, total):
         p = jnp.exp2(st[slots(c)] * gain - top)
-        total += jnp.sum(p, axis=0, keepdims=True)
-        p = p.astype(BF)
-        pt[slots(c)] = p
-        outs[...] += dot(vt[:, keys_of(c)], p)
-        return total
+        pt[slots(c)] = p.astype(BF)
+        return total + jnp.sum(p, axis=0, keepdims=True)
 
     inverse = 1.0 / lax.fori_loop(0, z * (SLAB // CHUNK), weigh_step, tops[...])
+    lax.fori_loop(0, z + 1, turn_keys, 0)
+    mail.arrive(2)
+    mail.arrive(3)
+
+    def turn_values(s, carry):
+        vt[:, cols(s, SLAB)] = v[rows(s, SLAB)].T
+        return carry
+
+    lax.fori_loop(0, z + 1, turn_values, 0)
+    for i in range(HEADS):
+        span = ROWS * (i + 1)
+        outs[:, lanes_of(i)] = dot(vt[:, pl.ds(pl.multiple_of(z * SLAB, SLAB), span)], pt[pl.ds(0, span), lanes_of(i)])
+
+    def attend_step(c, carry):
+        outs[...] += dot(vt[:, keys_of(c)], pt[slots(c)])
+        return carry
+
+    lax.fori_loop(0, z * (SLAB // CHUNK), attend_step, 0)
     out = outs[...] * inverse
-    block[...] = (stream[...].astype(F32) + out.T).astype(BF)
     ctt[...] = (ct[...].astype(F32).T * inverse).astype(BF)
     cs[...] = ctt[...].T
     delta[...] = jnp.sum(ctt[...].astype(F32) * out, axis=0, keepdims=True)
+
+    for i in reversed(range(HEADS)):
+        span = ROWS * (i + 1)
+        part = dot(pt[pl.ds(0, span), lanes_of(i)], cs[lanes_of(i)])
+        if i == HEADS - 1:
+            dv[pl.ds(0, SLAB)] = part
+        else:
+            dv[pl.ds(0, span)] += part
+    dv[pl.ds(SLAB, HALO)] = jnp.zeros((HALO, DH), F32)
+    edge[...] = dv[pl.ds(0, HALO)].astype(BF)
+
+    def parcel(d, to, kind):
+        src, dst, sent, got = ((dv_out, dv_in, dv_send, dv_recv), (dk_out, dk_in, dk_send, dk_recv))[kind]
+        return pltpu.make_async_remote_copy(
+            src_ref=src.at[d - 1],
+            dst_ref=dst.at[d - 1],
+            send_sem=sent.at[d - 1],
+            recv_sem=got.at[d - 1],
+            device_id=at_ctx(to, a),
+            device_id_type=MESH,
+        )
+
+    def value_step(d, carry):
+        s = z - d
+        dv_out[d - 1, pl.ds(SLAB, HALO)] = edge[...]
+        for n in range(SLAB // CHUNK):
+            part = dot(pt[slots(s * (SLAB // CHUNK) + n)], cs[...]).astype(BF)
+            dv_out[d - 1, pl.ds(n * CHUNK, CHUNK)] = part
+            if n == 0:
+                edge[...] = part[:HALO]
+        parcel(d, s, 0).start()
+        return carry
+
+    lax.fori_loop(1, z + 1, value_step, 0)
+    block[...] = (stream[...].astype(F32) + out.T).astype(BF)
     home(mail, block, block_home, z, a)
 
     for i in reversed(range(HEADS)):
         span = ROWS * (i + 1)
         here = pl.ds(pl.multiple_of(z * SLAB, SLAB), span)
         p = pt[pl.ds(0, span), lanes_of(i)]
-        value_part = dot(p, cs[lanes_of(i)])
         dp = dot(v[here], ctt[:, lanes_of(i)])
         ds = (p.astype(F32) * (dp - delta[:, lanes_of(i)])).astype(BF)
-        key_part = dot(ds, q[lanes_of(i)])
+        part = dot(ds, q[lanes_of(i)])
         dqt[:, lanes_of(i)] = dot(kt[:, here], ds)
         if i == HEADS - 1:
-            dva[...] = value_part
-            dka[...] = key_part
+            dka[...] = part
         else:
-            dva[pl.ds(0, span)] += value_part
-            dka[pl.ds(0, span)] += key_part
-    edge[...] = dva[pl.ds(0, HALO)].astype(BF)
-
-    def parcels(d, to):
-        return (
-            pltpu.make_async_remote_copy(
-                src_ref=dv_out.at[d - 1],
-                dst_ref=dv_in.at[d - 1],
-                send_sem=dv_send.at[d - 1],
-                recv_sem=dv_recv.at[d - 1],
-                device_id=at_ctx(to, a),
-                device_id_type=MESH,
-            ),
-            pltpu.make_async_remote_copy(
-                src_ref=dk_out.at[d - 1],
-                dst_ref=dk_in.at[d - 1],
-                send_sem=dk_send.at[d - 1],
-                recv_sem=dk_recv.at[d - 1],
-                device_id=at_ctx(to, a),
-                device_id_type=MESH,
-            ),
-        )
-
-    def grad_step(d, carry):
+            dka[pl.ds(0, span)] += part
+
+    def key_step(d, carry):
         s = z - d
-        dv_out[d - 1, pl.ds(SLAB, HALO)] = edge[...]
         for n in range(SLAB // CHUNK):
             c = s * (SLAB // CHUNK) + n
-            p = pt[slots(c)]
-            value_part = dot(p, cs[...]).astype(BF)
-            dv_out[d - 1, pl.ds(n * CHUNK, CHUNK)] = value_part
-            if n == 0:
-                edge[...] = value_part[:HALO]
             dp = dot(v[keys_of(c)], ctt[...])
-            ds = (p.astype(F32) * (dp - delta[...])).astype(BF)
+            ds = (pt[slots(c)].astype(F32) * (dp - delta[...])).astype(BF)
             dk_out[d - 1, pl.ds(n * CHUNK, CHUNK)] = (dot(ds, q[...]) * scale).astype(BF)
             dqt[...] += dot(kt[:, keys_of(c)], ds)
-        for copy in parcels(d, s):
-            copy.start()
-        return carry
-
-    lax.fori_loop(1, z + 1, grad_step, 0)
+        parcel(d, s, 1).start()
+        return carry
+
+    lax.fori_loop(1, z + 1, key_step, 0)
     dq[...] = (dqt[...].T * scale).astype(BF)
     home(mail, dq, dq_home, z, a)
 
-    dv[pl.ds(0, SLAB)] = dva[...]
-    dv[pl.ds(SLAB, HALO)] = jnp.zeros((HALO, DH), F32)
+    def add_values(d, carry):
+        parcel(d, turn(z, d, SLABS), 0).wait_recv()
+        dv[...] += dv_in[d - 1].astype(F32)
+        return carry
+
+    lax.fori_loop(1, SLABS - z, add_values, 0)
+    back(z, a, dv, ct, chalo, short, qm, km, vm, lm, feat, sg, fg, short_part, mg, stack, shifts, spread)
     dka[...] = dka[...] * scale
 
-    def value_step(d, carry):
-        parcels(d, turn(z, d, SLABS))[0].wait_recv()
-        dv[...] += dv_in[d - 1].astype(F32)
-        return carry
-
-    def key_step(d, carry):
-        parcels(d, turn(z, d, SLABS))[1].wait_recv()
+    def add_keys(d, carry):
+        parcel(d, turn(z, d, SLABS), 1).wait_recv()
         dka[...] += dk_in[d - 1].astype(F32)
         return carry
 
-    lax.fori_loop(1, SLABS - z, value_step, 0)
-    lax.fori_loop(1, SLABS - z, key_step, 0)
+    lax.fori_loop(1, SLABS - z, add_keys, 0)
     dk[...] = dka[...].astype(BF)
     mail.finish()
 
     def sent_step(d, carry):
-        for copy in parcels(d, turn(z, -d, SLABS)):
-            copy.wait_send()
+        for kind in range(2):
+            parcel(d, turn(z, -d, SLABS), kind).wait_send()
         return carry
 
     lax.fori_loop(1, z + 1, sent_step, 0)
 
 
-def attention(q, k, stream, ct):
+def middle(fx, tok, q, k, ct, chalo, short, mr):
     any_space, vmem = pl.BlockSpec(memory_space=pl.ANY), pl.BlockSpec(memory_space=pltpu.VMEM)
     whole = SLABS * SLAB
-    mine = shape(ROWS, WIDTH)
+    mine, head = shape(ROWS, WIDTH), shape(SLAB, DH)
     dma = pltpu.SemaphoreType.DMA
     return pl.pallas_call(
-        attention_kernel,
-        out_shape=[mine, mine, shape(SLAB + HALO, DH, kind=F32), shape(SLAB, DH)],
-        in_specs=[vmem] * 4,
-        out_specs=[any_space, any_space, vmem, vmem],
+        middle_kernel,
+        out_shape=[
+            mine,
+            mine,
+            head,
+            shape(3, SLAB, DH),
+            head,
+            shape(3 * 16, DH),
+            shape(SLAB + HALO, DH, kind=F32),
+            shape(HALO + SLAB + TAIL, DH, kind=F32),
+        ],
+        in_specs=[vmem] * 8,
+        out_specs=[any_space] * 2 + [vmem] * 6,
         scratch_shapes=[
+            pltpu.VMEM((SLAB, DH), BF),
             pltpu.VMEM((whole, DH), BF),
             pltpu.VMEM((DH, whole), BF),
             pltpu.VMEM((DH, whole), BF),
@@ -506,13 +680,21 @@
             pltpu.VMEM((SLAB, DH), BF),
             pltpu.VMEM((SLAB, DH), BF),
             pltpu.VMEM((DH, SLAB), F32),
-            pltpu.VMEM((SLAB, DH), F32),
+            pltpu.VMEM((SLAB + HALO, DH), F32),
             pltpu.VMEM((SLAB, DH), F32),
             pltpu.VMEM((HALO, DH), BF),
             pltpu.VMEM((SLABS - 1, SLAB + HALO, DH), BF),
             pltpu.VMEM((SLABS - 1, SLAB, DH), BF),
             pltpu.VMEM((SLABS - 1, SLAB + HALO, DH), BF),
             pltpu.VMEM((SLABS - 1, SLAB, DH), BF),
+            pltpu.VMEM((SLAB + HALO, DH), F32),
+            pltpu.VMEM((SLAB + TAIL, DH), F32),
+            pltpu.VMEM((SLAB + TAIL, DH), F32),
+            pltpu.VMEM((SLAB + TAIL, DH), F32),
+            pltpu.VMEM((3, EXT, DH), F32),
+            pltpu.VMEM((3, SLAB + TAIL, DH), F32),
+            pltpu.VMEM((TILE, SLAB + TAIL + MRLEN - TILE, DH), F32),
+            pltpu.VMEM((TILE, TAPS, TILE, DH), F32),
             dma((SLABS - 1,)),
             dma((SLABS - 1,)),
             dma((SLABS - 1,)),
@@ -524,13 +706,13 @@
         compiler_params=pltpu.CompilerParams(
             collective_id=2, has_side_effects=True, vmem_limit_bytes=58 << 20
         ),
-    )(q, k, stream, ct)
+    )(fx, tok, q, k, ct, chalo, short, mr)
 
 
 def finale_kernel(
-    fg, sg, dk, small, part0, part1, part2, part3, weights,
+    fg, sg, dk, short_part, mg, pr, part0, part1, part2, part3, weights,
     grad_input, grad_feat, dk_home, small_home,
-    w, tq, tqt, fgall, fgm, wsend, zr1, zr2, tsend, xr1, xr2, yr, ysend, sgh, slots, total,
+    w, tq, tqt, fgall, fgm, wsend, zr1, zr2, tsend, xr1, xr2, yr, ysend, sgh, slots, small, total, shifts, lines,
     send, recv, loc,
 ):
     mail = Courier(send, recv, loc)
@@ -546,22 +728,14 @@
     mail.keep(fg, fgall.at[a])
     for d, part in enumerate((part0, part1, part2, part3)):
         mail.keep(part, tq.at[rows(turn(a, -d, HEADS), ROWS)])
-    for j in range(3):
-        mail.keep(weights.at[j], w.at[j])
+    loads = [pltpu.make_async_copy(weights.at[j], w.at[j], loc.at[8 + j]) for j in range(3)]
+    for load in loads:
+        load.start()
     greet(around(z, a) + [{"row": 1 - row}, {"col": right}, {"col": left}])
 
     near_rows, far_rows = rows(side, pair), rows(1 - side, pair)
     to_mate = mail.push(fg, fgall.at[a], at_ctx(z, mate))
     first = mail.push(fg.at[:, far_rows], fgall.at[a, :, far_rows], at_ctx(z, far))
-    second = mail.push(fg.at[:, near_rows], fgall.at[a, :, near_rows], at_ctx(z, far))
-    small_in = [mail.push(small, slots.at[d - 1], at_ctx(turn(z, d, SLABS), a)) for d in range(1, SLABS)]
-    home_sg = []
-    for d in range(1, HEADS):
-        to = turn(a, d, HEADS)
-        home_sg.append(mail.push(sg.at[rows(to, ROWS)], sgh.at[:, cols(a)], at_ctx(z, to)))
-        mail.push(dk.at[rows(to, ROWS)], dk_home.at[:, cols(a)], at_ctx(z, to))
-    mail.keep(sg.at[rows(a, ROWS)], sgh.at[:, cols(a)])
-    mail.keep(dk.at[rows(a, ROWS)], dk_home.at[:, cols(a)])
     mail.settle()
 
     for b in range(SLABS):
@@ -604,8 +778,14 @@
     ring = [weight_first(0, a)]
     mail.arrive(to_mate)
     ring.append(weight_first(1, mate))
+    spread_shifts(shifts, pr, HALO - MRLEN + TILE, -1)
+    tap_grads(shifts, mg, lines)
+    small[pl.ds(0, MRLEN)] = lines[...].reshape(MRLEN, DH).astype(BF)
+    small[pl.ds(MRLEN, short_part.shape[0])] = short_part[...]
     mail.arrive(first)
     relay = mail.push(fgall.at[far, :, near_rows], fgall.at[far, :, near_rows], at_ctx(z, mate))
+    second = mail.push(fg.at[:, near_rows], fgall.at[a, :, near_rows], at_ctx(z, far))
+    small_in = [mail.push(small, slots.at[d - 1], at_ctx(turn(z, d, SLABS), a)) for d in range(1, SLABS)]
     ring[0] = weight_second(0, ring[0])
     ring[1] = weight_second(1, ring[1])
     mail.arrive(relay)
@@ -613,6 +793,9 @@
     for j in range(3):
         for h in range(HEADS):
             fgm[j, :, pl.ds(h * DH, DH)] = fgall[h, j, rows(a, ROWS)]
+
+    for load in loads:
+        load.wait()
 
     def term_block(dc):
         for r in range(2):
@@ -636,6 +819,13 @@
     mail.arrive(from_right)
     tsend[3, :, bottom] = (tsend[3, :, bottom].astype(F32) + xr1[1].astype(F32)).astype(BF)
     from_right = mail.push(tsend.at[3], xr2.at[1], {"col": left})
+    home_sg = []
+    for d in range(1, HEADS):
+        to = turn(a, d, HEADS)
+        home_sg.append(mail.push(sg.at[rows(to, ROWS)], sgh.at[:, cols(a)], at_ctx(z, to)))
+        mail.push(dk.at[rows(to, ROWS)], dk_home.at[:, cols(a)], at_ctx(z, to))
+    mail.keep(sg.at[rows(a, ROWS)], sgh.at[:, cols(a)])
+    mail.keep(dk.at[rows(a, ROWS)], dk_home.at[:, cols(a)])
     term_block(0)
 
     mail.arrive(second)
@@ -665,6 +855,7 @@
     weight_third(1, mate, ring[1])
     for k in home_sg:
         mail.arrive(k)
+    mail.settle()
     mail.arrive(across)
     grad_input[...] = (sgh[...].astype(F32) + term_sum(row) + yr[...].astype(F32)).astype(BF)
     weight_third(2, far, ring[2])
@@ -676,8 +867,8 @@
     return small[...].astype(F32) + sum(slots[d].astype(F32) for d in range(SLABS - 1))
 
 
-def finale(fg, sg, dk, small, parts, weights):
-    lines = small.shape[0]
+def finale(fg, sg, dk, short_part, mg, pr, parts, weights):
+    lines = MRLEN + short_part.shape[0]
     any_space, vmem = pl.BlockSpec(memory_space=pl.ANY), pl.BlockSpec(memory_space=pltpu.VMEM)
     remotes = 3 + 3 + 6 + 16 + 2 + 4 + 3 + 1
     return pl.pallas_call(
@@ -688,7 +879,7 @@
             shape(ROWS, WIDTH),
             shape(lines, WIDTH),
         ],
-        in_specs=[any_space, any_space, any_space, vmem] + [any_space] * 5,
+        in_specs=[any_space] * 3 + [vmem] * 3 + [any_space] * 5,
         out_specs=[vmem, vmem, any_space, any_space],
         scratch_shapes=[
             pltpu.VMEM(weights.shape, BF),
@@ -707,6 +898,9 @@
             pltpu.VMEM((ROWS, WIDTH), BF),
             pltpu.VMEM((SLABS - 1, lines, DH), BF),
             pltpu.VMEM((lines, DH), BF),
+            pltpu.VMEM((lines, DH), BF),
+            pltpu.VMEM((TILE, SLAB + TAIL + MRLEN - TILE, DH), F32),
+            pltpu.VMEM((TAPS, TILE, DH), F32),
             pltpu.SemaphoreType.DMA((remotes,)),
             pltpu.SemaphoreType.DMA((remotes,)),
             pltpu.SemaphoreType.DMA((11,)),
@@ -714,217 +908,64 @@
         compiler_params=pltpu.CompilerParams(
             collective_id=5, has_side_effects=True, vmem_limit_bytes=56 << 20
         ),
-    )(fg, sg, dk, small, *parts, weights)
-
-
-def compute(body, outs, scratch, *ins, vmem=56 << 20):
-    z, a = place()
+    )(fg, sg, dk, short_part, mg, pr, *parts, weights)
+
+
+def deliver_kernel(block, grad_q, grad_k, grad_in, grad_feat, small, block_o, in_o, feat_o, short_o, mr_o, q_o, k_o):
+    feat_o[...] = grad_feat[...]
+
+    @pl.when(pl.program_id(0) == 0)
+    def _():
+        block_o[...] = block[...]
+        in_o[...] = grad_in[...]
+        q_o[...] = grad_q[...]
+        k_o[...] = grad_k[...]
+        mr_o[...] = small[pl.ds(0, MRLEN)].astype(F32)
+        for j in range(3):
+            short_o[j] = small[pl.ds(MRLEN + 16 * j, 16)].astype(F32)[:SHORT]
+
+
+def deliver(*ins):
+    def fixed(*dims):
+        return pl.BlockSpec(dims, lambda j: (0,) * len(dims))
+
+    mine = fixed(ROWS, WIDTH)
+    feat = pl.BlockSpec((1, ROWS, WIDTH), lambda j: (j, 0, 0))
+    out = shape(ROWS, WIDTH)
     return pl.pallas_call(
-        body,
-        out_shape=outs,
-        in_specs=[pl.BlockSpec(memory_space=pltpu.SMEM)] + [pl.BlockSpec(memory_space=pltpu.VMEM)] * len(ins),
-        out_specs=[pl.BlockSpec(memory_space=pltpu.VMEM)] * len(outs),
-        scratch_shapes=scratch,
-        compiler_params=pltpu.CompilerParams(vmem_limit_bytes=vmem),
-    )(jnp.stack([z, a]).astype(jnp.int32), *ins)
-
-
-GROUP = 40
-
-
-def spread_taps(spread, taps, a):
-    for i in range(MRLEN):
-        spread[i] = jnp.broadcast_to(taps[pl.ds(i, 1), cols(a)], (8, DH))
-
-
-def hyena_body(where, fx, short, mr, tok, stream, qm, km, vm, lm, pr, feat, spread):
-    z, a = where[0], where[1]
-    spread_taps(spread, mr, a)
-    keep_head = (z > 0).astype(F32)
-    keep_tail = (z < SLABS - 1).astype(F32)
-    for j in range(3):
-        feat[j, pl.ds(0, HALO)] = fx[j, pl.ds(0, HALO)].astype(F32) * keep_head
-        feat[j, pl.ds(HALO, SLAB)] = fx[j, pl.ds(HALO, SLAB)].astype(F32)
-        feat[j, pl.ds(HALO + SLAB, HALO)] = fx[j, pl.ds(HALO + SLAB, HALO)].astype(F32) * keep_tail
-
-    taps = [[short[j, pl.ds(s, 1), cols(a)] for s in range(SHORT)] for j in range(3)]
-
-    def mixed(j, base, count):
-        total = taps[j][0] * feat[j, pl.ds(base, count)]
-        for s in range(1, SHORT):
-            total += taps[j][s] * feat[j, pl.ds(base - s, count)]
-        return total
-
-    pr[pl.ds(0, 16)] = jnp.zeros((16, DH), F32)
-
-    def head_step(g, carry):
-        base = pl.multiple_of(16 + g * 16, 16)
-        pr[pl.ds(base, 16)] = (mixed(1, base, 16) * mixed(2, base, 16)).astype(BF).astype(F32)
-        return carry
-
-    lax.fori_loop(0, (HALO - 16) // 16, head_step, 0)
-
-    def mix_step(g, carry):
-        base = pl.multiple_of(HALO + g * GROUP, 8)
-        local = pl.multiple_of(g * GROUP, 8)
-        key, value = mixed(1, base, GROUP), mixed(2, base, GROUP)
-        km[pl.ds(local, GROUP)] = key
-        vm[pl.ds(local, GROUP)] = value
-        qm[pl.ds(local, GROUP)] = mixed(0, base, GROUP)
-        pr[pl.ds(base, GROUP)] = (key * value).astype(BF).astype(F32)
-        return carry
-
-    lax.fori_loop(0, (SLAB + TAIL) // GROUP, mix_step, 0)
-
-    def tail_step(g, carry):
-        local = pl.multiple_of(SLAB + TAIL + g * 16, 16)
-        qm[pl.ds(local, 16)] = mixed(0, local + HALO, 16)
-        return carry
-
-    lax.fori_loop(0, (HALO - TAIL) // 16, tail_step, 0)
-
-    def long_step(g, carry):
-        base = pl.multiple_of(HALO + g * GROUP, 8)
-        local = pl.multiple_of(g * GROUP, 8)
-        total = [jnp.zeros((8, DH), F32) for _ in range(GROUP // 8)]
-        for i in range(MRLEN):
-            tap = spread[i]
-            for n in range(GROUP // 8):
-                total[n] += tap * pr[pl.ds(base + (n * 8 - i), 8)]
-        for n in range(GROUP // 8):
-            lm[pl.ds(local + n * 8, 8)] = total[n]
-        return carry
-
-    lax.fori_loop(0, (SLAB + TAIL) // GROUP, long_step, 0)
-    own = pl.ds(0, SLAB)
-    stream[...] = (tok[...].astype(F32) + qm[own] * lm[own]).astype(BF)
-
-
-def back_body(where, dv, ch, chalo, fx, short, mr, qm, km, vm, lm, pr, sg, fg, small, mg, stack, feat, spread):
-    z, a = where[0], where[1]
-    spread_taps(spread, mr, a)
-    keep_head = (z > 0).astype(F32)
-    keep_tail = (z < SLABS - 1).astype(F32)
-    own, halo = pl.ds(0, SLAB), pl.ds(SLAB, HALO)
-
-    grad = (ch[...].astype(F32) + dv[own]).astype(BF)
-    sg[...] = grad
-    mg[own] = (grad.astype(F32) * qm[own]).astype(BF).astype(F32)
-    grad_halo = (chalo[...].astype(F32) + dv[halo]).astype(BF).astype(F32) * keep_tail
-    mg[halo] = (grad_halo * qm[halo]).astype(BF).astype(F32)
-    stack[0, own] = grad.astype(F32) * lm[own]
-    stack[0, pl.ds(SLAB, TAIL)] = grad_halo[:TAIL] * lm[pl.ds(SLAB, TAIL)]
-    for j in range(3):
-        feat[j, pl.ds(0, 16)] = fx[j, pl.ds(HALO - 16, 16)].astype(F32) * keep_head
-        feat[j, pl.ds(16, SLAB)] = fx[j, pl.ds(HALO, SLAB)].astype(F32)
-
-    def long_step(g, carry):
-        local = pl.multiple_of(g * GROUP, 8)
-        total = [jnp.zeros((8, DH), F32) for _ in range(GROUP // 8)]
-        for i in range(MRLEN):
-            tap = spread[i]
-            for n in range(GROUP // 8):
-                total[n] += tap * mg[pl.ds(local + (n * 8 + i), 8)]
-        for n in range(GROUP // 8):
-            part = pl.ds(local + n * 8, 8)
-            stack[1, part] = total[n] * vm[part]
-            stack[2, part] = total[n] * km[part]
-        return carry
-
-    lax.fori_loop(0, (SLAB + TAIL) // GROUP, long_step, 0)
-
-    for j in range(3):
-        taps = [short[j, pl.ds(s, 1), cols(a)] for s in range(SHORT)]
-
-        def short_step(g, sums):
-            base = pl.multiple_of(g * 32, 32)
-            total = taps[0] * stack[j, pl.ds(base, 32)]
-            for s in range(1, SHORT):
-                total += taps[s] * stack[j, pl.ds(base + s, 32)]
-            fg[j, pl.ds(base, 32)] = total.astype(BF)
-            out = []
-            for s in range(SHORT):
-                term = stack[j, pl.ds(base, 32)] * feat[j, pl.ds(base + 16 - s, 32)]
-                out.append(sums[s] + (term[0:8] + term[8:16] + term[16:24] + term[24:32]))
-            return tuple(out)
-
-        sums = lax.fori_loop(0, SLAB // 32, short_step, tuple(jnp.zeros((8, DH), F32) for _ in range(SHORT)))
-        lines = [jnp.sum(t, axis=0, keepdims=True) for t in sums]
-        small[pl.ds(MRLEN + 16 * j, 16)] = jnp.concatenate(lines + [jnp.zeros((16 - SHORT, DH), F32)], axis=0).astype(BF)
-
-    def tap_step(c, carry):
-        first = c * 16
-
-        def row_step(g, sums):
-            base = pl.multiple_of(g * 16, 16)
-            out = list(sums)
-            for n in range(2):
-                line = mg[pl.ds(base + n * 8, 8)]
-                for s in range(16):
-                    out[s] += line * pr[pl.ds(base + (HALO + n * 8 - s) - first, 8)]
-            return tuple(out)
-
-        sums = lax.fori_loop(0, SLAB // 16, row_step, tuple(jnp.zeros((8, DH), F32) for _ in range(16)))
-        lines = [jnp.sum(t, axis=0, keepdims=True) for t in sums]
-        small[pl.ds(pl.multiple_of(first, 16), 16)] = jnp.concatenate(lines, axis=0).astype(BF)
-        return carry
-
-    lax.fori_loop(0, MRLEN // 16, tap_step, 0)
+        deliver_kernel,
+        grid=(3,),
+        out_shape=[
+            out,
+            out,
+            shape(3, ROWS, WIDTH, kind=F32),
+            shape(3, SHORT, WIDTH, kind=F32),
+            shape(MRLEN, WIDTH, kind=F32),
+            out,
+            out,
+        ],
+        in_specs=[mine] * 4 + [feat, fixed(*ins[-1].shape)],
+        out_specs=[mine, mine, feat, fixed(3, SHORT, WIDTH), fixed(MRLEN, WIDTH), mine, mine],
+        compiler_params=pltpu.CompilerParams(vmem_limit_bytes=32 << 20),
+    )(*ins)
 
 
 def local(tokens, w_feat, short_filter, mr_filter, queries, key_rows, cotangent):
     weights = w_feat.transpose(1, 0, 2)
     short_taps = short_filter.transpose(1, 0, 2)
-    head = shape(SLAB, DH)
-    th, qh, ch, chalo, fx, kfull, pieces = front(tokens, queries, key_rows, cotangent, weights)
+    th, qh, ch, chalo, fx, kfull, *pieces = front(tokens, queries, key_rows, cotangent, weights)
     token_parts = [pieces[0]]
     for d in range(1, HEADS):
         route = [(s * HEADS + a, s * HEADS + (a + d) % HEADS) for s in range(SLABS) for a in range(HEADS)]
         token_parts.append(lax.ppermute(pieces[d], "ctx", route))
-    filters = [pltpu.VMEM((MRLEN, 8, DH), F32)]
-    stream, qm, km, vm, lm, pr = compute(
-        hyena_body,
-        [
-            head,
-            shape(SLAB + HALO, DH, kind=F32),
-            shape(SLAB + TAIL, DH, kind=F32),
-            shape(SLAB + TAIL, DH, kind=F32),
-            shape(SLAB + TAIL, DH, kind=F32),
-            shape(HALO + SLAB + TAIL, DH, kind=F32),
-        ],
-        [pltpu.VMEM((3, EXT, DH), F32)] + filters,
-        fx,
-        short_taps,
-        mr_filter,
-        th,
+    block, grad_queries, sg, fg, dk, short_part, mg, pr = middle(
+        fx, th, qh, kfull, ch, chalo, short_taps, mr_filter
     )
-    block_out, grad_queries, dv, dk = attention(qh, kfull, stream, ch)
-    sg, fg, small = compute(
-        back_body,
-        [head, shape(3, SLAB, DH), shape(MRLEN + 3 * 16, DH)],
-        [
-            pltpu.VMEM((SLAB + HALO, DH), F32),
-            pltpu.VMEM((3, SLAB + TAIL, DH), F32),
-            pltpu.VMEM((3, SLAB + 16, DH), F32),
-        ]
-        + filters,
-        dv,
-        ch,
-        chalo,
-        fx,
-        short_taps,
-        mr_filter,
-        qm,
-        km,
-        vm,
-        lm,
-        pr,
+    grad_input, grad_feat, grad_keys, small = finale(fg, sg, dk, short_part, mg, pr, token_parts, weights)
+    block_out, grad_input, grad_feat, grad_short, grad_mr, grad_queries, grad_keys = deliver(
+        block, grad_queries, grad_keys, grad_input, grad_feat, small
     )
-    grad_input, grad_feat, grad_keys, small_home = finale(fg, sg, dk, small, token_parts, weights)
-    sums = small_home.astype(F32)
-    grad_short = sums[MRLEN:].reshape(3, 16, WIDTH)[:, :SHORT].transpose(1, 0, 2)
-    grad_feat = grad_feat.transpose(1, 0, 2)
-    grad_mr = sums[:MRLEN]
+    grad_feat, grad_short = grad_feat.transpose(1, 0, 2), grad_short.transpose(1, 0, 2)
     return (block_out, grad_input, grad_feat, grad_short, grad_mr, grad_queries, grad_keys)
 
 

time: 203 us -> 164 us (0.81)
  Pallas kernels: 182 us -> 155 us
  local copies, waits for them, and re-layouts: 11.8 us -> 5.32 us
  starting transfers between devices: 8.04 us -> 2.42 us
    pallas_call x3 -> x2, Pallas kernels: 88.4 us -> 59.7 us  [the longest x1 57.5 us: middle(): pl.pallas_call(middle_kernel, out_shape=[mine, mine, head, shape(3, SLAB,...]
    ppermute x3, starting transfers between devices: 8.04 us -> 2.42 us  [local(): token_parts.append(lax.ppermute(pieces[d], 'ctx', route))]
    slice x2 -> x0, local copies, waits for them, and re-layouts: 2.56 us -> none  [the longest x1 1.63 us: local(): grad_mr = sums[:MRLEN]]
    squeeze x1 -> x0, local copies, waits for them, and re-layouts: 2.48 us -> none  [local(): token_parts.append(lax.ppermute(pieces[d], 'ctx', route))]
    unnamed x19 -> x18, local copies, waits for them, and re-layouts: 6.11 us -> 5.32 us
  transfers between devices with their start and end apart: 3 -> 3, of which waited for: 0 -> 0; matrix products, arithmetic and copies ran while one was open for 0% -> 0% of each run, Pallas kernels for 44% -> 35%
where the time goes in v4:
time: 164 us; the launch traced here: 163 us
  Pallas kernels  155 us (95%)
  local copies, waits for them, and re-layouts  5.32 us (3%)
  starting transfers between devices  2.42 us (1%)
    pallas_call x1, Pallas kernels, middle(): pl.pallas_call(middle_kernel, out_shape=[mine, mine, head, shape(3, SLAB,...  57.5 us
    pallas_call x1, Pallas kernels, finale(): pl.pallas_call(finale_kernel, out_shape=[shape(ROWS, WIDTH), shape(3, ROW...  50 us
    pallas_call x1, Pallas kernels, front(): pl.pallas_call(front_kernel, out_shape=outs, in_specs=[vmem] * 4 + [any_s...  45.2 us
    unnamed x18, local copies, waits for them, and re-layouts  5.32 us
  transfers between devices with their start and end apart: 3, of which 0 were waited for; matrix products, arithmetic and copies ran while one was open for 0% of the time, Pallas kernels for 35%

profile of v4, /device:TPU:1, one launch (start us, length us, event | category | flops | bytes accessed | tf_op | source)
XLA Modules:
  0.0 163.4 jit_solution(5596280094847833685)
XLA Ops:
  0.6 45.2 %shard_map.126 = (bf16[1024,128]{1,0:T(8,128)(2,1)}, bf16[1024,128]{1,0:T(8,128)(2,1)}, bf16[1024,128]{1,0:T(8,128)(2,1)}, bf16[144,128]{1,0:T(8,128)(2,1)}, bf1...) custom-call(bf16[256,512]{1,0:T(8,128)(2,1)} %tokens.1, ...), custom_call_target="tpu_custom_call" | custom-call | tf_op jit(solution)/shard_map/pallas_call | solution.py:262
  45.9 0.2 collective-permute-start
  46.1 2.2 %collective-permute-start.1 = (bf16[256,1024]{1,0:T(8,128)(2,1)}, bf16[256,1024]{1,0:T(8,128)(2,1)S(1)}, u32[]{:S(2)}, u32[]{:S(2)}) collective-permute-start(bf16[256,1024]{1,0:T(8,128)(2,1)} %get-tuple-element.52), channel_id=1, source_target_pairs={{0,16},{8,24},{16,0},{24,8},{32,48},{40,56},{48,32},{56,40},{64,80... | collective-permute-start | bytes 1572872 | tf_op jit(solution)/shard_map/ppermute | solution.py:960
  48.3 0.0 collective-permute-start.2
  48.3 57.5 %shard_map.127 = (bf16[256,512]{1,0:T(8,128)(2,1)}, bf16[256,512]{1,0:T(8,128)(2,1)}, bf16[1024,128]{1,0:T(8,128)(2,1)}, bf16[3,1024,128]{2,1,0:T(8,128)(2,1)}, ...) custom-call(bf16[3,1312,128]{2,1,0:T(8,128)(2,1)} %get-tuple-element.36.fx, ...), custom_call_target="tpu_custom_call" | custom-call | tf_op jit(solution)/shard_map/pallas_call | solution.py:654
  105.8 0.0 collective-permute-done.part1
  105.8 0.0 copy-start.6
  105.8 0.0 collective-permute-done.1.part2
  105.8 0.0 copy-start.7
  105.8 0.0 collective-permute-done.2.part3
  105.8 0.0 copy-start.8
  105.9 0.7 copy-done.6
  106.6 0.2 copy-done.7
  106.8 0.2 copy-done.8
  106.9 0.0 copy-start.1
  106.9 50.0 %shard_map.128 = (bf16[256,512]{1,0:T(8,128)(2,1)}, f32[3,256,512]{2,1,0:T(8,128)}, bf16[256,512]{1,0:T(8,128)(2,1)}, bf16[176,512]{1,0:T(8,128)(2,1)}) custom-call(bf16[3,1024,128]{2,1,0:T(8,128)(2,1)} %get-tuple-element.44.fg, bf16[1024,128]{1,0:T(8,128)(2,1)} %get-tuple-element.45.sg, bf16[1024,128]{1,0:T(8,128)(2,1)} %get-tuple-element.46.dk, ...), custom_call_target="tpu_custom_call" | custom-call | tf_op jit(solution)/shard_map/pallas_call | solution.py:874
  156.9 0.0 copy-done.1
  157.0 0.0 copy-done.2
  157.0 0.0 copy-start
  157.0 1.4 copy-done
  158.4 0.9 copy-done.3
  159.3 0.9 copy-done.4
  160.3 0.9 copy-done.5
  161.2 2.2 %shard_map.129 = (bf16[256,512]{1,0:T(8,128)(2,1)}, bf16[256,512]{1,0:T(8,128)(2,1)}, f32[3,256,512]{2,1,0:T(8,128)}, f32[3,7,512]{2,1,0:T(8,128)}, f32[128,512]...) custom-call(bf16[256,512]{1,0:T(8,128)(2,1)S(1)} %copy-done.1, bf16[256,512]{1,0:T(8,128)(2,1)S(1)} %copy-done.2, ...), custom_call_target="tpu_custom_call" | custom-call | tf_op jit(solution)/shard_map/pallas_call | solution.py:935
  (4 shorter events, 0.0 us)
Async XLA Ops:
  45.9 59.9 %collective-permute-start = (bf16[256,1024]{1,0:T(8,128)(2,1)}, bf16[256,1024]{1,0:T(8,128)(2,1)S(1)}, u32[]{:S(2)}, u32[]{:S(2)}) collective-permute-start(bf16[256,1024]{1,0:T(8,128)(2,1)} %get-tuple-element.51), channel_id=1, source_target_pairs={{0,8},{8,16},{16,24},{24,0},{32,40},{40,48},{48,56},{56,32},{64,72... | collective-permute-start | bytes 1572872 | tf_op jit(solution)/shard_map/ppermute | solution.py:960
  46.1 59.8 %collective-permute-start.1 = (bf16[256,1024]{1,0:T(8,128)(2,1)}, bf16[256,1024]{1,0:T(8,128)(2,1)S(1)}, u32[]{:S(2)}, u32[]{:S(2)}) collective-permute-start(bf16[256,1024]{1,0:T(8,128)(2,1)} %get-tuple-element.52), channel_id=1, source_target_pairs={{0,16},{8,24},{16,0},{24,8},{32,48},{40,56},{48,32},{56,40},{64,80... | collective-permute-start | bytes 1572872 | tf_op jit(solution)/shard_map/ppermute | solution.py:960
  48.3 57.6 %collective-permute-start.2 = (bf16[256,1024]{1,0:T(8,128)(2,1)}, bf16[256,1024]{1,0:T(8,128)(2,1)S(1)}, u32[]{:S(2)}, u32[]{:S(2)}) collective-permute-start(bf16[256,1024]{1,0:T(8,128)(2,1)} %get-tuple-element.53), channel_id=1, source_target_pairs={{0,24},{8,0},{16,8},{24,16},{32,56},{40,32},{48,40},{56,48},{64,88... | collective-permute-start | bytes 1572872 | tf_op jit(solution)/shard_map/ppermute | solution.py:960
  105.8 0.8 copy-start.6
  105.8 1.0 copy-start.7
  105.8 1.1 copy-start.8
  106.9 50.0 %copy-start.1 = (bf16[256,512]{1,0:T(8,128)(2,1)S(1)}, bf16[256,512]{1,0:T(8,128)(2,1)}, u32[]{:S(2)}) copy-start(bf16[256,512]{1,0:T(8,128)(2,1)} %get-tuple-element.42.block) | copy-start | bytes 786436
  106.9 50.0 %copy-start.2 = (bf16[256,512]{1,0:T(8,128)(2,1)S(1)}, bf16[256,512]{1,0:T(8,128)(2,1)}, u32[]{:S(2)}) copy-start(bf16[256,512]{1,0:T(8,128)(2,1)} %get-tuple-element.43.grad_q) | copy-start | bytes 786436
  157.0 1.4 copy-start
  158.4 0.9 copy-start.3
  159.3 0.9 copy-start.4
  160.3 0.9 copy-start.5

commit v5 on v4

--- a/solution.py
+++ b/solution.py
@@ -48,7 +48,7 @@
     barrier = pltpu.get_barrier_semaphore()
     for device in devices:
         pl.semaphore_signal(barrier, inc=1, device_id=device, device_id_type=MESH)
-    pl.semaphore_wait(barrier, len(devices))
+    return functools.partial(pl.semaphore_wait, barrier, len(devices))
 
 
 class Courier:
@@ -128,13 +128,17 @@
     other = 1 - row
     right, left, across = turn(col, 1, 4), turn(col, -1, 4), turn(col, 2, 4)
     up, down = turn(z, 1, SLABS), turn(z, -1, SLABS)
-    for j in range(3):
-        mail.keep(weights.at[j], w.at[j])
-    greet(
+    greeted = greet(
         [{"row": other}, {"col": right}, {"col": left}]
         + [at_ctx(z, turn(a, d, HEADS)) for d in range(1, HEADS)]
         + [at_ctx(s, b) for s in (up, down) for b in range(HEADS)]
     )
+    for j in range(3):
+        mail.keep(weights.at[j], w.at[j])
+    full[:, cols(row * 4 + col, WIDTH)] = tokens[...]
+    kh[rows(a, ROWS)] = keys[:, cols(a)]
+    acc[...] = jnp.zeros_like(acc)
+    greeted()
 
     def block(r, c):
         return full.at[:, cols(r * 4 + c, WIDTH)]
@@ -150,9 +154,6 @@
     vertical = mail.push(tokens, block(row, col), {"row": other})
     fr = mail.push(tokens, block(row, col), {"col": right})
     fl = mail.push(tokens, block(row, col), {"col": left})
-    full[:, cols(row * 4 + col, WIDTH)] = tokens[...]
-    kh[rows(a, ROWS)] = keys[:, cols(a)]
-    acc[...] = jnp.zeros_like(acc)
     mail.settle()
     project(row, col, tokens[...])
     mail.arrive(vertical)
@@ -461,8 +462,8 @@
 
 
 def middle_kernel(
-    fx, tok, q, k, ct, chalo, short, mr,
-    block_home, dq_home, sg, fg, dk, short_part, mg, pr,
+    fx, tok, q, k, ct, chalo, short, mr, piece1, piece2, piece3,
+    block_home, dq_home, part1, part2, part3, sg, fg, dk, short_part, mg, pr,
     stream, v, kt, vt, st, pt, tops, outs, ctt, cs, delta, block, dq, dqt, dv, dka, edge, dv_out, dk_out, dv_in, dk_in,
     qm, km, vm, lm, feat, stack, shifts, spread,
     dv_send, dv_recv, dk_send, dk_recv, send, recv, loc,
@@ -473,6 +474,7 @@
     gain = scale * 1.4426950408889634
     mine = rows(z, SLAB)
     up, down = at_ctx(turn(z, 1, SLABS), a), at_ctx(turn(z, -1, SLABS), a)
+    greeted = greet(around(z, a))
     spread_taps(spread, mr, a)
 
     def turn_keys(s, carry):
@@ -480,10 +482,12 @@
         return carry
 
     hyena(z, a, fx, short, tok, stream, qm, km, vm, lm, pr, feat, shifts, spread)
-    greet(around(z, a))
+    greeted()
     from_down = mail.push(stream, v.at[mine], up)
     from_up = mail.push(stream, v.at[mine], down)
     v[mine] = stream[...]
+    for d, (piece, part) in enumerate(((piece1, part1), (piece2, part2), (piece3, part3)), 1):
+        mail.push(piece, part, at_ctx(z, turn(a, d, HEADS)))
 
     def lanes_of(i):
         return pl.ds(i * ROWS, ROWS)
@@ -516,10 +520,10 @@
     half = SLAB // 2
     mail.arrive(from_down)
     lower = v.at[pl.ds(pl.multiple_of(turn(z, -1, SLABS) * SLAB, SLAB), half)]
-    mail.push(lower, lower, up)
+    low = mail.push(lower, lower, up)
     mail.arrive(from_up)
     upper = v.at[pl.ds(pl.multiple_of(turn(z, 1, SLABS) * SLAB + half, half), half)]
-    mail.push(upper, upper, down)
+    high = mail.push(upper, upper, down)
 
     for i in range(HEADS):
         span = ROWS * (i + 1)
@@ -534,8 +538,8 @@
 
     inverse = 1.0 / lax.fori_loop(0, z * (SLAB // CHUNK), weigh_step, tops[...])
     lax.fori_loop(0, z + 1, turn_keys, 0)
-    mail.arrive(2)
-    mail.arrive(3)
+    mail.arrive(low)
+    mail.arrive(high)
 
     def turn_values(s, carry):
         vt[:, cols(s, SLAB)] = v[rows(s, SLAB)].T
@@ -646,7 +650,7 @@
     lax.fori_loop(1, z + 1, sent_step, 0)
 
 
-def middle(fx, tok, q, k, ct, chalo, short, mr):
+def middle(fx, tok, q, k, ct, chalo, short, mr, *pieces):
     any_space, vmem = pl.BlockSpec(memory_space=pl.ANY), pl.BlockSpec(memory_space=pltpu.VMEM)
     whole = SLABS * SLAB
     mine, head = shape(ROWS, WIDTH), shape(SLAB, DH)
@@ -656,6 +660,7 @@
         out_shape=[
             mine,
             mine,
+            *pieces,
             head,
             shape(3, SLAB, DH),
             head,
@@ -663,8 +668,8 @@
             shape(SLAB + HALO, DH, kind=F32),
             shape(HALO + SLAB + TAIL, DH, kind=F32),
         ],
-        in_specs=[vmem] * 8,
-        out_specs=[any_space] * 2 + [vmem] * 6,
+        in_specs=[vmem] * 8 + [any_space] * 3,
+        out_specs=[any_space] * 5 + [vmem] * 6,
         scratch_shapes=[
             pltpu.VMEM((SLAB, DH), BF),
             pltpu.VMEM((whole, DH), BF),
@@ -699,14 +704,14 @@
             dma((SLABS - 1,)),
             dma((SLABS - 1,)),
             dma((SLABS - 1,)),
-            dma((10,)),
-            dma((10,)),
+            dma((13,)),
+            dma((13,)),
             dma((2,)),
         ],
         compiler_params=pltpu.CompilerParams(
             collective_id=2, has_side_effects=True, vmem_limit_bytes=58 << 20
         ),
-    )(fx, tok, q, k, ct, chalo, short, mr)
+    )(fx, tok, q, k, ct, chalo, short, mr, *pieces)
 
 
 def finale_kernel(
@@ -728,14 +733,18 @@
     mail.keep(fg, fgall.at[a])
     for d, part in enumerate((part0, part1, part2, part3)):
         mail.keep(part, tq.at[rows(turn(a, -d, HEADS), ROWS)])
+    greeted = greet(around(z, a) + [{"row": 1 - row}, {"col": right}, {"col": left}])
     loads = [pltpu.make_async_copy(weights.at[j], w.at[j], loc.at[8 + j]) for j in range(3)]
     for load in loads:
         load.start()
-    greet(around(z, a) + [{"row": 1 - row}, {"col": right}, {"col": left}])
+    greeted()
 
     near_rows, far_rows = rows(side, pair), rows(1 - side, pair)
+    direct = [
+        mail.push(fg.at[:, rows(to, ROWS)], fgall.at[a, :, rows(to, ROWS)], at_ctx(z, to)) for to in (far, far_mate)
+    ]
     to_mate = mail.push(fg, fgall.at[a], at_ctx(z, mate))
-    first = mail.push(fg.at[:, far_rows], fgall.at[a, :, far_rows], at_ctx(z, far))
+    second = mail.push(fg.at[:, near_rows], fgall.at[a, :, near_rows], at_ctx(z, far))
     mail.settle()
 
     for b in range(SLABS):
@@ -782,43 +791,50 @@
     tap_grads(shifts, mg, lines)
     small[pl.ds(0, MRLEN)] = lines[...].reshape(MRLEN, DH).astype(BF)
     small[pl.ds(MRLEN, short_part.shape[0])] = short_part[...]
-    mail.arrive(first)
-    relay = mail.push(fgall.at[far, :, near_rows], fgall.at[far, :, near_rows], at_ctx(z, mate))
-    second = mail.push(fg.at[:, near_rows], fgall.at[a, :, near_rows], at_ctx(z, far))
     small_in = [mail.push(small, slots.at[d - 1], at_ctx(turn(z, d, SLABS), a)) for d in range(1, SLABS)]
-    ring[0] = weight_second(0, ring[0])
-    ring[1] = weight_second(1, ring[1])
-    mail.arrive(relay)
-
+    for k in direct:
+        mail.arrive(k)
+    relays = [
+        mail.push(fgall.at[h, :, rows(a, ROWS)], fgall.at[h, :, rows(a, ROWS)], at_ctx(z, mate))
+        for h in (far, far_mate)
+    ]
+
+    for n in range(2):
+        ring[n] = weight_second(n, ring[n])
     for j in range(3):
         for h in range(HEADS):
             fgm[j, :, pl.ds(h * DH, DH)] = fgall[h, j, rows(a, ROWS)]
-
     for load in loads:
         load.wait()
 
-    def term_block(dc):
-        for r in range(2):
-            columns = rows(r * 4 + turn(col, dc, 4), WIDTH)
-            out = jnp.zeros((ROWS, WIDTH), F32)
-            for j in range(3):
-                out += lax.dot_general(
-                    fgm[j], w[j, columns], (((1,), (1,)), ((), ())), preferred_element_type=F32
-                )
-            tsend[dc, r] = out.astype(BF)
-
     top, bottom = pl.ds(0, half), pl.ds(half, half)
-    term_block(2)
-    from_left = mail.push(tsend.at[2, :, top], xr1.at[0], {"col": right})
-    from_right = mail.push(tsend.at[2, :, bottom], xr1.at[1], {"col": left})
-    term_block(1)
-    term_block(3)
-    mail.arrive(from_left)
-    tsend[1, :, top] = (tsend[1, :, top].astype(F32) + xr1[0].astype(F32)).astype(BF)
-    from_left = mail.push(tsend.at[1], xr2.at[0], {"col": right})
-    mail.arrive(from_right)
-    tsend[3, :, bottom] = (tsend[3, :, bottom].astype(F32) + xr1[1].astype(F32)).astype(BF)
-    from_right = mail.push(tsend.at[3], xr2.at[1], {"col": left})
+    shares = (1 - row, row)
+
+    def term_block(dc, n):
+        columns = rows(shares[n] * 4 + turn(col, dc, 4), WIDTH)
+        out = jnp.zeros((ROWS, WIDTH), F32)
+        for j in range(3):
+            out += lax.dot_general(fgm[j], w[j, columns], (((1,), (1,)), ((), ())), preferred_element_type=F32)
+        tsend[dc, n] = out.astype(BF)
+
+    firsts, seconds = [], []
+    for n in range(2):
+        term_block(2, n)
+        firsts.append(
+            (
+                mail.push(tsend.at[2, n, top], xr1.at[0, n], {"col": right}),
+                mail.push(tsend.at[2, n, bottom], xr1.at[1, n], {"col": left}),
+            )
+        )
+    for n in range(2):
+        term_block(1, n)
+        term_block(3, n)
+        mail.arrive(firsts[n][0])
+        tsend[1, n, top] = (tsend[1, n, top].astype(F32) + xr1[0, n].astype(F32)).astype(BF)
+        from_left = mail.push(tsend.at[1, n], xr2.at[0, n], {"col": right})
+        mail.arrive(firsts[n][1])
+        tsend[3, n, bottom] = (tsend[3, n, bottom].astype(F32) + xr1[1, n].astype(F32)).astype(BF)
+        seconds.append((from_left, mail.push(tsend.at[3, n], xr2.at[1, n], {"col": left})))
     home_sg = []
     for d in range(1, HEADS):
         to = turn(a, d, HEADS)
@@ -826,13 +842,23 @@
         mail.push(dk.at[rows(to, ROWS)], dk_home.at[:, cols(a)], at_ctx(z, to))
     mail.keep(sg.at[rows(a, ROWS)], sgh.at[:, cols(a)])
     mail.keep(dk.at[rows(a, ROWS)], dk_home.at[:, cols(a)])
-    term_block(0)
-
+    term_block(0, 0)
+    term_block(0, 1)
     mail.arrive(second)
-    relay = mail.push(fgall.at[far, :, far_rows], fgall.at[far, :, far_rows], at_ctx(z, mate))
+    relays.append(mail.push(fgall.at[far, :, far_rows], fgall.at[far, :, far_rows], at_ctx(z, mate)))
+    for k in relays[:2]:
+        mail.arrive(k)
     ring.append(weight_first(2, far))
-    mail.arrive(relay)
+    mail.arrive(relays[2])
     ring.append(weight_first(3, far_mate))
+
+    def term_sum(n):
+        for k in seconds[n]:
+            mail.arrive(k)
+        return tsend[0, n].astype(F32) + xr2[0, n].astype(F32) + xr2[1, n].astype(F32)
+
+    ysend[...] = term_sum(0).astype(BF)
+    across = mail.push(ysend, yr, {"row": 1 - row})
     ring[2] = weight_second(2, ring[2])
     ring[3] = weight_second(3, ring[3])
 
@@ -843,21 +869,13 @@
         mail.push(total, small_home.at[:, cols(a)], at_ctx(z, turn(a, d, HEADS)))
     mail.keep(total, small_home.at[:, cols(a)])
 
-    mail.arrive(from_left)
-    mail.arrive(from_right)
-
-    def term_sum(r):
-        return tsend[0, r].astype(F32) + xr2[0, r].astype(F32) + xr2[1, r].astype(F32)
-
-    ysend[...] = term_sum(1 - row).astype(BF)
-    across = mail.push(ysend, yr, {"row": 1 - row})
     weight_third(0, a, ring[0])
     weight_third(1, mate, ring[1])
     for k in home_sg:
         mail.arrive(k)
     mail.settle()
     mail.arrive(across)
-    grad_input[...] = (sgh[...].astype(F32) + term_sum(row) + yr[...].astype(F32)).astype(BF)
+    grad_input[...] = (sgh[...].astype(F32) + term_sum(1) + yr[...].astype(F32)).astype(BF)
     weight_third(2, far, ring[2])
     weight_third(3, far_mate, ring[3])
     mail.finish()
@@ -870,7 +888,7 @@
 def finale(fg, sg, dk, short_part, mg, pr, parts, weights):
     lines = MRLEN + short_part.shape[0]
     any_space, vmem = pl.BlockSpec(memory_space=pl.ANY), pl.BlockSpec(memory_space=pltpu.VMEM)
-    remotes = 3 + 3 + 6 + 16 + 2 + 4 + 3 + 1
+    remotes = 1 + 3 + 3 + 6 + 6 + 16 + 8 + 1
     return pl.pallas_call(
         finale_kernel,
         out_shape=[
@@ -946,7 +964,7 @@
         ],
         in_specs=[mine] * 4 + [feat, fixed(*ins[-1].shape)],
         out_specs=[mine, mine, feat, fixed(3, SHORT, WIDTH), fixed(MRLEN, WIDTH), mine, mine],
-        compiler_params=pltpu.CompilerParams(vmem_limit_bytes=32 << 20),
+        compiler_params=pltpu.CompilerParams(vmem_limit_bytes=60 << 20),
     )(*ins)
 
 
@@ -954,14 +972,10 @@
     weights = w_feat.transpose(1, 0, 2)
     short_taps = short_filter.transpose(1, 0, 2)
     th, qh, ch, chalo, fx, kfull, *pieces = front(tokens, queries, key_rows, cotangent, weights)
-    token_parts = [pieces[0]]
-    for d in range(1, HEADS):
-        route = [(s * HEADS + a, s * HEADS + (a + d) % HEADS) for s in range(SLABS) for a in range(HEADS)]
-        token_parts.append(lax.ppermute(pieces[d], "ctx", route))
-    block, grad_queries, sg, fg, dk, short_part, mg, pr = middle(
-        fx, th, qh, kfull, ch, chalo, short_taps, mr_filter
+    block, grad_queries, *token_parts, sg, fg, dk, short_part, mg, pr = middle(
+        fx, th, qh, kfull, ch, chalo, short_taps, mr_filter, *pieces[1:]
     )
-    grad_input, grad_feat, grad_keys, small = finale(fg, sg, dk, short_part, mg, pr, token_parts, weights)
+    grad_input, grad_feat, grad_keys, small = finale(fg, sg, dk, short_part, mg, pr, [pieces[0], *token_parts], weights)
     block_out, grad_input, grad_feat, grad_short, grad_mr, grad_queries, grad_keys = deliver(
         block, grad_queries, grad_keys, grad_input, grad_feat, small
     )

time: 164 us -> 149 us (0.909)
  Pallas kernels: 155 us -> 148 us
  local copies, waits for them, and re-layouts: 5.32 us -> 0 us
  starting transfers between devices: 2.42 us -> 0 us
    pallas_call x1, Pallas kernels: 50 us -> 42 us  [finale(): pl.pallas_call(finale_kernel, out_shape=[shape(ROWS, WIDTH), shape(3, ROW...]
    unnamed x18 -> x0, local copies, waits for them, and re-layouts: 5.32 us -> none
    ppermute x3 -> x0, starting transfers between devices: 2.42 us -> none  [local(): token_parts.append(lax.ppermute(pieces[d], 'ctx', route))]
    pallas_call x1, Pallas kernels: 2.19 us -> 4.27 us  [deliver(): pl.pallas_call(deliver_kernel, grid=(3,), out_shape=[out, out, shape(3, R...]
  transfers between devices with their start and end apart: 3 -> 0, of which waited for: 0 -> 0; matrix products, arithmetic and copies ran while one was open for 0% -> 0% of each run, Pallas kernels for 35% -> 0%
where the time goes in v5:
time: 149 us
  Pallas kernels  148 us (99%)
    pallas_call x1, Pallas kernels, middle(): pl.pallas_call(middle_kernel, out_shape=[mine, mine, *pieces, head, shape...  57 us
    pallas_call x1, Pallas kernels, front(): pl.pallas_call(front_kernel, out_shape=outs, in_specs=[vmem] * 4 + [any_s...  45.2 us
    pallas_call x1, Pallas kernels, finale(): pl.pallas_call(finale_kernel, out_shape=[shape(ROWS, WIDTH), shape(3, ROW...  42 us
    pallas_call x1, Pallas kernels, deliver(): pl.pallas_call(deliver_kernel, grid=(3,), out_shape=[out, out, shape(3, R...  4.27 us

profile of v5, /device:TPU:1, one launch (start us, length us, event | category | flops | bytes accessed | tf_op | source)
XLA Modules:
  0.0 149.3 jit_solution(12685058021029562849)
XLA Ops:
  0.6 45.2 %shard_map.126 = (bf16[1024,128]{1,0:T(8,128)(2,1)}, bf16[1024,128]{1,0:T(8,128)(2,1)}, bf16[1024,128]{1,0:T(8,128)(2,1)}, bf16[144,128]{1,0:T(8,128)(2,1)}, bf1...) custom-call(bf16[256,512]{1,0:T(8,128)(2,1)} %tokens.1, ...), custom_call_target="tpu_custom_call" | custom-call | tf_op jit(solution)/shard_map/pallas_call | solution.py:263
  45.9 57.0 %shard_map.127 = (bf16[256,512]{1,0:T(8,128)(2,1)}, bf16[256,512]{1,0:T(8,128)(2,1)}, bf16[256,1024]{1,0:T(8,128)(2,1)}, bf16[256,1024]{1,0:T(8,128)(2,1)}, bf16...) custom-call(bf16[3,1312,128]{2,1,0:T(8,128)(2,1)} %get-tuple-element, ...), custom_call_target="tpu_custom_call" | custom-call | tf_op jit(solution)/shard_map/pallas_call | solution.py:658
  102.9 42.0 %shard_map.128 = (bf16[256,512]{1,0:T(8,128)(2,1)}, f32[3,256,512]{2,1,0:T(8,128)}, bf16[256,512]{1,0:T(8,128)(2,1)}, bf16[176,512]{1,0:T(8,128)(2,1)}) custom-call(bf16[3,1024,128]{2,1,0:T(8,128)(2,1)} %get-tuple-element.50.fg, bf16[1024,128]{1,0:T(8,128)(2,1)} %get-tuple-element.51.sg, bf16[1024,128]{1,0:T(8,128)(2,1)} %get-tuple-element.52.dk, ...), custom_call_target="tpu_custom_call" | custom-call | tf_op jit(solution)/shard_map/pallas_call | solution.py:892
  144.9 4.3 %shard_map.129 = (bf16[256,512]{1,0:T(8,128)(2,1)}, bf16[256,512]{1,0:T(8,128)(2,1)}, f32[3,256,512]{2,1,0:T(8,128)}, f32[3,7,512]{2,1,0:T(8,128)}, f32[128,512]...) custom-call(bf16[256,512]{1,0:T(8,128)(2,1)} %get-tuple-element.48.block, ...), custom_call_target="tpu_custom_call" | custom-call | tf_op jit(solution)/shard_map/pallas_call | solution.py:953

commit v6 on v5

--- a/solution.py
+++ b/solution.py
@@ -117,10 +117,8 @@
     mail.push(upper, upper, at_ctx(down, a))
 
 
-def front_kernel(
-    tokens, queries, keys, cot, weights,
-    th, qh, ch, chalo, fx, kfull, piece0, piece1, piece2, piece3,
-    full, w, acc, feats, kh, send, recv, loc,
+def front_phase(
+    greeted, w, tokens, queries, keys, cot, weights, th, qh, ch, chalo, fx, kfull, full, acc, feats, kh, send, recv, loc,
 ):
     mail = Courier(send, recv, loc)
     z, a = place()
@@ -128,11 +126,6 @@
     other = 1 - row
     right, left, across = turn(col, 1, 4), turn(col, -1, 4), turn(col, 2, 4)
     up, down = turn(z, 1, SLABS), turn(z, -1, SLABS)
-    greeted = greet(
-        [{"row": other}, {"col": right}, {"col": left}]
-        + [at_ctx(z, turn(a, d, HEADS)) for d in range(1, HEADS)]
-        + [at_ctx(s, b) for s in (up, down) for b in range(HEADS)]
-    )
     for j in range(3):
         mail.keep(weights.at[j], w.at[j])
     full[:, cols(row * 4 + col, WIDTH)] = tokens[...]
@@ -228,9 +221,6 @@
             for copy in last_rows(b):
                 copy.start()
 
-    for d, piece in enumerate((piece0, piece1, piece2, piece3)):
-        for s in range(SLABS):
-            mail.keep(full.at[:, cols(s * HEADS + turn(a, d, HEADS), ROWS)], piece.at[:, pl.ds(s * ROWS, ROWS)])
     mail.finish()
     for copy in first_rows(0) + last_rows(0):
         copy.wait_recv()
@@ -246,39 +236,6 @@
         for b in range(HEADS):
             for copy in last_rows(b):
                 copy.wait_send()
-
-
-def front(tokens, queries, keys, cot, weights):
-    any_space, vmem = pl.BlockSpec(memory_space=pl.ANY), pl.BlockSpec(memory_space=pltpu.VMEM)
-    head = shape(SLAB, DH)
-    outs = [
-        head,
-        head,
-        head,
-        shape(HALO, DH),
-        shape(3, EXT, DH),
-        shape(SLABS * SLAB, DH),
-    ] + [shape(ROWS, SLABS * ROWS)] * HEADS
-    remotes = 3 + 2 + 12 + 4 + 3 + 4 + 12
-    return pl.pallas_call(
-        front_kernel,
-        out_shape=outs,
-        in_specs=[vmem] * 4 + [any_space],
-        out_specs=[any_space] * len(outs),
-        scratch_shapes=[
-            pltpu.VMEM((ROWS, 8 * WIDTH), BF),
-            pltpu.VMEM(weights.shape, BF),
-            pltpu.VMEM((3, ROWS, WIDTH), F32),
-            pltpu.VMEM((3, ROWS, WIDTH), BF),
-            pltpu.VMEM((SLAB, DH), BF),
-            pltpu.SemaphoreType.DMA((remotes,)),
-            pltpu.SemaphoreType.DMA((remotes,)),
-            pltpu.SemaphoreType.DMA((3 + 3 + 1 + 1 + HEADS * SLABS,)),
-        ],
-        compiler_params=pltpu.CompilerParams(
-            collective_id=0, has_side_effects=True, vmem_limit_bytes=56 << 20
-        ),
-    )(tokens, queries, keys, cot, weights)
 
 
 def around(z, a):
@@ -461,10 +418,10 @@
         short_part[pl.ds(16 * j, 16)] = jnp.concatenate(lines + [jnp.zeros((16 - SHORT, DH), F32)], axis=0).astype(BF)
 
 
-def middle_kernel(
-    fx, tok, q, k, ct, chalo, short, mr, piece1, piece2, piece3,
-    block_home, dq_home, part1, part2, part3, sg, fg, dk, short_part, mg, pr,
-    stream, v, kt, vt, st, pt, tops, outs, ctt, cs, delta, block, dq, dqt, dv, dka, edge, dv_out, dk_out, dv_in, dk_in,
+def middle_phase(
+    st, full, fx, tok, q, k, ct, chalo, short, mr,
+    block_home, dq_home, part0, part1, part2, part3, sg, fg, dk, short_part, mg, pr,
+    stream, v, kt, vt, pt, tops, outs, ctt, cs, delta, block, dq, dqt, dv, dka, edge, dv_out, dk_out, dv_in, dk_in,
     qm, km, vm, lm, feat, stack, shifts, spread,
     dv_send, dv_recv, dk_send, dk_recv, send, recv, loc,
 ):
@@ -474,7 +431,6 @@
     gain = scale * 1.4426950408889634
     mine = rows(z, SLAB)
     up, down = at_ctx(turn(z, 1, SLABS), a), at_ctx(turn(z, -1, SLABS), a)
-    greeted = greet(around(z, a))
     spread_taps(spread, mr, a)
 
     def turn_keys(s, carry):
@@ -482,12 +438,17 @@
         return carry
 
     hyena(z, a, fx, short, tok, stream, qm, km, vm, lm, pr, feat, shifts, spread)
-    greeted()
     from_down = mail.push(stream, v.at[mine], up)
     from_up = mail.push(stream, v.at[mine], down)
     v[mine] = stream[...]
-    for d, (piece, part) in enumerate(((piece1, part1), (piece2, part2), (piece3, part3)), 1):
-        mail.push(piece, part, at_ctx(z, turn(a, d, HEADS)))
+    for d, part in enumerate((part0, part1, part2, part3)):
+        to = turn(a, d, HEADS)
+        for n in range(SLABS):
+            piece, slot = full.at[:, cols(n * HEADS + to, ROWS)], part.at[:, pl.ds(n * ROWS, ROWS)]
+            if d:
+                mail.push(piece, slot, at_ctx(z, to))
+            else:
+                mail.keep(piece, slot)
 
     def lanes_of(i):
         return pl.ds(i * ROWS, ROWS)
@@ -650,17 +611,42 @@
     lax.fori_loop(1, z + 1, sent_step, 0)
 
 
-def middle(fx, tok, q, k, ct, chalo, short, mr, *pieces):
+FRONT_REFS = 13
+OUT_REFS = 12
+
+
+def opening_kernel(tokens, queries, keys, cot, weights, short, mr, *refs):
+    outs, held, rest = refs[:OUT_REFS], refs[OUT_REFS : OUT_REFS + FRONT_REFS], refs[OUT_REFS + FRONT_REFS :]
+    th, qh, ch, chalo, fx, kfull, full = held[:7]
+    z, a = place()
+    row, col = lax.axis_index("row"), lax.axis_index("col")
+    greeted = greet(
+        [{"row": 1 - row}, {"col": turn(col, 1, 4)}, {"col": turn(col, -1, 4)}]
+        + [at_ctx(z, turn(a, d, HEADS)) for d in range(1, HEADS)]
+        + [at_ctx(turn(z, d, SLABS), b) for d in (1, -1) for b in range(HEADS)]
+        + [at_ctx(turn(z, 2, SLABS), a)]
+    )
+    pl.run_scoped(
+        lambda w: front_phase(greeted, w, tokens, queries, keys, cot, weights, *held), pltpu.VMEM(weights.shape, BF)
+    )
+    pl.run_scoped(
+        lambda st: middle_phase(st, full, fx, th, qh, kfull, ch, chalo, short, mr, *outs, *rest),
+        pltpu.VMEM((SLABS * SLAB, SLAB), F32),
+    )
+
+
+def opening(tokens, queries, keys, cot, weights, short, mr):
     any_space, vmem = pl.BlockSpec(memory_space=pl.ANY), pl.BlockSpec(memory_space=pltpu.VMEM)
     whole = SLABS * SLAB
     mine, head = shape(ROWS, WIDTH), shape(SLAB, DH)
     dma = pltpu.SemaphoreType.DMA
+    remotes = 3 + 2 + 12 + 4 + 2 + 2 + 3 + 12
     return pl.pallas_call(
-        middle_kernel,
+        opening_kernel,
         out_shape=[
             mine,
             mine,
-            *pieces,
+            *[shape(ROWS, SLABS * ROWS)] * HEADS,
             head,
             shape(3, SLAB, DH),
             head,
@@ -668,14 +654,26 @@
             shape(SLAB + HALO, DH, kind=F32),
             shape(HALO + SLAB + TAIL, DH, kind=F32),
         ],
-        in_specs=[vmem] * 8 + [any_space] * 3,
-        out_specs=[any_space] * 5 + [vmem] * 6,
+        in_specs=[vmem] * 4 + [any_space] + [vmem] * 2,
+        out_specs=[any_space] * 6 + [vmem] * 6,
         scratch_shapes=[
+            pltpu.VMEM((SLAB, DH), BF),
+            pltpu.VMEM((SLAB, DH), BF),
+            pltpu.VMEM((SLAB, DH), BF),
+            pltpu.VMEM((HALO, DH), BF),
+            pltpu.VMEM((3, EXT, DH), BF),
+            pltpu.VMEM((whole, DH), BF),
+            pltpu.VMEM((ROWS, 8 * WIDTH), BF),
+            pltpu.VMEM((3, ROWS, WIDTH), F32),
+            pltpu.VMEM((3, ROWS, WIDTH), BF),
+            pltpu.VMEM((SLAB, DH), BF),
+            dma((remotes,)),
+            dma((remotes,)),
+            dma((3 + 3 + 1 + 1,)),
             pltpu.VMEM((SLAB, DH), BF),
             pltpu.VMEM((whole, DH), BF),
             pltpu.VMEM((DH, whole), BF),
             pltpu.VMEM((DH, whole), BF),
-            pltpu.VMEM((whole, SLAB), F32),
             pltpu.VMEM((whole, SLAB), BF),
             pltpu.VMEM((1, SLAB), F32),
             pltpu.VMEM((DH, SLAB), F32),
@@ -704,14 +702,14 @@
             dma((SLABS - 1,)),
             dma((SLABS - 1,)),
             dma((SLABS - 1,)),
-            dma((13,)),
-            dma((13,)),
-            dma((2,)),
+            dma((22,)),
+            dma((22,)),
+            dma((6,)),
         ],
         compiler_params=pltpu.CompilerParams(
-            collective_id=2, has_side_effects=True, vmem_limit_bytes=58 << 20
+            collective_id=2, has_side_effects=True, vmem_limit_bytes=60 << 20
         ),
-    )(fx, tok, q, k, ct, chalo, short, mr, *pieces)
+    )(tokens, queries, keys, cot, weights, short, mr)
 
 
 def finale_kernel(
@@ -931,28 +929,30 @@
 
 def deliver_kernel(block, grad_q, grad_k, grad_in, grad_feat, small, block_o, in_o, feat_o, short_o, mr_o, q_o, k_o):
     feat_o[...] = grad_feat[...]
+    block_o[...] = block[...]
+    in_o[...] = grad_in[...]
+    q_o[...] = grad_q[...]
+    k_o[...] = grad_k[...]
 
     @pl.when(pl.program_id(0) == 0)
     def _():
-        block_o[...] = block[...]
-        in_o[...] = grad_in[...]
-        q_o[...] = grad_q[...]
-        k_o[...] = grad_k[...]
         mr_o[...] = small[pl.ds(0, MRLEN)].astype(F32)
         for j in range(3):
             short_o[j] = small[pl.ds(MRLEN + 16 * j, 16)].astype(F32)[:SHORT]
 
 
 def deliver(*ins):
+    steps = 4
+
     def fixed(*dims):
-        return pl.BlockSpec(dims, lambda j: (0,) * len(dims))
-
-    mine = fixed(ROWS, WIDTH)
-    feat = pl.BlockSpec((1, ROWS, WIDTH), lambda j: (j, 0, 0))
+        return pl.BlockSpec(dims, lambda n: (0,) * len(dims))
+
+    mine = pl.BlockSpec((ROWS // steps, WIDTH), lambda n: (n, 0))
+    feat = pl.BlockSpec((3, ROWS // steps, WIDTH), lambda n: (0, n, 0))
     out = shape(ROWS, WIDTH)
     return pl.pallas_call(
         deliver_kernel,
-        grid=(3,),
+        grid=(steps,),
         out_shape=[
             out,
             out,
@@ -971,11 +971,10 @@
 def local(tokens, w_feat, short_filter, mr_filter, queries, key_rows, cotangent):
     weights = w_feat.transpose(1, 0, 2)
     short_taps = short_filter.transpose(1, 0, 2)
-    th, qh, ch, chalo, fx, kfull, *pieces = front(tokens, queries, key_rows, cotangent, weights)
-    block, grad_queries, *token_parts, sg, fg, dk, short_part, mg, pr = middle(
-        fx, th, qh, kfull, ch, chalo, short_taps, mr_filter, *pieces[1:]
+    block, grad_queries, *token_parts, sg, fg, dk, short_part, mg, pr = opening(
+        tokens, queries, key_rows, cotangent, weights, short_taps, mr_filter
     )
-    grad_input, grad_feat, grad_keys, small = finale(fg, sg, dk, short_part, mg, pr, [pieces[0], *token_parts], weights)
+    grad_input, grad_feat, grad_keys, small = finale(fg, sg, dk, short_part, mg, pr, token_parts, weights)
     block_out, grad_input, grad_feat, grad_short, grad_mr, grad_queries, grad_keys = deliver(
         block, grad_queries, grad_keys, grad_input, grad_feat, small
     )

time: 149 us -> 148 us (level)
    pallas_call x3 -> x2, Pallas kernels: 106 us -> 105 us  [the longest x1 100 us: opening(): pl.pallas_call(opening_kernel, out_shape=[mine, mine, *[shape(ROWS, SLABS...]
where the time goes in v6:
time: 148 us; the launch traced here: 147 us
  Pallas kernels  147 us (99%)
    pallas_call x1, Pallas kernels, opening(): pl.pallas_call(opening_kernel, out_shape=[mine, mine, *[shape(ROWS, SLABS...  100 us
    pallas_call x1, Pallas kernels, finale(): pl.pallas_call(finale_kernel, out_shape=[shape(ROWS, WIDTH), shape(3, ROW...  41.9 us
    pallas_call x1, Pallas kernels, deliver(): pl.pallas_call(deliver_kernel, grid=(steps,), out_shape=[out, out, shape(...  4.22 us

profile of v6, /device:TPU:1, one launch (start us, length us, event | category | flops | bytes accessed | tf_op | source)
XLA Modules:
  0.0 147.3 jit_solution(32394589475101526)
XLA Ops:
  0.6 100.4 %shard_map.126 = (bf16[256,512]{1,0:T(8,128)(2,1)}, bf16[256,512]{1,0:T(8,128)(2,1)}, bf16[256,1024]{1,0:T(8,128)(2,1)}, bf16[256,1024]{1,0:T(8,128)(2,1)}, bf16...) custom-call(bf16[256,512]{1,0:T(8,128)(2,1)} %tokens.1, ...), custom_call_target="tpu_custom_call" | custom-call | tf_op jit(solution)/shard_map/pallas_call | solution.py:644
  101.1 41.9 %shard_map.127 = (bf16[256,512]{1,0:T(8,128)(2,1)}, f32[3,256,512]{2,1,0:T(8,128)}, bf16[256,512]{1,0:T(8,128)(2,1)}, bf16[176,512]{1,0:T(8,128)(2,1)}) custom-call(bf16[3,1024,128]{2,1,0:T(8,128)(2,1)} %get-tuple-element.32.fg, bf16[1024,128]{1,0:T(8,128)(2,1)} %get-tuple-element.33.sg, bf16[1024,128]{1,0:T(8,128)(2,1)} %get-tuple-element.34.dk, ...), custom_call_target="tpu_custom_call" | custom-call | tf_op jit(solution)/shard_map/pallas_call | solution.py:890
  143.0 4.2 %shard_map.128 = (bf16[256,512]{1,0:T(8,128)(2,1)}, bf16[256,512]{1,0:T(8,128)(2,1)}, f32[3,256,512]{2,1,0:T(8,128)}, f32[3,7,512]{2,1,0:T(8,128)}, f32[128,512]...) custom-call(bf16[256,512]{1,0:T(8,128)(2,1)} %get-tuple-element.30.block, ...), custom_call_target="tpu_custom_call" | custom-call | tf_op jit(solution)/shard_map/pallas_call | solution.py:953

commit v7 on v6

--- a/solution.py
+++ b/solution.py
@@ -133,25 +133,54 @@
     acc[...] = jnp.zeros_like(acc)
     greeted()
 
-    def block(r, c):
-        return full.at[:, cols(r * 4 + c, WIDTH)]
-
-    def half(r, c, h):
-        return full.at[pl.ds(h * (ROWS // 2), ROWS // 2), cols(r * 4 + c, WIDTH)]
-
-    def project(r, c, lhs=None):
-        lhs = full[:, cols(r * 4 + c, WIDTH)] if lhs is None else lhs
+    half, quarter = ROWS // 2, ROWS // 4
+
+    def piece(r, c, h):
+        return full.at[pl.ds(h * half, half), cols(r * 4 + c, WIDTH)]
+
+    def part(r, c, h, n):
+        return full.at[pl.ds(h * half + n * quarter, quarter), cols(r * 4 + c, WIDTH)]
+
+    def project(r, c, h):
+        here = pl.ds(h * half, half)
+        lhs = full[here, cols(r * 4 + c, WIDTH)]
         for j in range(3):
-            acc[j] += jnp.dot(lhs, w[j, rows(r * 4 + c, WIDTH)], preferred_element_type=F32)
-
-    vertical = mail.push(tokens, block(row, col), {"row": other})
-    fr = mail.push(tokens, block(row, col), {"col": right})
-    fl = mail.push(tokens, block(row, col), {"col": left})
+            acc[j, here] += jnp.dot(lhs, w[j, rows(r * 4 + c, WIDTH)], preferred_element_type=F32)
+
+    def launch(h):
+        src, dst = tokens.at[pl.ds(h * half, half)], piece(row, col, h)
+        return [mail.push(src, dst, device) for device in ({"row": other}, {"col": right}, {"col": left})]
+
+    def sideways(h, arrival):
+        mail.arrive(arrival)
+        dst = piece(other, col, h)
+        return [mail.push(dst, dst, device) for device in ({"col": right}, {"col": left})]
+
+    def relay(r, h, from_left, from_right):
+        mail.arrive(from_left)
+        one = mail.push(part(r, left, h, 0), part(r, left, h, 0), {"col": right})
+        mail.arrive(from_right)
+        return one, mail.push(part(r, right, h, 1), part(r, right, h, 1), {"col": left})
+
+    def finish_half(h, relays):
+        for r, keys_in in zip((row, other), relays):
+            for k in keys_in:
+                mail.arrive(k)
+            project(r, across, h)
+        here = pl.ds(h * half, half)
+        for j in range(3):
+            feats[j, here] = acc[j, here].astype(BF)
+        there = pl.ds(pl.multiple_of(a * ROWS + (HALO + h * half), 16), half)
+        for d in range(1, HEADS):
+            to = turn(a, d, HEADS)
+            mail.push(feats.at[:, here, cols(to)], fx.at[:, there], at_ctx(z, to))
+        mail.keep(feats.at[:, here, cols(a)], fx.at[:, there])
+
+    first = launch(0)
     mail.settle()
-    project(row, col, tokens[...])
-    mail.arrive(vertical)
-    gr = mail.push(block(other, col), block(other, col), {"col": right})
-    gl = mail.push(block(other, col), block(other, col), {"col": left})
+    project(row, col, 0)
+    first_side = sideways(0, first[0])
+    second = launch(1)
     key_parts = []
     for src, dst in ((keys, kh), (tokens, th), (queries, qh), (cot, ch)):
         for d in range(1, HEADS):
@@ -161,32 +190,26 @@
                 key_parts.append(k)
         if dst is not kh:
             mail.keep(src.at[:, cols(a)], dst.at[rows(a, ROWS)])
-    project(other, col)
-    relays = []
-    for r, from_left, from_right in ((row, fr, fl), (other, gr, gl)):
-        mail.arrive(from_left)
-        relays.append(mail.push(half(r, left, 0), half(r, left, 0), {"col": right}))
-        mail.arrive(from_right)
-        relays.append(mail.push(half(r, right, 1), half(r, right, 1), {"col": left}))
-        project(r, left)
-        project(r, right)
-        if r is row:
-            for k in key_parts:
-                mail.arrive(k)
-            gathered = slab_gather(mail, kh, kfull, z, a)
-    for r, first in ((row, 0), (other, 2)):
-        mail.arrive(relays[first])
-        mail.arrive(relays[first + 1])
-        project(r, across)
-    slab_relay(mail, kfull, z, a, *gathered)
-    feats[...] = acc[...].astype(BF)
-
-    for d in range(1, HEADS):
-        to = turn(a, d, HEADS)
-        mail.push(feats.at[:, :, cols(to)], fx.at[:, rows(a, ROWS, HALO)], at_ctx(z, to))
-    mail.keep(feats.at[:, :, cols(a)], fx.at[:, rows(a, ROWS, HALO)])
-
-    n = len(mail.remote)
+    project(other, col, 0)
+    relays = [[relay(row, 0, *first[1:])], []]
+    second_side = sideways(1, second[0])
+    relays[0].append(relay(other, 0, *first_side))
+    for r in (row, other):
+        project(r, left, 0)
+        project(r, right, 0)
+    relays[1].append(relay(row, 1, *second[1:]))
+    finish_half(0, relays[0])
+    relays[1].append(relay(other, 1, *second_side))
+    for k in key_parts:
+        mail.arrive(k)
+    gathered = slab_gather(mail, kh, kfull, z, a)
+    for r in (row, other):
+        project(r, col, 1)
+        project(r, left, 1)
+        project(r, right, 1)
+    finish_half(1, relays[1])
+
+    n = len(mail.remote) + 2
 
     def edge(src, dst, k, b, device):
         return pltpu.make_async_remote_copy(
@@ -221,6 +244,7 @@
             for copy in last_rows(b):
                 copy.start()
 
+    slab_relay(mail, kfull, z, a, *gathered)
     mail.finish()
     for copy in first_rows(0) + last_rows(0):
         copy.wait_recv()
@@ -640,7 +664,7 @@
     whole = SLABS * SLAB
     mine, head = shape(ROWS, WIDTH), shape(SLAB, DH)
     dma = pltpu.SemaphoreType.DMA
-    remotes = 3 + 2 + 12 + 4 + 2 + 2 + 3 + 12
+    remotes = 6 + 4 + 8 + 12 + 2 + 2 + 6 + 12
     return pl.pallas_call(
         opening_kernel,
         out_shape=[
@@ -669,7 +693,7 @@
             pltpu.VMEM((SLAB, DH), BF),
             dma((remotes,)),
             dma((remotes,)),
-            dma((3 + 3 + 1 + 1,)),
+            dma((3 + 3 + 2 + 1,)),
             pltpu.VMEM((SLAB, DH), BF),
             pltpu.VMEM((whole, DH), BF),
             pltpu.VMEM((DH, whole), BF),

time: 148 us -> 144 us (0.973)
  Pallas kernels: 147 us -> 143 us
    pallas_call x1, Pallas kernels: 100 us -> 95.1 us  [opening(): pl.pallas_call(opening_kernel, out_shape=[mine, mine, *[shape(ROWS, SLABS...]
    pallas_call x1, Pallas kernels: 41.9 us -> 43.5 us  [finale(): pl.pallas_call(finale_kernel, out_shape=[shape(ROWS, WIDTH), shape(3, ROW...]
where the time goes in v7:
time: 144 us
  Pallas kernels  143 us (99%)
    pallas_call x1, Pallas kernels, opening(): pl.pallas_call(opening_kernel, out_shape=[mine, mine, *[shape(ROWS, SLABS...  95.1 us
    pallas_call x1, Pallas kernels, finale(): pl.pallas_call(finale_kernel, out_shape=[shape(ROWS, WIDTH), shape(3, ROW...  43.5 us
    pallas_call x1, Pallas kernels, deliver(): pl.pallas_call(deliver_kernel, grid=(steps,), out_shape=[out, out, shape(...  4.22 us

profile of v7, /device:TPU:1, one launch (start us, length us, event | category | flops | bytes accessed | tf_op | source)
XLA Modules:
  0.0 143.6 jit_solution(7855997241272306672)
XLA Ops:
  0.6 95.1 %shard_map.126 = (bf16[256,512]{1,0:T(8,128)(2,1)}, bf16[256,512]{1,0:T(8,128)(2,1)}, bf16[256,1024]{1,0:T(8,128)(2,1)}, bf16[256,1024]{1,0:T(8,128)(2,1)}, bf16...) custom-call(bf16[256,512]{1,0:T(8,128)(2,1)} %tokens.1, ...), custom_call_target="tpu_custom_call" | custom-call | tf_op jit(solution)/shard_map/pallas_call | solution.py:668
  95.7 43.5 %shard_map.127 = (bf16[256,512]{1,0:T(8,128)(2,1)}, f32[3,256,512]{2,1,0:T(8,128)}, bf16[256,512]{1,0:T(8,128)(2,1)}, bf16[176,512]{1,0:T(8,128)(2,1)}) custom-call(bf16[3,1024,128]{2,1,0:T(8,128)(2,1)} %get-tuple-element.32.fg, bf16[1024,128]{1,0:T(8,128)(2,1)} %get-tuple-element.33.sg, bf16[1024,128]{1,0:T(8,128)(2,1)} %get-tuple-element.34.dk, ...), custom_call_target="tpu_custom_call" | custom-call | tf_op jit(solution)/shard_map/pallas_call | solution.py:914
  139.2 4.2 %shard_map.128 = (bf16[256,512]{1,0:T(8,128)(2,1)}, bf16[256,512]{1,0:T(8,128)(2,1)}, f32[3,256,512]{2,1,0:T(8,128)}, f32[3,7,512]{2,1,0:T(8,128)}, f32[128,512]...) custom-call(bf16[256,512]{1,0:T(8,128)(2,1)} %get-tuple-element.30.block, ...), custom_call_target="tpu_custom_call" | custom-call | tf_op jit(solution)/shard_map/pallas_call | solution.py:977

commit v8 on v7

--- a/solution.py
+++ b/solution.py
@@ -118,7 +118,7 @@
 
 
 def front_phase(
-    greeted, w, tokens, queries, keys, cot, weights, th, qh, ch, chalo, fx, kfull, full, acc, feats, kh, send, recv, loc,
+    greeted, mix, w, tokens, queries, keys, cot, weights, th, qh, ch, chalo, fx, kfull, full, acc, feats, kh, send, recv, loc,
 ):
     mail = Courier(send, recv, loc)
     z, a = place()
@@ -173,7 +173,7 @@
         there = pl.ds(pl.multiple_of(a * ROWS + (HALO + h * half), 16), half)
         for d in range(1, HEADS):
             to = turn(a, d, HEADS)
-            mail.push(feats.at[:, here, cols(to)], fx.at[:, there], at_ctx(z, to))
+            needed.append(mail.push(feats.at[:, here, cols(to)], fx.at[:, there], at_ctx(z, to)))
         mail.keep(feats.at[:, here, cols(a)], fx.at[:, there])
 
     first = launch(0)
@@ -181,13 +181,15 @@
     project(row, col, 0)
     first_side = sideways(0, first[0])
     second = launch(1)
-    key_parts = []
+    key_parts, needed = [], []
     for src, dst in ((keys, kh), (tokens, th), (queries, qh), (cot, ch)):
         for d in range(1, HEADS):
             to = turn(a, d, HEADS)
             k = mail.push(src.at[:, cols(to)], dst.at[rows(a, ROWS)], at_ctx(z, to))
             if dst is kh:
                 key_parts.append(k)
+            elif dst is th:
+                needed.append(k)
         if dst is not kh:
             mail.keep(src.at[:, cols(a)], dst.at[rows(a, ROWS)])
     project(other, col, 0)
@@ -245,9 +247,13 @@
                 copy.start()
 
     slab_relay(mail, kfull, z, a, *gathered)
-    mail.finish()
+    mail.settle()
+    for k in needed:
+        mail.arrive(k)
     for copy in first_rows(0) + last_rows(0):
         copy.wait_recv()
+    mix()
+    mail.finish()
 
     @pl.when(a == 0)
     def _():
@@ -455,13 +461,10 @@
     gain = scale * 1.4426950408889634
     mine = rows(z, SLAB)
     up, down = at_ctx(turn(z, 1, SLABS), a), at_ctx(turn(z, -1, SLABS), a)
-    spread_taps(spread, mr, a)
-
     def turn_keys(s, carry):
         kt[:, cols(s, SLAB)] = k[rows(s, SLAB)].T
         return carry
 
-    hyena(z, a, fx, short, tok, stream, qm, km, vm, lm, pr, feat, shifts, spread)
     from_down = mail.push(stream, v.at[mine], up)
     from_up = mail.push(stream, v.at[mine], down)
     v[mine] = stream[...]
@@ -650,8 +653,14 @@
         + [at_ctx(turn(z, d, SLABS), b) for d in (1, -1) for b in range(HEADS)]
         + [at_ctx(turn(z, 2, SLABS), a)]
     )
+    stream, (qm, km, vm, lm, feat, _, shifts, spread), pr = rest[0], rest[20:28], outs[-1]
+
+    def mix():
+        spread_taps(spread, mr, a)
+        hyena(z, a, fx, short, th, stream, qm, km, vm, lm, pr, feat, shifts, spread)
+
     pl.run_scoped(
-        lambda w: front_phase(greeted, w, tokens, queries, keys, cot, weights, *held), pltpu.VMEM(weights.shape, BF)
+        lambda w: front_phase(greeted, mix, w, tokens, queries, keys, cot, weights, *held), pltpu.VMEM(weights.shape, BF)
     )
     pl.run_scoped(
         lambda st: middle_phase(st, full, fx, th, qh, kfull, ch, chalo, short, mr, *outs, *rest),

time: 144 us -> 145 us (level)
    pallas_call x1, Pallas kernels: 95.1 us -> 96.6 us  [opening(): pl.pallas_call(opening_kernel, out_shape=[mine, mine, *[shape(ROWS, SLABS...]
where the time goes in v8:
time: 145 us
  Pallas kernels  144 us (99%)
    pallas_call x1, Pallas kernels, opening(): pl.pallas_call(opening_kernel, out_shape=[mine, mine, *[shape(ROWS, SLABS...  96.6 us
    pallas_call x1, Pallas kernels, finale(): pl.pallas_call(finale_kernel, out_shape=[shape(ROWS, WIDTH), shape(3, ROW...  43.2 us
    pallas_call x1, Pallas kernels, deliver(): pl.pallas_call(deliver_kernel, grid=(steps,), out_shape=[out, out, shape(...  4.22 us

profile of v8, /device:TPU:1, one launch (start us, length us, event | category | flops | bytes accessed | tf_op | source)
XLA Modules:
  0.0 144.8 jit_solution(10932134481481925349)
XLA Ops:
  0.6 96.6 %shard_map.126 = (bf16[256,512]{1,0:T(8,128)(2,1)}, bf16[256,512]{1,0:T(8,128)(2,1)}, bf16[256,1024]{1,0:T(8,128)(2,1)}, bf16[256,1024]{1,0:T(8,128)(2,1)}, bf16...) custom-call(bf16[256,512]{1,0:T(8,128)(2,1)} %tokens.1, ...), custom_call_target="tpu_custom_call" | custom-call | tf_op jit(solution)/shard_map/pallas_call | solution.py:677
  97.2 43.2 %shard_map.127 = (bf16[256,512]{1,0:T(8,128)(2,1)}, f32[3,256,512]{2,1,0:T(8,128)}, bf16[256,512]{1,0:T(8,128)(2,1)}, bf16[176,512]{1,0:T(8,128)(2,1)}) custom-call(bf16[3,1024,128]{2,1,0:T(8,128)(2,1)} %get-tuple-element.32.fg, bf16[1024,128]{1,0:T(8,128)(2,1)} %get-tuple-element.33.sg, bf16[1024,128]{1,0:T(8,128)(2,1)} %get-tuple-element.34.dk, ...), custom_call_target="tpu_custom_call" | custom-call | tf_op jit(solution)/shard_map/pallas_call | solution.py:923
  140.4 4.2 %shard_map.128 = (bf16[256,512]{1,0:T(8,128)(2,1)}, bf16[256,512]{1,0:T(8,128)(2,1)}, f32[3,256,512]{2,1,0:T(8,128)}, f32[3,7,512]{2,1,0:T(8,128)}, f32[128,512]...) custom-call(bf16[256,512]{1,0:T(8,128)(2,1)} %get-tuple-element.30.block, ...), custom_call_target="tpu_custom_call" | custom-call | tf_op jit(solution)/shard_map/pallas_call | solution.py:986

commit v9 on v7

--- a/solution.py
+++ b/solution.py
@@ -810,10 +810,6 @@
     mail.arrive(to_mate)
     ring.append(weight_first(1, mate))
     spread_shifts(shifts, pr, HALO - MRLEN + TILE, -1)
-    tap_grads(shifts, mg, lines)
-    small[pl.ds(0, MRLEN)] = lines[...].reshape(MRLEN, DH).astype(BF)
-    small[pl.ds(MRLEN, short_part.shape[0])] = short_part[...]
-    small_in = [mail.push(small, slots.at[d - 1], at_ctx(turn(z, d, SLABS), a)) for d in range(1, SLABS)]
     for k in direct:
         mail.arrive(k)
     relays = [
@@ -851,6 +847,11 @@
     for n in range(2):
         term_block(1, n)
         term_block(3, n)
+        if n == 0:
+            tap_grads(shifts, mg, lines)
+            small[pl.ds(0, MRLEN)] = lines[...].reshape(MRLEN, DH).astype(BF)
+            small[pl.ds(MRLEN, short_part.shape[0])] = short_part[...]
+            small_in = [mail.push(small, slots.at[d - 1], at_ctx(turn(z, d, SLABS), a)) for d in range(1, SLABS)]
         mail.arrive(firsts[n][0])
         tsend[1, n, top] = (tsend[1, n, top].astype(F32) + xr1[0, n].astype(F32)).astype(BF)
         from_left = mail.push(tsend.at[1, n], xr2.at[0, n], {"col": right})

time: 144 us -> 145 us (level)
  no operation moved by 1% of the time
where the time goes in v9:
time: 145 us; the launch traced here: 144 us
  Pallas kernels  144 us (99%)
    pallas_call x1, Pallas kernels, opening(): pl.pallas_call(opening_kernel, out_shape=[mine, mine, *[shape(ROWS, SLABS...  95.1 us
    pallas_call x1, Pallas kernels, finale(): pl.pallas_call(finale_kernel, out_shape=[shape(ROWS, WIDTH), shape(3, ROW...  44.4 us
    pallas_call x1, Pallas kernels, deliver(): pl.pallas_call(deliver_kernel, grid=(steps,), out_shape=[out, out, shape(...  4.22 us

profile of v9, /device:TPU:1, one launch (start us, length us, event | category | flops | bytes accessed | tf_op | source)
XLA Modules:
  0.0 144.4 jit_solution(4211562816844803745)
XLA Ops:
  0.6 95.1 %shard_map.126 = (bf16[256,512]{1,0:T(8,128)(2,1)}, bf16[256,512]{1,0:T(8,128)(2,1)}, bf16[256,1024]{1,0:T(8,128)(2,1)}, bf16[256,1024]{1,0:T(8,128)(2,1)}, bf16...) custom-call(bf16[256,512]{1,0:T(8,128)(2,1)} %tokens.1, ...), custom_call_target="tpu_custom_call" | custom-call | tf_op jit(solution)/shard_map/pallas_call | solution.py:668
  95.7 44.4 %shard_map.127 = (bf16[256,512]{1,0:T(8,128)(2,1)}, f32[3,256,512]{2,1,0:T(8,128)}, bf16[256,512]{1,0:T(8,128)(2,1)}, bf16[176,512]{1,0:T(8,128)(2,1)}) custom-call(bf16[3,1024,128]{2,1,0:T(8,128)(2,1)} %get-tuple-element.32.fg, bf16[1024,128]{1,0:T(8,128)(2,1)} %get-tuple-element.33.sg, bf16[1024,128]{1,0:T(8,128)(2,1)} %get-tuple-element.34.dk, ...), custom_call_target="tpu_custom_call" | custom-call | tf_op jit(solution)/shard_map/pallas_call | solution.py:915
  140.1 4.2 %shard_map.128 = (bf16[256,512]{1,0:T(8,128)(2,1)}, bf16[256,512]{1,0:T(8,128)(2,1)}, f32[3,256,512]{2,1,0:T(8,128)}, f32[3,7,512]{2,1,0:T(8,128)}, f32[128,512]...) custom-call(bf16[256,512]{1,0:T(8,128)(2,1)} %get-tuple-element.30.block, ...), custom_call_target="tpu_custom_call" | custom-call | tf_op jit(solution)/shard_map/pallas_call | solution.py:978
